TPU v7x, 32 devices: a whole 2x2x4 slice. The times are simulated.
32 devices in a mesh: sp: 8 (over z, y), tp: 4 (over x, core).
Axes of the slice: x: 2, y: 2, z: 4, core: 2. Of those that a mesh axis runs over, the one named last changes fastest.
Arguments:
- inputs: bfloat16 [25088, 1024], P(('sp', 'tp')), may hold values from -100 to 100, as said below
- grad_out: bfloat16 [25088, 512], P(('sp', 'tp')), may hold values from -6 to 6
- window_valid: int32 [512], P('sp'), may hold values 0 or 1
- window_edge: int32 [512], P('sp'), may hold values from 0 to 3
- merge_gain: bfloat16 [1024], replicated, may hold values from 0.5 to 1.5
- merge_bias: bfloat16 [1024], replicated, may hold values from -1.75 to 1.75
- merge_weight: bfloat16 [1024, 512], P(None, 'tp'), may hold values from -0.1875 to 0.1875
- attn_gain: bfloat16 [512], replicated, may hold values from 0.5 to 1.5
- attn_bias: bfloat16 [512], replicated, may hold values from -1.75 to 1.75
- query_key_value_weight: bfloat16 [512, 3, 512], P(None, None, 'tp'), may hold values from -0.25 to 0.25
- qv_bias: bfloat16 [2, 512], P(None, 'tp'), may hold values from -1.75 to 1.75
- rel_table: bfloat16 [169, 16], P(None, 'tp'), may hold values from -6 to 6
- proj_weight: bfloat16 [512, 512], P('tp'), may hold values from -0.75 to 0.75
- proj_bias: bfloat16 [512], replicated, may hold values from -1.75 to 1.75
- mlp_gain: bfloat16 [512], replicated, may hold values from 0.5 to 1.5
- mlp_bias: bfloat16 [512], replicated, may hold values from -1.75 to 1.75
- up_weight: bfloat16 [512, 2048], P(None, 'tp'), may hold values from -0.25 to 0.25
- up_bias: bfloat16 [2048], P('tp'), may hold values from -1.75 to 1.75
- down_weight: bfloat16 [2048, 512], P('tp'), may hold values from -0.125 to 0.125
- down_bias: bfloat16 [512], replicated, may hold values from -1.75 to 1.75
Outputs:
- block_out: bfloat16 [25088, 512], P(('sp', 'tp'))
- grad_inputs: float32 [25088, 1024], P(('sp', 'tp'))
- grad_merge_gain: float32 [1024], replicated
- grad_merge_bias: float32 [1024], replicated
- grad_merge_weight: float32 [1024, 512], P(None, 'tp')
- grad_attn_gain: float32 [512], replicated
- grad_attn_bias: float32 [512], replicated
- grad_qkv_weight: float32 [512, 3, 512], P(None, None, 'tp')
- grad_qv_bias: float32 [2, 512], P(None, 'tp')
- grad_rel_table: float32 [169, 16], P(None, 'tp')
- grad_proj_weight: float32 [512, 512], P('tp')
- grad_proj_bias: float32 [512], replicated
- grad_mlp_gain: float32 [512], replicated
- grad_mlp_bias: float32 [512], replicated
- grad_up_weight: float32 [512, 2048], P(None, 'tp')
- grad_up_bias: float32 [2048], P('tp')
- grad_down_weight: float32 [2048, 512], P('tp')
- grad_down_bias: float32 [512], replicated
Inputs may be any that keep to these rules, and one draw needn't show every extreme that they name: `inputs`: section-2 features; each feature has its own scale and each token its own. `window_edge`: bit 0 set: the window's last three columns come from the page's other side under the shift; bit 1: the same for its last three rows. `window_valid`: 0 marks a window of a padded page area.
All inputs are finite; a program needn't handle non-finite values. No bound on the sum of `window_valid` on one device may be relied on, other than what follows from the above.
Results may differ from a plain program's by a relative error of at most 0.02.
Values may be sent and summed in bfloat16 or wider, within the bound.
A program may use at most 128 MiB of HBM per device.

v0:
```python
from functools import partial

import jax
import jax.numpy as jnp
from jax import lax
from jax.sharding import PartitionSpec as P

SIDE = 7


EPSILON = 1e-05
NEG_FILL = -1000000000.0
FULL_PRECISION = lax.Precision.HIGHEST


def norm_forward(values, gain_vec, shift_term):
    row_mean = jnp.mean(values, -1, keepdims=True)
    centred = values - row_mean
    variance = jnp.mean(centred * centred, -1, keepdims=True)
    inv_std = lax.rsqrt(variance + EPSILON)
    normed = centred * inv_std
    return (normed * gain_vec + shift_term, normed, inv_std)


def norm_backward(upstream, normed, inv_std, gain_vec):
    scaled = upstream * gain_vec
    result = (
        scaled
        - jnp.mean(scaled, -1, keepdims=True)
        - normed * jnp.mean(scaled * normed, -1, keepdims=True)
    )
    return (result * inv_std, jnp.sum(upstream * normed, 0), jnp.sum(upstream, 0))


def contract_rows(left_side, right_side):
    return lax.dot_general(
        left_side, right_side, (((0,), (0,)), ((), ())), preferred_element_type=jnp.float32
    )


def contract_cols(left_side, right_side):
    return lax.dot_general(
        left_side, right_side, (((1,), (1,)), ((), ())), preferred_element_type=jnp.float32
    )


def window_tables(edge_ids):
    position = jnp.arange(SIDE * SIDE, dtype=jnp.int32)
    row_of = position // SIDE
    col_of = position % SIDE
    rel_index = (row_of[:, None] - row_of[None, :] + SIDE - 1) * (2 * SIDE - 1) + (
        col_of[:, None] - col_of[None, :] + SIDE - 1
    )
    onehot = (
        rel_index[:, :, None] == jnp.arange((2 * SIDE - 1) ** 2, dtype=jnp.int32)[None, None, :]
    ).astype(jnp.float32)
    shift_size = SIDE // 2
    col_high = (col_of >= SIDE - shift_size).astype(jnp.int32)
    row_high = (row_of >= SIDE - shift_size).astype(jnp.int32)
    region = (edge_ids % 2)[:, None] * col_high[None, :] + 2 * (edge_ids // 2)[:, None] * row_high[
        None, :
    ]
    allowed = region[:, :, None] == region[:, None, :]
    return (onehot, allowed)


def window_split(values, windows, head_count):
    return values.reshape(windows, SIDE * SIDE, head_count, -1)


def window_logits(queries, key_rows, bias_heads, allowed):
    windows, head_count = (allowed.shape[0], bias_heads.shape[0])
    query_win = window_split(queries, windows, head_count)
    key_win = window_split(key_rows, windows, head_count)
    factor = query_win.shape[-1] ** (-0.5)
    logits = (
        jnp.einsum("wihd,wjhd->whij", query_win, key_win, preferred_element_type=jnp.float32)
        * factor
        + bias_heads[None]
    )
    return jnp.where(allowed[:, None], logits, NEG_FILL)


def attend_forward(queries, key_rows, value_rows, bias_heads, allowed):
    windows, head_count = (allowed.shape[0], bias_heads.shape[0])
    logits = window_logits(queries, key_rows, bias_heads, allowed)
    row_top = jnp.max(logits, -1, keepdims=True)
    exp_terms = jnp.exp(logits - row_top)
    row_total = jnp.sum(exp_terms, -1, keepdims=True)
    attn_probs = (exp_terms / row_total).astype(jnp.bfloat16)
    attended = jnp.einsum(
        "whij,wjhd->wihd",
        attn_probs,
        window_split(value_rows, windows, head_count),
        preferred_element_type=jnp.float32,
    )
    return (attended.reshape(queries.shape).astype(jnp.bfloat16), row_top + jnp.log(row_total))


def attend_backward(d_attended, queries, key_rows, value_rows, bias_heads, allowed, log_total):
    windows, head_count = (allowed.shape[0], bias_heads.shape[0])
    logits = window_logits(queries, key_rows, bias_heads, allowed)
    attn_probs = jnp.exp(logits - log_total)
    d_win = window_split(d_attended, windows, head_count)
    query_win = window_split(queries, windows, head_count)
    key_win = window_split(key_rows, windows, head_count)
    value_win = window_split(value_rows, windows, head_count)
    d_probs = jnp.einsum("wihd,wjhd->whij", d_win, value_win, preferred_element_type=jnp.float32)
    d_values = jnp.einsum(
        "whij,wihd->wjhd",
        attn_probs.astype(jnp.bfloat16),
        d_win,
        preferred_element_type=jnp.float32,
    )
    d_logits = (attn_probs * (d_probs - jnp.sum(d_probs * attn_probs, -1, keepdims=True))).astype(
        jnp.bfloat16
    )
    factor = query_win.shape[-1] ** (-0.5)
    d_queries = (
        jnp.einsum("whij,wjhd->wihd", d_logits, key_win, preferred_element_type=jnp.float32)
        * factor
    )
    d_keys = (
        jnp.einsum("whij,wihd->wjhd", d_logits, query_win, preferred_element_type=jnp.float32)
        * factor
    )
    d_bias = jnp.sum(d_logits.astype(jnp.float32), 0)
    flat_shape = queries.shape
    return (
        d_queries.reshape(flat_shape).astype(jnp.bfloat16),
        d_keys.reshape(flat_shape).astype(jnp.bfloat16),
        d_values.reshape(flat_shape).astype(jnp.bfloat16),
        d_bias,
    )


def on_device(
    inputs,
    grad_out,
    window_valid,
    window_edge,
    merge_gain,
    merge_bias,
    merge_weight,
    attn_gain,
    attn_bias,
    query_key_value_weight,
    qv_bias,
    rel_table,
    proj_weight,
    proj_bias,
    mlp_gain,
    mlp_bias,
    up_weight,
    up_bias,
    down_weight,
    down_bias,
):
    row_count = inputs.shape[0]
    windows = row_count // (SIDE * SIDE)
    tp_index = lax.axis_index("tp")
    valid_mine = lax.dynamic_slice_in_dim(window_valid, tp_index * windows, windows, 0)
    keep_rows = jnp.repeat(valid_mine.astype(jnp.float32), SIDE * SIDE)[:, None]
    query_key_value_rows, qv_all, table_all, proj_all, up_all, up_bias_all, down_all = (
        query_key_value_weight,
        qv_bias,
        rel_table,
        proj_weight,
        up_weight,
        up_bias,
        down_weight,
    )
    merged, merge_hat, merge_inv = norm_forward(
        inputs.astype(jnp.float32), merge_gain.astype(jnp.float32), merge_bias.astype(jnp.float32)
    )
    merged = merged.astype(jnp.bfloat16)
    merged_rows = lax.all_gather(merged, "tp", axis=0, tiled=True)
    section_cols = jnp.dot(merged_rows, merge_weight, preferred_element_type=jnp.float32).astype(
        jnp.bfloat16
    )
    section_out = lax.all_to_all(section_cols, "tp", split_axis=0, concat_axis=1, tiled=True)
    section_float = section_out.astype(jnp.float32)
    attn_gain_f = attn_gain.astype(jnp.float32)
    attn_normed, attn_hat, attn_inv = norm_forward(
        section_float, attn_gain_f, attn_bias.astype(jnp.float32)
    )
    attention_input = attn_normed.astype(jnp.bfloat16)
    attention_rows = lax.all_gather(attention_input, "tp", axis=0, tiled=True)
    projected_rows = jnp.einsum(
        "tv,vfq->tfq", attention_rows, query_key_value_rows, preferred_element_type=jnp.float32
    )
    queries = (projected_rows[:, 0] + qv_all[0].astype(jnp.float32)).astype(jnp.bfloat16)
    key_rows = projected_rows[:, 1].astype(jnp.bfloat16)
    value_rows = (projected_rows[:, 2] + qv_all[1].astype(jnp.float32)).astype(jnp.bfloat16)
    onehot, allowed = window_tables(window_edge)
    bias_heads = jnp.einsum(
        "ijr,rh->hij", onehot, table_all.astype(jnp.float32), precision=FULL_PRECISION
    )
    attended, log_total = attend_forward(queries, key_rows, value_rows, bias_heads, allowed)
    attn_out = lax.psum_scatter(
        jnp.dot(attended, proj_weight, preferred_element_type=jnp.float32).astype(jnp.bfloat16),
        "tp",
        scatter_dimension=0,
        tiled=True,
    ).astype(jnp.float32)
    residual = section_float + attn_out + proj_bias.astype(jnp.float32)
    mlp_gain_f = mlp_gain.astype(jnp.float32)
    mlp_normed, mlp_hat, mlp_inv = norm_forward(residual, mlp_gain_f, mlp_bias.astype(jnp.float32))
    mlp_in = mlp_normed.astype(jnp.bfloat16)
    mlp_rows = lax.all_gather(mlp_in, "tp", axis=0, tiled=True)
    pre_act = jnp.dot(mlp_rows, up_all, preferred_element_type=jnp.float32) + up_bias_all.astype(
        jnp.float32
    )
    hidden_float, gelu_pullback = jax.vjp(partial(jax.nn.gelu, approximate=False), pre_act)
    hidden = hidden_float.astype(jnp.bfloat16)
    mlp_out = lax.psum_scatter(
        jnp.dot(
            lax.slice_in_dim(hidden, 0, lax.axis_size("tp") * row_count, axis=0),
            down_weight,
            preferred_element_type=jnp.float32,
        ).astype(jnp.bfloat16),
        "tp",
        scatter_dimension=0,
        tiled=True,
    ).astype(jnp.float32)
    block_out = ((residual + mlp_out + down_bias.astype(jnp.float32)) * keep_rows).astype(
        jnp.bfloat16
    )
    d_out = grad_out.astype(jnp.float32) * keep_rows
    d_down_bias = jnp.sum(d_out, 0)
    d_mlp = d_out.astype(jnp.bfloat16)
    d_mlp_rows = lax.all_gather(d_mlp, "tp", axis=0, tiled=True)
    d_hidden = contract_cols(d_mlp_rows, down_all)
    d_down_weight = contract_rows(hidden, d_mlp_rows)
    d_pre = gelu_pullback(d_hidden)[0].astype(jnp.bfloat16)
    d_up_bias = jnp.sum(d_pre.astype(jnp.float32), 0)
    d_up_weight = contract_rows(mlp_rows, d_pre)
    d_mlp_in = lax.psum_scatter(
        contract_cols(d_pre, up_weight).astype(jnp.bfloat16), "tp", scatter_dimension=0, tiled=True
    ).astype(jnp.float32)
    d_mlp_norm, d_mlp_gain, d_mlp_bias = norm_backward(d_mlp_in, mlp_hat, mlp_inv, mlp_gain_f)
    d_residual = d_out + d_mlp_norm
    d_proj_bias = jnp.sum(d_residual, 0)
    d_attn = d_residual.astype(jnp.bfloat16)
    d_attn_rows = lax.all_gather(d_attn, "tp", axis=0, tiled=True)
    d_attended = contract_cols(d_attn_rows, proj_all).astype(jnp.bfloat16)
    d_proj_weight = contract_rows(attended, d_attn_rows)
    d_queries, d_keys, d_values, d_bias = attend_backward(
        d_attended, queries, key_rows, value_rows, bias_heads, allowed, log_total
    )
    d_rel_table = jnp.einsum("ijr,hij->rh", onehot, d_bias, precision=FULL_PRECISION)
    d_qv_bias = jnp.stack(
        [jnp.sum(d_queries.astype(jnp.float32), 0), jnp.sum(d_values.astype(jnp.float32), 0)]
    )
    projected_gradient = jnp.stack([d_queries, d_keys, d_values], axis=1)
    d_qkv_weight = jnp.einsum(
        "pi,pyt->iyt", attention_rows, projected_gradient, preferred_element_type=jnp.float32
    )
    d_attn_in = lax.psum_scatter(
        jnp.einsum(
            "qut,xut->qx",
            projected_gradient,
            query_key_value_weight,
            preferred_element_type=jnp.float32,
        ).astype(jnp.bfloat16),
        "tp",
        scatter_dimension=0,
        tiled=True,
    ).astype(jnp.float32)
    d_attn_norm, d_attn_gain, d_attn_bias = norm_backward(
        d_attn_in, attn_hat, attn_inv, attn_gain_f
    )
    d_section = (d_residual + d_attn_norm).astype(jnp.bfloat16)
    d_cols = lax.all_to_all(d_section, "tp", split_axis=1, concat_axis=0, tiled=True)
    d_merge_weight = contract_rows(merged_rows, d_cols)
    d_merged = lax.psum_scatter(
        contract_cols(d_cols, merge_weight).astype(jnp.bfloat16),
        "tp",
        scatter_dimension=0,
        tiled=True,
    ).astype(jnp.float32)
    d_inputs, d_merge_gain, d_merge_bias = norm_backward(
        d_merged, merge_hat, merge_inv, merge_gain.astype(jnp.float32)
    )
    shard_sums = (
        lax.psum(d_merge_weight.astype(jnp.bfloat16), "sp").astype(jnp.float32),
        lax.psum(d_qkv_weight.astype(jnp.bfloat16), "sp").astype(jnp.float32),
        lax.psum(d_qv_bias.astype(jnp.bfloat16), "sp").astype(jnp.float32),
        lax.psum(d_rel_table.astype(jnp.bfloat16), "sp").astype(jnp.float32),
        lax.psum(d_proj_weight.astype(jnp.bfloat16), "sp").astype(jnp.float32),
        lax.psum(d_up_weight.astype(jnp.bfloat16), "sp").astype(jnp.float32),
        lax.psum(d_up_bias.astype(jnp.bfloat16), "sp").astype(jnp.float32),
        lax.psum(d_down_weight.astype(jnp.bfloat16), "sp").astype(jnp.float32),
    )
    shared_sums = lax.psum(
        (
            d_merge_gain,
            d_merge_bias,
            d_attn_gain,
            d_attn_bias,
            d_proj_bias,
            d_mlp_gain,
            d_mlp_bias,
            d_down_bias,
        ),
        ("sp", "tp"),
    )
    return (
        block_out,
        d_inputs,
        shared_sums[0],
        shared_sums[1],
        shard_sums[0],
        shared_sums[2],
        shared_sums[3],
        shard_sums[1],
        shard_sums[2],
        shard_sums[3],
        shard_sums[4],
        shared_sums[4],
        shared_sums[5],
        shared_sums[6],
        shard_sums[5],
        shard_sums[6],
        shard_sums[7],
        shared_sums[7],
    )


def solution(mesh):
    placed = (
        P(("sp", "tp"), None),
        P(("sp", "tp"), None),
        P("sp"),
        P("sp"),
        P(),
        P(),
        P(None, "tp"),
        P(),
        P(),
        P(None, None, "tp"),
        P(None, "tp"),
        P(None, "tp"),
        P("tp", None),
        P(),
        P(),
        P(),
        P(None, "tp"),
        P("tp"),
        P("tp", None),
        P(),
    )
    return jax.shard_map(
        on_device,
        mesh=mesh,
        in_specs=placed,
        out_specs=(
            P(("sp", "tp"), None),
            P(("sp", "tp"), None),
            P(),
            P(),
            P(None, "tp"),
            P(),
            P(),
            P(None, None, "tp"),
            P(None, "tp"),
            P(None, "tp"),
            P("tp", None),
            P(),
            P(),
            P(),
            P(None, "tp"),
            P("tp"),
            P("tp", None),
            P(),
        ),
        check_vma=False,
    )
```

profile of v0, /device:TPU:0, one launch (start us, length us, event | category | flops | bytes accessed | tf_op | source)
XLA Modules:
  0.0 774.4 jit_solution(6858031083178034510)
XLA Ops:
  14.5 49.9 %all-gather.6.cloned.1.call-done = bf16[3136,1024]{1,0:T(8,128)(2,1)} async-done(((bf16[784,1024]{1,0:T(8,128)(2,1)}), bf16[3136,1024]{1,0:T(8,128)(2,1)}) %all-gather.6.cloned.1.call-update) | async-done | bytes 6422544 | tf_op jit(solution)/shard_map/all_gather | solution.py:177
  73.7 11.7 %all-to-all-done = bf16[4,784,128]{2,1,0:T(8,128)(2,1)S(1)} async-done(((bf16[4,784,128]{2,1,0:T(8,128)(2,1)}), bf16[4,784,128]{2,1,0:T(8,128)(2,1)S(1)}, u32[]{:S(2)}, u32[]{:S(2)}) %all-to-all-start) | async-done | bytes 802848 | tf_op jit(solution)/shard_map/all_to_all | solution.py:181
  92.4 24.8 %all-gather.8.cloned.1.call-done = bf16[3136,512]{1,0:T(8,128)(2,1)} async-done(((bf16[784,512]{1,0:T(8,128)(2,1)}), bf16[3136,512]{1,0:T(8,128)(2,1)}) %all-gather.8.cloned.1.call-update) | async-done | bytes 3211280 | tf_op jit(solution)/shard_map/all_gather | solution.py:188
  133.2 5.7 copy.81
  138.9 8.4 %squeeze.10 = f32[64,49,4,32]{1,0,3,2:T(8,128)} reshape(f32[3136,1,128]{0,2,1:T(8,128)} %copy.78) | data formatting | bytes 3211264 | tf_op jit(solution)/shard_map/squeeze | solution.py:192
  147.3 8.4 %squeeze.4 = f32[64,49,4,32]{1,0,3,2:T(8,128)} reshape(f32[3136,1,128]{0,2,1:T(8,128)} %copy.77) | data formatting | bytes 3211264 | tf_op jit(solution)/shard_map/squeeze | solution.py:194
  183.9 37.9 %reduce-scatter.6.cloned.1.call-done = bf16[784,512]{1,0:T(8,128)(2,1)} async-done(((bf16[3136,512]{1,0:T(8,128)(2,1)}), bf16[784,512]{1,0:T(8,128)(2,1)}) %reduce-scatter.6.cloned.1.call-update) | async-done | bytes 802832 | tf_op jit(solution)/shard_map/reduce_scatter | solution.py:200
  227.5 26.4 %all-gather.10.cloned.1.call-done = bf16[3136,512]{1,0:T(8,128)(2,1)} async-done(((bf16[784,512]{1,0:T(8,128)(2,1)}), bf16[3136,512]{1,0:T(8,128)(2,1)}) %all-gather.10.cloned.1.call-update) | async-done | bytes 3211280 | tf_op jit(solution)/shard_map/all_gather | solution.py:210
  253.9 6.5 convolution_add_fusion
  260.4 24.5 %all-gather.12.cloned.1.call-done = bf16[3136,512]{1,0:T(8,128)(2,1)} async-done(((bf16[784,512]{1,0:T(8,128)(2,1)}), bf16[3136,512]{1,0:T(8,128)(2,1)}) %all-gather.12.cloned.1.call-update) | async-done | bytes 3211280 | tf_op jit(solution)/shard_map/all_gather | solution.py:232
  284.9 19.9 %fusion.78 = (bf16[512]{0:T(512)(128)(2,1)}, bf16[3136,512]{1,0:T(8,128)(2,1)S(1)}, f32[3136,512]{1,0:T(8,128)}) fusion(f32[3136,512]{1,0:T(8,128)} %convolution_add_fusion, bf16[3136,512]{1,0:T(8,128)(2,1)} %all-gather.12.cloned.1.call-done, bf16[512,512]{1,0:T(8,128)(2,1)S(1)} %copy-done), kind=kOutput, calls=%fused_computation.166 | convolution fusion | flops 1761377792 | bytes 19792896 | tf_op jit(solution)/shard_map/dot_general | solution.py:42
  310.5 6.4 multiply_convert_fusion.1
  322.9 25.8 %reduce-scatter.10.cloned.1.call-done = bf16[784,512]{1,0:T(8,128)(2,1)} async-done(((bf16[3136,512]{1,0:T(8,128)(2,1)}), bf16[784,512]{1,0:T(8,128)(2,1)}) %reduce-scatter.10.cloned.1.call-update) | async-done | bytes 802832 | tf_op jit(solution)/shard_map/reduce_scatter | solution.py:238
  351.3 38.4 %reduce-scatter.8.cloned.1.call-done = bf16[784,512]{1,0:T(8,128)(2,1)} async-done(((bf16[3136,512]{1,0:T(8,128)(2,1)}), bf16[784,512]{1,0:T(8,128)(2,1)}) %reduce-scatter.8.cloned.1.call-update) | async-done | bytes 802832 | tf_op jit(solution)/shard_map/reduce_scatter | solution.py:216
  395.8 29.0 %all-gather.14.cloned.1.call-done = bf16[3136,512]{1,0:T(8,128)(2,1)} async-done(((bf16[784,512]{1,0:T(8,128)(2,1)}), bf16[3136,512]{1,0:T(8,128)(2,1)}) %all-gather.14.cloned.1.call-update) | async-done | bytes 3211280 | tf_op jit(solution)/shard_map/all_gather | solution.py:245
  430.1 5.7 copy.87
  435.8 7.1 fusion.86
  443.0 8.9 %multiply_reduce_fusion = (f32[64,4,49]{2,1,0:T(4,128)S(1)}, f32[64,4,49,49]{2,3,1,0:T(8,128)S(1)}) fusion(f32[64,4,49,49]{2,3,1,0:T(8,128)} %copy-done.1, f32[64,4,49]{2,1,0:T(4,128)S(1)} %bitcast.115, bf16[64,49,4,32]{1,3,2,0:T(8,128)(2,1)S(1)} %copy.87, bf16[64,49,4,32]{1,0,3,2:T(8,128)(2,1)S(1)} %copy-done.10), kind=kOutput, calls=%fused_computation.4 | convolution fusion | flops 41169408 | bytes 6623232 | tf_op jit(solution)/shard_map/wihd,wjhd->whij/dot_general | solution.py:108
  497.9 5.8 convolution_convert_fusion.7
  506.5 29.9 %reduce-scatter.12.cloned.1.call-done = bf16[784,512]{1,0:T(8,128)(2,1)} async-done(((bf16[3136,512]{1,0:T(8,128)(2,1)}), bf16[784,512]{1,0:T(8,128)(2,1)}) %reduce-scatter.12.cloned.1.call-update) | async-done | bytes 802832 | tf_op jit(solution)/shard_map/reduce_scatter | solution.py:259
  568.9 22.8 %all-reduce.1 = (bf16[2,128]{1,0:T(2,128)(2,1)S(1)}, bf16[169,4]{0,1:T(4,128)(2,1)S(1)}, bf16[512]{0:T(512)(128)(2,1)S(1)}) all-reduce(bf16[2,128]{1,0:T(2,128)(2,1)S(1)} %pad_maximum_fusion, bf16[169,4]{0,1:T(4,128)(2,1)S(1)} %fusion.74, bf16[512]{0:T(512)(128)(2,1)S(1)} %copy-done.61), channel_id=1, replica_groups=mesh['sp'=8,'tp'=4] {'sp'}, use_global_device_ids=true, to_apply=%region_32.33 | all-reduce | flops 1444 | bytes 5776 | tf_op jit(solution)/shard_map/psum | solution.py:288
  593.5 66.2 %all-reduce.5.cloned.1.call-done = (bf16[1024,128]{1,0:T(8,128)(2,1)}, bf16[512,3,128]{2,0,1:T(8,128)(2,1)}, bf16[128,512]{1,0:T(8,128)(2,1)}, bf16[512,512]{1,0:T(8,128)(2,1)}, bf16[512,512]{1,0:T(8,128)(2,1)}) async-done(((bf16[1024,128]{1,0:T(8,128)(2,1)}, bf16[512,3,128]{2,0,1:T(8,128)(2,1)}, bf16[128,512]{1,0:T(8,128)(2,1)}, bf16[512,512]{1,0:T(8,128)(2,1)}, bf16[512,512]{1,0:T(8,128)(2,1)}), ...) | async-done | bytes 1835024 | tf_op jit(solution)/shard_map/psum | solution.py:286
  668.4 52.7 %reduce-scatter.14.cloned.1.call-done = bf16[784,1024]{1,0:T(8,128)(2,1)} async-done(((bf16[3136,1024]{1,0:T(8,128)(2,1)}), bf16[784,1024]{1,0:T(8,128)(2,1)}) %reduce-scatter.14.cloned.1.call-update) | async-done | bytes 1605648 | tf_op jit(solution)/shard_map/reduce_scatter | solution.py:276
  724.2 39.9 %all-reduce = (f32[1024]{0:T(1024)}, f32[1024]{0:T(1024)}, f32[512]{0:T(512)}, f32[512]{0:T(512)}, f32[512]{0:T(512)}, /*index=5*/f32[512]{0:T(512)}, f32[512]{0:T(512)}, f32[512]{0:T(512)}) all-reduce(f32[1024]{0:T(1024)S(1)} %get-tuple-element.18, f32[1024]{0:T(1024)S(1)} %get-tuple-element.25, ...), channel_id=1, replica_groups=mesh['sp'=8,'tp'=4] {'sp','tp'}, use_global_device_ids=true, to_apply=%region_21.22 | all-reduce | flops 5120 | bytes 40960 | tf_op jit(solution)/shard_map/psum | solution.py:295
  (269 shorter events, 196.8 us)
Async XLA Ops:
  7.2 277.7 %copy-start = (bf16[512,512]{1,0:T(8,128)(2,1)S(1)}, bf16[512,512]{1,0:T(8,128)(2,1)}, u32[]{:S(2)}) copy-start(bf16[512,512]{1,0:T(8,128)(2,1)} %param.38) | copy-start | bytes 1572868
  7.2 57.2 %all-gather.6.cloned.1.call-start = ((), (), s32[]{:S(2)}) async-start(), calls=%async_computation.7 | async-start | bytes 8028160 | tf_op jit(solution)/shard_map/all_gather | solution.py:177
  14.4 59.2 %copy-start.54 = (bf16[512]{0:T(512)(128)(2,1)S(1)}, bf16[512]{0:T(512)(128)(2,1)}, u32[]{:S(2)}) copy-start(bf16[512]{0:T(512)(128)(2,1)} %param.27) | copy-start | bytes 3076
  14.5 59.2 %copy-start.55 = (bf16[512]{0:T(512)(128)(2,1)S(1)}, bf16[512]{0:T(512)(128)(2,1)}, u32[]{:S(2)}) copy-start(bf16[512]{0:T(512)(128)(2,1)} %param.28) | copy-start | bytes 3076
  70.0 15.4 %all-to-all-start = ((bf16[4,784,128]{2,1,0:T(8,128)(2,1)}), bf16[4,784,128]{2,1,0:T(8,128)(2,1)S(1)}, u32[]{:S(2)}, u32[]{:S(2)}) async-start(bf16[4,784,128]{2,1,0:T(8,128)(2,1)} %bitcast), calls=%async_computation | async-start | bytes 1605632 | tf_op jit(solution)/shard_map/all_to_all | solution.py:181
  73.6 43.5 %all-gather.8.cloned.1.call-start = ((), (), s32[]{:S(2)}) async-start(), calls=%async_computation.8 | async-start | bytes 4014080 | tf_op jit(solution)/shard_map/all_gather | solution.py:188
  88.1 133.7 %reduce-scatter.6.cloned.1.call-start = ((), (), s32[]{:S(2)}) async-start(), calls=%async_computation.9 | async-start | bytes 4014080 | tf_op jit(solution)/shard_map/reduce_scatter | solution.py:200
  183.2 70.7 %all-gather.10.cloned.1.call-start = ((), (), s32[]{:S(2)}) async-start(), calls=%async_computation.10 | async-start | bytes 4014080 | tf_op jit(solution)/shard_map/all_gather | solution.py:210
  224.9 60.1 %all-gather.12.cloned.1.call-start = ((), (), s32[]{:S(2)}) async-start(), calls=%async_computation.12 | async-start | bytes 4014080 | tf_op jit(solution)/shard_map/all_gather | solution.py:232
  227.4 121.3 %reduce-scatter.10.cloned.1.call-start = ((), (), s32[]{:S(2)}) async-start(), calls=%async_computation.13 | async-start | bytes 4014080 | tf_op jit(solution)/shard_map/reduce_scatter | solution.py:238
  310.2 79.5 %reduce-scatter.8.cloned.1.call-start = ((), (), s32[]{:S(2)}) async-start(), calls=%async_computation.11 | async-start | bytes 4014080 | tf_op jit(solution)/shard_map/reduce_scatter | solution.py:216
  322.2 102.5 %all-gather.14.cloned.1.call-start = ((), (), s32[]{:S(2)}) async-start(), calls=%async_computation.14 | async-start | bytes 4014080 | tf_op jit(solution)/shard_map/all_gather | solution.py:245
  395.7 140.8 %reduce-scatter.12.cloned.1.call-start = ((), (), s32[]{:S(2)}) async-start(), calls=%async_computation.15 | async-start | bytes 4014080 | tf_op jit(solution)/shard_map/reduce_scatter | solution.py:259
  541.1 15.3 %all-to-all-start.1 = ((bf16[784,4,128]{2,0,1:T(8,128)(2,1)}), bf16[784,4,128]{2,0,1:T(8,128)(2,1)S(1)}, u32[]{:S(2)}, u32[]{:S(2)}) async-start(bf16[784,4,128]{2,0,1:T(8,128)(2,1)} %copy_bitcast_fusion), calls=%async_computation.5 | async-start | bytes 1605632 | tf_op jit(solution)/shard_map/all_to_all | solution.py:274
  544.6 115.2 %all-reduce.5.cloned.1.call-start = ((), (), s32[]{:S(2)}) async-start(), calls=%async_computation.17 | async-start | bytes 3670016 | tf_op jit(solution)/shard_map/psum | solution.py:286
  561.9 159.3 %reduce-scatter.14.cloned.1.call-start = ((), (), s32[]{:S(2)}) async-start(), calls=%async_computation.16 | async-start | bytes 8028160 | tf_op jit(solution)/shard_map/reduce_scatter | solution.py:276
  567.7 153.4 %copy-start.3 = (bf16[784,1024]{1,0:T(8,128)(2,1)S(1)}, bf16[784,1024]{1,0:T(8,128)(2,1)}, u32[]{:S(2)}) copy-start(bf16[784,1024]{1,0:T(8,128)(2,1)} %param.20) | copy-start | bytes 4816900
  567.7 153.4 %copy-start.37 = (f32[784]{0:T(1024)S(1)}, f32[784]{0:T(1024)}, u32[]{:S(2)}) copy-start(f32[784]{0:T(1024)} %copy-done.36) | copy-start | bytes 9412
  567.8 153.4 %copy-start.41 = (f32[1024]{0:T(1024)S(1)}, f32[1024]{0:T(1024)}, u32[]{:S(2)}) copy-start(f32[1024]{0:T(1024)} %copy-done.40) | copy-start | bytes 12292
  567.8 153.4 %copy-start.43 = (f32[784]{0:T(1024)S(1)}, f32[784]{0:T(1024)}, u32[]{:S(2)}) copy-start(f32[784]{0:T(1024)} %copy-done.42) | copy-start | bytes 9412
  665.1 59.1 %copy-start.48 = (f32[512]{0:T(512)S(1)}, f32[512]{0:T(512)}, u32[]{:S(2)}) copy-start(f32[512]{0:T(512)} %get-tuple-element.53) | copy-start | bytes 6148
  665.1 59.1 %copy-start.49 = (f32[512]{0:T(512)S(1)}, f32[512]{0:T(512)}, u32[]{:S(2)}) copy-start(f32[512]{0:T(512)} %get-tuple-element.60) | copy-start | bytes 6148
  665.1 59.1 %copy-start.50 = (f32[512]{0:T(512)S(1)}, f32[512]{0:T(512)}, u32[]{:S(2)}) copy-start(f32[512]{0:T(512)} %get-tuple-element.20) | copy-start | bytes 6148
  665.1 59.1 %copy-start.51 = (f32[512]{0:T(512)S(1)}, f32[512]{0:T(512)}, u32[]{:S(2)}) copy-start(f32[512]{0:T(512)} %get-tuple-element.28) | copy-start | bytes 6148
  (59 other events, 572.5 us)
Sparse Core Ops, SparseCore 0:
  14.6 49.8 all-gather.5
  88.2 28.8 all-gather.7
  183.3 38.3 reduce-scatter.5
  225.0 28.8 all-gather.9
  256.0 28.8 all-gather.11
  310.3 38.3 reduce-scatter.9
  351.3 38.3 reduce-scatter.7
  395.8 28.8 all-gather.13
  498.0 38.3 reduce-scatter.11
  562.0 97.6 all-reduce.4
  662.3 58.8 reduce-scatter.13
where the time goes:
time: 780 us; the launch traced here: 774 us
  waiting for transfers between devices  421 us (54%)
  matrix products  113 us (14%)
  local copies, waits for them, and re-layouts  94.4 us (12%)
  blocking collectives  62.7 us (8%)
  other arithmetic  59.8 us (8%)
  between operations  14.9 us (2%)
  starting transfers between devices  8.31 us (1%)
    psum x1, waiting for transfers between devices, on_device(): lax.psum(d_merge_weight.astype(jnp.bfloat16), 'sp').astype(jnp.float32)  66.2 us
    reduce_scatter x1, waiting for transfers between devices, on_device(): lax.psum_scatter(contract_cols(d_cols, merge_weight).astype(jnp.bfloat16)...  52.7 us
    all_gather x1, waiting for transfers between devices, on_device(): merged_rows = lax.all_gather(merged, 'tp', axis=0, tiled=True)  49.9 us
    psum x1, blocking collectives, on_device(): lax.psum((d_merge_gain, d_merge_bias, d_attn_gain, d_attn_bias, d_proj_bi...  39.9 us
    reduce_scatter x1, waiting for transfers between devices, on_device(): lax.psum_scatter(jnp.dot(lax.slice_in_dim(hidden, 0, lax.axis_size('tp')...  38.4 us
    reduce_scatter x1, waiting for transfers between devices, on_device(): lax.psum_scatter(jnp.dot(attended, proj_weight, preferred_element_type=jn...  37.9 us
    dot_general x4, matrix products, contract_cols(): lax.dot_general(left_side, right_side, (((1,), (1,)), ((), ())), preferre...  31 us
    reduce_scatter x1, waiting for transfers between devices, on_device(): lax.psum_scatter(jnp.einsum('qut,xut->qx', projected_gradient, query_key_...  29.9 us
  transfers between devices with their start and end apart: 13, of which 13 were waited for; matrix products, arithmetic and copies ran while one was open for 7% of the time, Pallas kernels for 0%

commit v1 on v0

--- a/solution.py
+++ b/solution.py
@@ -161,90 +161,81 @@
     tp_index = lax.axis_index("tp")
     valid_mine = lax.dynamic_slice_in_dim(window_valid, tp_index * windows, windows, 0)
     keep_rows = jnp.repeat(valid_mine.astype(jnp.float32), SIDE * SIDE)[:, None]
-    query_key_value_rows, qv_all, table_all, proj_all, up_all, up_bias_all, down_all = (
-        query_key_value_weight,
-        qv_bias,
-        rel_table,
-        proj_weight,
-        up_weight,
-        up_bias,
-        down_weight,
-    )
+    gather_last = lambda block: lax.all_gather(block, "tp", axis=block.ndim - 1, tiled=True)
+    gather_first = lambda block: lax.all_gather(block, "tp", axis=0, tiled=True)
+    merge_all = gather_last(merge_weight)
+    qkv_all = gather_last(query_key_value_weight)
+    qv_all = gather_last(qv_bias)
+    table_all = gather_last(rel_table)
+    proj_all = gather_first(proj_weight)
+    up_all = gather_last(up_weight)
+    up_bias_all = gather_first(up_bias)
+    down_all = gather_first(down_weight)
+    edge_mine = lax.dynamic_slice_in_dim(window_edge, tp_index * windows, windows, 0)
+    merge_gain_f = merge_gain.astype(jnp.float32)
     merged, merge_hat, merge_inv = norm_forward(
-        inputs.astype(jnp.float32), merge_gain.astype(jnp.float32), merge_bias.astype(jnp.float32)
+        inputs.astype(jnp.float32), merge_gain_f, merge_bias.astype(jnp.float32)
     )
     merged = merged.astype(jnp.bfloat16)
-    merged_rows = lax.all_gather(merged, "tp", axis=0, tiled=True)
-    section_cols = jnp.dot(merged_rows, merge_weight, preferred_element_type=jnp.float32).astype(
+    section_out = jnp.dot(merged, merge_all, preferred_element_type=jnp.float32).astype(
         jnp.bfloat16
     )
-    section_out = lax.all_to_all(section_cols, "tp", split_axis=0, concat_axis=1, tiled=True)
     section_float = section_out.astype(jnp.float32)
     attn_gain_f = attn_gain.astype(jnp.float32)
     attn_normed, attn_hat, attn_inv = norm_forward(
         section_float, attn_gain_f, attn_bias.astype(jnp.float32)
     )
     attention_input = attn_normed.astype(jnp.bfloat16)
-    attention_rows = lax.all_gather(attention_input, "tp", axis=0, tiled=True)
     projected_rows = jnp.einsum(
-        "tv,vfq->tfq", attention_rows, query_key_value_rows, preferred_element_type=jnp.float32
+        "tv,vfq->tfq", attention_input, qkv_all, preferred_element_type=jnp.float32
     )
     queries = (projected_rows[:, 0] + qv_all[0].astype(jnp.float32)).astype(jnp.bfloat16)
     key_rows = projected_rows[:, 1].astype(jnp.bfloat16)
     value_rows = (projected_rows[:, 2] + qv_all[1].astype(jnp.float32)).astype(jnp.bfloat16)
-    onehot, allowed = window_tables(window_edge)
+    onehot, allowed = window_tables(edge_mine)
     bias_heads = jnp.einsum(
         "ijr,rh->hij", onehot, table_all.astype(jnp.float32), precision=FULL_PRECISION
     )
     attended, log_total = attend_forward(queries, key_rows, value_rows, bias_heads, allowed)
-    attn_out = lax.psum_scatter(
-        jnp.dot(attended, proj_weight, preferred_element_type=jnp.float32).astype(jnp.bfloat16),
-        "tp",
-        scatter_dimension=0,
-        tiled=True,
-    ).astype(jnp.float32)
+    attn_out = jnp.dot(attended, proj_all, preferred_element_type=jnp.float32)
     residual = section_float + attn_out + proj_bias.astype(jnp.float32)
     mlp_gain_f = mlp_gain.astype(jnp.float32)
     mlp_normed, mlp_hat, mlp_inv = norm_forward(residual, mlp_gain_f, mlp_bias.astype(jnp.float32))
     mlp_in = mlp_normed.astype(jnp.bfloat16)
-    mlp_rows = lax.all_gather(mlp_in, "tp", axis=0, tiled=True)
-    pre_act = jnp.dot(mlp_rows, up_all, preferred_element_type=jnp.float32) + up_bias_all.astype(
+    pre_act = jnp.dot(mlp_in, up_all, preferred_element_type=jnp.float32) + up_bias_all.astype(
         jnp.float32
     )
     hidden_float, gelu_pullback = jax.vjp(partial(jax.nn.gelu, approximate=False), pre_act)
     hidden = hidden_float.astype(jnp.bfloat16)
-    mlp_out = lax.psum_scatter(
-        jnp.dot(
-            lax.slice_in_dim(hidden, 0, lax.axis_size("tp") * row_count, axis=0),
-            down_weight,
-            preferred_element_type=jnp.float32,
-        ).astype(jnp.bfloat16),
-        "tp",
-        scatter_dimension=0,
-        tiled=True,
-    ).astype(jnp.float32)
+    mlp_out = jnp.dot(hidden, down_all, preferred_element_type=jnp.float32)
     block_out = ((residual + mlp_out + down_bias.astype(jnp.float32)) * keep_rows).astype(
         jnp.bfloat16
     )
+    scatter_last = lambda grad: lax.psum(
+        lax.psum_scatter(
+            grad.astype(jnp.bfloat16), "tp", scatter_dimension=grad.ndim - 1, tiled=True
+        ),
+        "sp",
+    ).astype(jnp.float32)
+    scatter_first = lambda grad: lax.psum(
+        lax.psum_scatter(grad.astype(jnp.bfloat16), "tp", scatter_dimension=0, tiled=True),
+        "sp",
+    ).astype(jnp.float32)
     d_out = grad_out.astype(jnp.float32) * keep_rows
     d_down_bias = jnp.sum(d_out, 0)
     d_mlp = d_out.astype(jnp.bfloat16)
-    d_mlp_rows = lax.all_gather(d_mlp, "tp", axis=0, tiled=True)
-    d_hidden = contract_cols(d_mlp_rows, down_all)
-    d_down_weight = contract_rows(hidden, d_mlp_rows)
+    d_hidden = contract_cols(d_mlp, down_all)
+    d_down_weight = scatter_first(contract_rows(hidden, d_mlp))
     d_pre = gelu_pullback(d_hidden)[0].astype(jnp.bfloat16)
     d_up_bias = jnp.sum(d_pre.astype(jnp.float32), 0)
-    d_up_weight = contract_rows(mlp_rows, d_pre)
-    d_mlp_in = lax.psum_scatter(
-        contract_cols(d_pre, up_weight).astype(jnp.bfloat16), "tp", scatter_dimension=0, tiled=True
-    ).astype(jnp.float32)
+    d_up_weight = scatter_last(contract_rows(mlp_in, d_pre))
+    d_mlp_in = contract_cols(d_pre, up_all)
     d_mlp_norm, d_mlp_gain, d_mlp_bias = norm_backward(d_mlp_in, mlp_hat, mlp_inv, mlp_gain_f)
     d_residual = d_out + d_mlp_norm
     d_proj_bias = jnp.sum(d_residual, 0)
     d_attn = d_residual.astype(jnp.bfloat16)
-    d_attn_rows = lax.all_gather(d_attn, "tp", axis=0, tiled=True)
-    d_attended = contract_cols(d_attn_rows, proj_all).astype(jnp.bfloat16)
-    d_proj_weight = contract_rows(attended, d_attn_rows)
+    d_attended = contract_cols(d_attn, proj_all).astype(jnp.bfloat16)
+    d_proj_weight = scatter_first(contract_rows(attended, d_attn))
     d_queries, d_keys, d_values, d_bias = attend_backward(
         d_attended, queries, key_rows, value_rows, bias_heads, allowed, log_total
     )
@@ -253,46 +244,24 @@
         [jnp.sum(d_queries.astype(jnp.float32), 0), jnp.sum(d_values.astype(jnp.float32), 0)]
     )
     projected_gradient = jnp.stack([d_queries, d_keys, d_values], axis=1)
-    d_qkv_weight = jnp.einsum(
-        "pi,pyt->iyt", attention_rows, projected_gradient, preferred_element_type=jnp.float32
-    )
-    d_attn_in = lax.psum_scatter(
+    d_qkv_weight = scatter_last(
         jnp.einsum(
-            "qut,xut->qx",
-            projected_gradient,
-            query_key_value_weight,
-            preferred_element_type=jnp.float32,
-        ).astype(jnp.bfloat16),
-        "tp",
-        scatter_dimension=0,
-        tiled=True,
-    ).astype(jnp.float32)
+            "pi,pyt->iyt", attention_input, projected_gradient, preferred_element_type=jnp.float32
+        )
+    )
+    d_attn_in = jnp.einsum(
+        "qut,xut->qx", projected_gradient, qkv_all, preferred_element_type=jnp.float32
+    )
     d_attn_norm, d_attn_gain, d_attn_bias = norm_backward(
         d_attn_in, attn_hat, attn_inv, attn_gain_f
     )
     d_section = (d_residual + d_attn_norm).astype(jnp.bfloat16)
-    d_cols = lax.all_to_all(d_section, "tp", split_axis=1, concat_axis=0, tiled=True)
-    d_merge_weight = contract_rows(merged_rows, d_cols)
-    d_merged = lax.psum_scatter(
-        contract_cols(d_cols, merge_weight).astype(jnp.bfloat16),
-        "tp",
-        scatter_dimension=0,
-        tiled=True,
-    ).astype(jnp.float32)
+    d_merge_weight = scatter_last(contract_rows(merged, d_section))
+    d_merged = contract_cols(d_section, merge_all)
     d_inputs, d_merge_gain, d_merge_bias = norm_backward(
-        d_merged, merge_hat, merge_inv, merge_gain.astype(jnp.float32)
-    )
-    shard_sums = (
-        lax.psum(d_merge_weight.astype(jnp.bfloat16), "sp").astype(jnp.float32),
-        lax.psum(d_qkv_weight.astype(jnp.bfloat16), "sp").astype(jnp.float32),
-        lax.psum(d_qv_bias.astype(jnp.bfloat16), "sp").astype(jnp.float32),
-        lax.psum(d_rel_table.astype(jnp.bfloat16), "sp").astype(jnp.float32),
-        lax.psum(d_proj_weight.astype(jnp.bfloat16), "sp").astype(jnp.float32),
-        lax.psum(d_up_weight.astype(jnp.bfloat16), "sp").astype(jnp.float32),
-        lax.psum(d_up_bias.astype(jnp.bfloat16), "sp").astype(jnp.float32),
-        lax.psum(d_down_weight.astype(jnp.bfloat16), "sp").astype(jnp.float32),
-    )
-    shared_sums = lax.psum(
+        d_merged, merge_hat, merge_inv, merge_gain_f
+    )
+    sums = lax.psum(
         (
             d_merge_gain,
             d_merge_bias,
@@ -302,28 +271,37 @@
             d_mlp_gain,
             d_mlp_bias,
             d_down_bias,
+            d_qv_bias,
+            d_rel_table,
+            d_up_bias,
         ),
         ("sp", "tp"),
+    )
+    mine_last = lambda whole: lax.dynamic_slice_in_dim(
+        whole,
+        tp_index * (whole.shape[-1] // lax.axis_size("tp")),
+        whole.shape[-1] // lax.axis_size("tp"),
+        whole.ndim - 1,
     )
     return (
         block_out,
         d_inputs,
-        shared_sums[0],
-        shared_sums[1],
-        shard_sums[0],
-        shared_sums[2],
-        shared_sums[3],
-        shard_sums[1],
-        shard_sums[2],
-        shard_sums[3],
-        shard_sums[4],
-        shared_sums[4],
-        shared_sums[5],
-        shared_sums[6],
-        shard_sums[5],
-        shard_sums[6],
-        shard_sums[7],
-        shared_sums[7],
+        sums[0],
+        sums[1],
+        d_merge_weight,
+        sums[2],
+        sums[3],
+        d_qkv_weight,
+        mine_last(sums[8]),
+        mine_last(sums[9]),
+        d_proj_weight,
+        sums[4],
+        sums[5],
+        sums[6],
+        d_up_weight,
+        mine_last(sums[10]),
+        d_down_weight,
+        sums[7],
     )
 
 

time: 780 us -> 476 us (0.61)
  waiting for transfers between devices: 421 us -> 160 us
  other arithmetic: 59.8 us -> 35.7 us
  matrix products: 113 us -> 94.9 us
    all_gather x5 -> x4, waiting for transfers between devices: 155 us -> 0.05 us  [the longest x3 0.04 us: on_device(): lax.all_gather(block, 'tp', axis=block.ndim - 1, tiled=True)]
    reduce_scatter x5 -> x3, waiting for transfers between devices: 185 us -> 88.5 us  [the longest x2 54.5 us: on_device(): lax.psum_scatter(grad.astype(jnp.bfloat16), 'tp', scatter_dimension=0, ti...]
    all_gather x0 -> x4, blocking collectives: none -> 27 us  [the longest x2 15.7 us: on_device(): gather_first = lambda block: lax.all_gather(block, 'tp', axis=0, tiled=True)]
    psum x1 -> x0, blocking collectives: 22.8 us -> none  [on_device(): lax.psum(d_qv_bias.astype(jnp.bfloat16), 'sp').astype(jnp.float32)]
    unnamed x11 -> x12, waiting for transfers between devices: 0.18 us -> 22.1 us
    psum x1, waiting for transfers between devices: 66.2 us -> 49.1 us  [on_device(): lax.psum(lax.psum_scatter(grad.astype(jnp.bfloat16), 'tp', scatter_dimens...]
    all_to_all x2 -> x0, waiting for transfers between devices: 15.5 us -> none  [the longest x1 11.7 us: on_device(): lax.all_to_all(section_cols, 'tp', split_axis=0, concat_axis=1, tiled=True)]
    convert_element_type x16 -> x7, other arithmetic: 25.2 us -> 9.9 us  [the longest x3 5.91 us: on_device(): scatter_last = lambda grad: lax.psum(lax.psum_scatter(grad.astype(jnp.bfl...]
  transfers between devices with their start and end apart: 13 -> 10, of which waited for: 13 -> 5; matrix products, arithmetic and copies ran while one was open for 7% -> 28% of each run, Pallas kernels for 0% -> 0%
where the time goes in v1:
time: 476 us; the launch traced here: 470 us
  waiting for transfers between devices  160 us (34%)
  matrix products  94.9 us (20%)
  local copies, waits for them, and re-layouts  93.4 us (20%)
  blocking collectives  70.2 us (15%)
  other arithmetic  35.7 us (8%)
  between operations  15.3 us (3%)
    reduce_scatter x2, waiting for transfers between devices, on_device(): lax.psum_scatter(grad.astype(jnp.bfloat16), 'tp', scatter_dimension=0, ti...  54.5 us
    psum x1, waiting for transfers between devices, on_device(): lax.psum(lax.psum_scatter(grad.astype(jnp.bfloat16), 'tp', scatter_dimens...  49.1 us
    psum x1, blocking collectives, on_device(): lax.psum((d_merge_gain, d_merge_bias, d_attn_gain, d_attn_bias, d_proj_bi...  43.2 us
    reduce_scatter x1, waiting for transfers between devices, on_device(): lax.psum_scatter(grad.astype(jnp.bfloat16), 'tp', scatter_dimension=grad....  34 us
    unnamed x130, local copies, waits for them, and re-layouts  25.6 us
    unnamed x12, waiting for transfers between devices  22.1 us
    dot_general x1, matrix products, on_device(): jnp.dot(mlp_in, up_all, preferred_element_type=jnp.float32)  19.4 us
    dot_general x4, matrix products, contract_rows(): lax.dot_general(left_side, right_side, (((0,), (0,)), ((), ())), preferre...  17 us
  transfers between devices with their start and end apart: 10, of which 5 were waited for; matrix products, arithmetic and copies ran while one was open for 28% of the time, Pallas kernels for 0%

profile of v1, /device:TPU:0, one launch (start us, length us, event | category | flops | bytes accessed | tf_op | source)
XLA Modules:
  0.0 469.9 jit_solution(4562165764583428442)
XLA Ops:
  15.5 6.1 %all_gather.26 = bf16[2,512]{1,0:T(2,128)(2,1)S(1)} all-gather(bf16[2,128]{1,0:T(2,128)(2,1)} %param.30), channel_id=1, replica_groups=mesh['sp'=8,'tp'=4] {'tp'}, dimensions={1}, use_global_device_ids=true | all-gather | bytes 2560 | tf_op jit(solution)/shard_map/all_gather | solution.py:164
  28.0 5.3 %all-gather.1 = bf16[4,1,512]{2,1,0:T(2,128)(2,1)S(1)} all-gather(bf16[1,1,512]{2,1,0:T(2,128)(2,1)S(1)} %reshape.400), channel_id=1, replica_groups=mesh['sp'=8,'tp'=4] {'tp'}, dimensions={0}, use_global_device_ids=true | all-gather | bytes 5120 | tf_op jit(solution)/shard_map/all_gather | solution.py:165
  35.4 5.2 %all-gather = bf16[4,4,169]{2,1,0:T(4,128)(2,1)S(1)} all-gather(bf16[1,4,169]{2,1,0:T(4,128)(2,1)S(1)} %bitcast.90), channel_id=1, replica_groups=mesh['sp'=8,'tp'=4] {'tp'}, dimensions={0}, use_global_device_ids=true | all-gather | bytes 6760 | tf_op jit(solution)/shard_map/all_gather | solution.py:164
  42.8 10.3 %all_gather.28 = bf16[512,512]{1,0:T(8,128)(2,1)} all-gather(bf16[128,512]{1,0:T(8,128)(2,1)S(1)} %copy-done.26), channel_id=1, replica_groups=mesh['sp'=8,'tp'=4] {'tp'}, dimensions={0}, use_global_device_ids=true | all-gather | bytes 655360 | tf_op jit(solution)/shard_map/all_gather | solution.py:165
  65.3 5.6 %squeeze.10 = f32[16,49,16,32]{1,0,3,2:T(8,128)} reshape(f32[784,1,512]{0,2,1:T(8,128)} %copy.74) | data formatting | bytes 3211264 | tf_op jit(solution)/shard_map/squeeze | solution.py:192
  70.9 4.5 squeeze.4
  104.0 19.4 %multiply_convert_fusion.1 = (bf16[784,2048]{1,0:T(8,128)(2,1)}, f32[784,2048]{1,0:T(8,128)}, f32[784,2048]{1,0:T(8,128)}) fusion(f32[2048]{0:T(1024)S(1)} %bitcast.88, bf16[512,2048]{1,0:T(8,128)(2,1)} %all-gather.11.cloned.1.call-done, f32[784,512]{1,0:T(8,128)S(1)} %get-tuple-element.64, f32[512]{0:T(512)S(1)} %copy-done.28, f32[512]{0:T(512)S(1)} %copy-done.27, ...), kind=kOutput, calls=%fused_computation.12 | convolution fusion | flops 1752145920 | bytes 19777664 | tf_op jit(solution)/shard_map/dot_general | solution.py:205
  123.4 9.4 %convert_reduce_fusion.1 = (f32[2048]{0:T(1024)S(1)}, bf16[784,2048]{1,0:T(8,128)(2,1)S(1)}) fusion(f32[784,2048]{1,0:T(8,128)} %get-tuple-element.53, bf16[2048,512]{1,0:T(8,128)(2,1)} %all-gather.13.cloned.1.call-done, bf16[784,512]{1,0:T(8,128)(2,1)} %param.21, f32[784]{0:T(1024)S(1)} %copy-done.41, f32[784,2048]{1,0:T(8,128)} %get-tuple-element.65, ...), kind=kOutput, calls=%fused_computation.10 | convolution fusion | flops 1672665088 | bytes 18975808 | tf_op jit(solution)/shard_map/dot_general | solution.py:42
  141.2 5.5 %copy.83 = bf16[16,49,16,32]{1,3,2,0:T(8,128)(2,1)} copy(bf16[16,49,16,32]{3,2,1,0:T(8,128)(2,1)} %reshape.416) | data formatting | bytes 1605632 | tf_op jit(solution)/shard_map/reshape | solution.py:68
  146.7 7.3 %convert_reduce_fusion.2 = (f32[16,32]{1,0:T(8,128)S(1)}, bf16[16,16,32,49]{3,2,1,0:T(8,128)(2,1)}) fusion(bf16[16,49,16,32]{1,3,2,0:T(8,128)(2,1)} %copy.83, f32[16,16,49,49]{2,3,1,0:T(8,128)} %copy-done, f32[16,16,49]{2,1,0:T(8,128)S(1)} %log_add_fusion), kind=kOutput, calls=%fused_computation.27 | convolution fusion | flops 41771008 | bytes 4116480 | tf_op jit(solution)/shard_map/whij,wihd->wjhd/dot_general | solution.py:109
  165.8 4.5 copy.104
  174.2 4.3 copy.102
  182.3 4.3 copy.103
  202.2 5.1 %convolution_convert_fusion.2 = bf16[512,3,512]{2,0,1:T(8,128)(2,1)} fusion(bf16[784,3,512]{2,0,1:T(8,128)(2,1)} %copy-done.25, bf16[784,512]{1,0:T(8,128)(2,1)} %copy-done.17, f32[512]{0:T(512)S(1)} %copy-done.51, f32[512]{0:T(512)S(1)} %copy-done.45, f32[784]{0:T(1024)S(1)} %copy-done.43, f32[784]{0:T(1024)S(1)} %copy-done.32), kind=kOutput, calls=%fused_computation.73 | convolution fusion | flops 1236320256 | bytes 4794496 | tf_op jit(solution)/shard_map/pi,pyt->iyt/dot_general | solution.py:248
  207.3 4.4 copy.107
  217.8 6.0 %convolution_convert_fusion = bf16[2048,512]{1,0:T(8,128)(2,1)} fusion(bf16[784,2048]{1,0:T(8,128)(2,1)} %get-tuple-element.52, bf16[784,512]{1,0:T(8,128)(2,1)} %param.21, f32[784]{0:T(1024)S(1)} %copy-done.41), kind=kOutput, calls=%fused_computation.51 | convolution fusion | flops 1646419968 | bytes 6114368 | tf_op jit(solution)/shard_map/dot_general | solution.py:36
  223.9 5.8 %convolution_convert_fusion.1 = bf16[512,2048]{1,0:T(8,128)(2,1)} fusion(bf16[784,2048]{1,0:T(8,128)(2,1)} %copy-done.16, f32[784,512]{1,0:T(8,128)S(1)} %copy-done.8, f32[512]{0:T(512)S(1)} %copy-done.28, f32[512]{0:T(512)S(1)} %copy-done.27, f32[784]{0:T(1024)S(1)} %add_rsqrt_fusion, f32[784]{0:T(1024)S(1)} %broadcast_multiply_fusion.4), kind=kOutput, calls=%fused_computation.52 | convolution fusion | flops 1647222784 | bytes 6924416 | tf_op jit(solution)/shard_map/dot_general | solution.py:36
  231.8 4.6 fusion.23
  238.3 19.4 %reduce-scatter.18.cloned.1.call-done = bf16[128,1536]{1,0:T(8,128)(2,1)} async-done(((bf16[512,1536]{1,0:T(8,128)(2,1)}), bf16[128,1536]{1,0:T(8,128)(2,1)}) %reduce-scatter.18.cloned.1.call-update) | async-done | bytes 393232
  262.1 20.3 %reduce-scatter.10.cloned.1.call-done = bf16[128,512]{1,0:T(8,128)(2,1)} async-done(((bf16[512,512]{1,0:T(8,128)(2,1)}), bf16[128,512]{1,0:T(8,128)(2,1)}) %reduce-scatter.10.cloned.1.call-update) | async-done | bytes 131088 | tf_op jit(solution)/shard_map/reduce_scatter | solution.py:221
  282.4 34.2 %reduce-scatter.14.cloned.1.call-done = bf16[512,512]{1,0:T(8,128)(2,1)} async-done(((bf16[2048,512]{1,0:T(8,128)(2,1)}), bf16[512,512]{1,0:T(8,128)(2,1)}) %reduce-scatter.14.cloned.1.call-update) | async-done | bytes 524304 | tf_op jit(solution)/shard_map/reduce_scatter | solution.py:221
  316.5 34.0 %reduce-scatter.12.cloned.1.call-done = bf16[512,512]{1,0:T(8,128)(2,1)} async-done(((bf16[512,2048]{1,0:T(8,128)(2,1)}), bf16[512,512]{1,0:T(8,128)(2,1)}) %reduce-scatter.12.cloned.1.call-update) | async-done | bytes 524304 | tf_op jit(solution)/shard_map/reduce_scatter | solution.py:215
  352.8 43.2 %all-reduce = (f32[1024]{0:T(1024)}, f32[1024]{0:T(1024)}, f32[512]{0:T(512)}, f32[512]{0:T(512)}, f32[2,512]{1,0:T(2,128)S(1)}, /*index=5*/f32[169,16]{0,1:T(8,...) all-reduce(f32[1024]{0:T(1024)S(1)} %get-tuple-element.18, ...), channel_id=1, replica_groups=mesh['sp'=8,'tp'=4] {'sp','tp'}, use_global_device_ids=true, to_apply=%region_16.17 | all-reduce | flops 10896 | bytes 87168 | tf_op jit(solution)/shard_map/psum | solution.py:264
  405.2 49.1 %all-reduce.4.cloned.1.call-done = (bf16[1024,128]{1,0:T(8,128)(2,1)}, bf16[512,3,128]{2,0,1:T(8,128)(2,1)}, bf16[128,512]{1,0:T(8,128)(2,1)}, bf16[512,512]{1,0:T(8,128)(2,1)}, bf16[512,512]{1,0:T(8,128)(2,1)}) async-done(((bf16[1024,128]{1,0:T(8,128)(2,1)}, bf16[512,3,128]{2,0,1:T(8,128)(2,1)}, bf16[128,512]{1,0:T(8,128)(2,1)}, bf16[512,512]{1,0:T(8,128)(2,1)}, bf16[512,512]{1,0:T(8,128)(2,1)}), ...) | async-done | bytes 1835024 | tf_op jit(solution)/shard_map/psum | solution.py:214
  (242 shorter events, 137.0 us)
Async XLA Ops:
  7.2 19.5 %copy-start.5 = (bf16[784,1024]{1,0:T(8,128)(2,1)S(1)}, bf16[784,1024]{1,0:T(8,128)(2,1)}, u32[]{:S(2)}) copy-start(bf16[784,1024]{1,0:T(8,128)(2,1)} %param.20) | copy-start | bytes 4816900
  7.2 28.2 %copy-start.49 = (bf16[169,4]{0,1:T(4,128)(2,1)S(1)}, bf16[169,4]{0,1:T(4,128)(2,1)}, u32[]{:S(2)}) copy-start(bf16[169,4]{0,1:T(4,128)(2,1)} %param.31) | copy-start | bytes 4060
  7.2 45.9 %all-gather.7.cloned.1.call-start = ((), (), s32[]{:S(2)}) async-start(), calls=%async_computation.5 | async-start | bytes 1310720 | tf_op jit(solution)/shard_map/all_gather | solution.py:164
  7.9 48.1 %all-gather.9.cloned.1.call-start = ((), (), s32[]{:S(2)}) async-start(), calls=%async_computation.6 | async-start | bytes 1966080 | tf_op jit(solution)/shard_map/all_gather | solution.py:164
  8.7 34.1 %copy-start.26 = (bf16[128,512]{1,0:T(8,128)(2,1)S(1)}, bf16[128,512]{1,0:T(8,128)(2,1)}, u32[]{:S(2)}) copy-start(bf16[128,512]{1,0:T(8,128)(2,1)} %param.32) | copy-start | bytes 393220
  8.7 95.3 %all-gather.11.cloned.1.call-start = ((), (), s32[]{:S(2)}) async-start(), calls=%async_computation.7 | async-start | bytes 2621440 | tf_op jit(solution)/shard_map/all_gather | solution.py:164
  9.4 114.0 %all-gather.13.cloned.1.call-start = ((), (), s32[]{:S(2)}) async-start(), calls=%async_computation.8 | async-start | bytes 2621440 | tf_op jit(solution)/shard_map/all_gather | solution.py:165
  10.0 226.4 %reduce-scatter.16.cloned.1.call-start = ((), (), s32[]{:S(2)}) async-start(), calls=%async_computation.12 | async-start | bytes 1310720
  12.3 43.8 %copy-start.44 = (f32[512]{0:T(512)}, f32[512]{0:T(512)S(1)}, u32[]{:S(2)}) copy-start(f32[512]{0:T(512)S(1)} %convert_element_type.227) | copy-start | bytes 6148
  14.2 41.8 %copy-start.50 = (f32[512]{0:T(512)}, f32[512]{0:T(512)S(1)}, u32[]{:S(2)}) copy-start(f32[512]{0:T(512)S(1)} %convert_element_type.228) | copy-start | bytes 6148
  24.3 31.2 %copy-start.37 = (f32[1024]{0:T(1024)}, f32[1024]{0:T(1024)S(1)}, u32[]{:S(2)}) copy-start(f32[1024]{0:T(1024)S(1)} %convert_element_type.222) | copy-start | bytes 12292
  25.0 30.5 %copy-start.47 = (f32[1024]{0:T(1024)}, f32[1024]{0:T(1024)S(1)}, u32[]{:S(2)}) copy-start(f32[1024]{0:T(1024)S(1)} %convert_element_type.223) | copy-start | bytes 12292
  26.7 28.8 %copy-start.29 = (f32[784]{0:T(1024)}, f32[784]{0:T(1024)S(1)}, u32[]{:S(2)}) copy-start(f32[784]{0:T(1024)S(1)} %broadcast_multiply_fusion.8) | copy-start | bytes 9412
  27.3 28.2 %copy-start.39 = (f32[784]{0:T(1024)}, f32[784]{0:T(1024)S(1)}, u32[]{:S(2)}) copy-start(f32[784]{0:T(1024)S(1)} %add_rsqrt_fusion.2) | copy-start | bytes 9412
  101.2 22.2 %copy-start.15 = (bf16[784,512]{0,1:T(8,128)(2,1)}, bf16[784,512]{0,1:T(8,128)(2,1)S(1)}, u32[]{:S(2)}) copy-start(bf16[784,512]{0,1:T(8,128)(2,1)S(1)} %convert_element_type.238) | copy-start | bytes 2408452
  103.6 31.7 %copy-start.7 = (f32[784,512]{1,0:T(8,128)}, f32[784,512]{1,0:T(8,128)S(1)}, u32[]{:S(2)}) copy-start(f32[784,512]{1,0:T(8,128)S(1)} %get-tuple-element.64) | copy-start | bytes 4816900
  104.0 19.4 %copy-start.41 = (f32[784]{0:T(1024)S(1)}, f32[784]{0:T(1024)}, u32[]{:S(2)}) copy-start(f32[784]{0:T(1024)} %mul.299) | copy-start | bytes 9412
  141.2 12.8 %slice-start = ((s8[7340032]{0:T(1024)(128)(4,1)}), s8[3145728]{0:T(1024)(128)(4,1)S(1)}, s32[]{:S(2)}) async-start(s8[7340032]{0:T(1024)(128)(4,1)} %bitcast.79), calls=%async_computation.15 | async-start | bytes 6291456
  201.8 55.9 %reduce-scatter.18.cloned.1.call-start = ((), (), s32[]{:S(2)}) async-start(), calls=%async_computation.13 | async-start | bytes 1966080
  215.0 67.4 %reduce-scatter.10.cloned.1.call-start = ((), (), s32[]{:S(2)}) async-start(), calls=%async_computation.9 | async-start | bytes 655360 | tf_op jit(solution)/shard_map/reduce_scatter | solution.py:221
  217.8 98.8 %reduce-scatter.14.cloned.1.call-start = ((), (), s32[]{:S(2)}) async-start(), calls=%async_computation.11 | async-start | bytes 2621440 | tf_op jit(solution)/shard_map/reduce_scatter | solution.py:221
  223.9 126.7 %reduce-scatter.12.cloned.1.call-start = ((), (), s32[]{:S(2)}) async-start(), calls=%async_computation.10 | async-start | bytes 2621440 | tf_op jit(solution)/shard_map/reduce_scatter | solution.py:215
  229.7 224.5 %all-reduce.4.cloned.1.call-start = ((), (), s32[]{:S(2)}) async-start(), calls=%async_computation.14 | async-start | bytes 3670016 | tf_op jit(solution)/shard_map/psum | solution.py:214
  236.4 114.1 %copy-start.36 = (s32[49,49]{1,0:T(8,128)S(1)}, s32[49,49]{1,0:T(8,128)}, u32[]{:S(2)}) copy-start(s32[49,49]{1,0:T(8,128)} %copy-done.35) | copy-start | bytes 28816
  (46 other events, 175.5 us)
Sparse Core Ops, SparseCore 0:
  9.6 19.5 all-gather.6
  30.7 22.4 all-gather.8
  54.8 22.1 all-gather.10
  78.4 22.5 all-gather.12
  201.9 24.9 reduce-scatter.15
  229.4 28.1 reduce-scatter.17
  260.7 21.6 reduce-scatter.9
  285.1 31.4 reduce-scatter.13
  319.1 31.4 reduce-scatter.11
  355.7 98.4 all-reduce.3

commit v2 on v1

v2 whole, which is shorter than its diff:
```python
import functools
import math

import jax
import jax.numpy as jnp
from jax import lax
from jax.experimental import pallas as pl
from jax.experimental.pallas import tpu as pltpu
from jax.sharding import PartitionSpec as P

SIDE = 7
TOK = SIDE * SIDE
REL_SIDE = 2 * SIDE - 1
REL = REL_SIDE * REL_SIDE
SPAN = 64
GROUP = 4
HD = 32
LANES = 128
EPSILON = 1e-05
NEG_FILL = -1000000000.0
MIB = 1 << 20
F32 = jnp.float32
BF16 = jnp.bfloat16


def dot(left, right):
    return jnp.dot(left, right, preferred_element_type=F32)


def dot_cols(left, right):
    return lax.dot_general(left, right, (((1,), (1,)), ((), ())), preferred_element_type=F32)


def dot_rows(left, right):
    return lax.dot_general(left, right, (((0,), (0,)), ((), ())), preferred_element_type=F32)


def rows_at(index, size):
    return pl.ds(pl.multiple_of(index * size, size), size)


def each(count, body, unroll=1):
    def step(index, carry):
        body(index)
        return carry

    lax.fori_loop(0, count, step, 0, unroll=unroll)


def fold(values):
    total = values[0:8]
    for start in range(8, values.shape[0], 8):
        total = total + values[start : start + 8]
    return total


def iota(shape, dim):
    return lax.broadcasted_iota(jnp.int32, shape, dim)


def norm_rows(values):
    mean = jnp.mean(values, -1, keepdims=True)
    centred = values - mean
    inv = lax.rsqrt(jnp.mean(centred * centred, -1, keepdims=True) + EPSILON)
    return centred * inv, mean, inv


def norm_back(upstream, normed, inv, gain):
    scaled = upstream * gain
    return inv * (
        scaled
        - jnp.mean(scaled, -1, keepdims=True)
        - normed * jnp.mean(scaled * normed, -1, keepdims=True)
    )


def gelu_both(values):
    size = jnp.abs(values) * 0.7071067811865476
    bell = jnp.exp(-size * size)
    t = 1.0 / (1.0 + 0.3275911 * size)
    poly = t * (
        0.254829592
        + t * (-0.284496736 + t * (1.421413741 + t * (-1.453152027 + t * 1.061405429)))
    )
    tail = 0.5 * poly * bell
    phi = jnp.where(values >= 0, 1.0 - tail, tail)
    return values * phi, phi + values * bell * 0.3989422804014327


def window_row_col(index):
    row = (index * 37) >> 8
    return row, index - SIDE * row


def region_ids(index, edge, outside):
    row, col = window_row_col(index)
    high = SIDE - SIDE // 2
    region = (edge & 1) * (col >= high).astype(jnp.int32) + 2 * (edge >> 1) * (
        row >= high
    ).astype(jnp.int32)
    return jnp.where((index >= 0) & (index < TOK), region, outside)


def head_masks():
    lane = iota((1, LANES), 1)
    return [((lane >> 5) == head).astype(F32).astype(BF16) for head in range(GROUP)]


def spread_heads(block, masks):
    return jnp.concatenate([block * mask for mask in masks], axis=0)


def pick_heads(product):
    lane = iota((SPAN, LANES), 1)
    result = product[3 * SPAN : 4 * SPAN]
    for head in (2, 1, 0):
        result = jnp.where(
            lane < (head + 1) * HD, product[head * SPAN : (head + 1) * SPAN], result
        )
    return result


def same_head(rows, columns):
    return (
        (iota((rows, columns), 0) // (rows // GROUP))
        == (iota((rows, columns), 1) // (columns // GROUP))
    ).astype(F32).astype(BF16)


def offset_select(half):
    place = iota((LANES, LANES), 0)
    lane = iota((LANES, LANES), 1)
    token = lane - half * SPAN
    row, col = window_row_col(token & (SPAN - 1))
    wanted = (SIDE - 1) * (REL_SIDE + 1) - (REL_SIDE * row + col)
    hit = (place == wanted) & (token >= 0) & (token < TOK)
    return hit.astype(F32).astype(BF16)


def build_bias(table, spread_ref, bias_ref):
    heads = table.shape[0]

    def one(index):
        row = index // SIDE
        shift = index + (SIDE - 1) * row
        rolled = pltpu.roll(table, (2 * LANES - shift) % (2 * LANES), 1)
        spread_ref[rows_at(index, heads), :] = rolled[:, :LANES]

    spread_ref[...] = jnp.zeros_like(spread_ref)
    for index in range(TOK):
        one(index)
    low, high = offset_select(0), offset_select(1)
    for pair in range(heads // 2):
        first = spread_ref[pl.ds(2 * pair, SPAN, stride=heads), :].astype(BF16)
        second = spread_ref[pl.ds(2 * pair + 1, SPAN, stride=heads), :].astype(BF16)
        bias_ref[:, pair * LANES : (pair + 1) * LANES] = dot(first, low) + dot(second, high)


def split_bf16(values):
    high = values.astype(BF16)
    return high, (values - high.astype(F32)).astype(BF16)


def reduce_bias(bias_ref, spread_ref, heads):
    low, high = offset_select(0), offset_select(1)
    for pair in range(heads // 2):
        parts = split_bf16(bias_ref[:, pair * LANES : (pair + 1) * LANES])
        spread_ref[pl.ds(2 * pair, SPAN, stride=heads), :] = sum(
            dot_cols(part, low) for part in parts
        )
        spread_ref[pl.ds(2 * pair + 1, SPAN, stride=heads), :] = sum(
            dot_cols(part, high) for part in parts
        )
    total = jnp.zeros((heads, 2 * LANES), F32)
    blank = jnp.zeros((heads, LANES), F32)
    for index in range(TOK):
        shift = index + (SIDE - 1) * (index // SIDE)
        row = jnp.concatenate([spread_ref[index * heads : (index + 1) * heads, :], blank], axis=1)
        total = total + (pltpu.roll(row, shift, 1) if shift else row)
    return total


def shift_both(ref, forward):
    rows, columns = ref.shape
    down, right = (1, 1) if forward else (rows - 1, columns - 1)
    ref[...] = pltpu.roll(pltpu.roll(ref[...], down, 0), right, 1)


def attention_forward(window, edge, qkv, bias_ref, probs_ref, att_ref):
    base = pl.ds(pl.multiple_of(window * (TOK - 1), 16), SPAN)
    masks = head_masks()
    ones = same_head(GROUP * SPAN, GROUP * SPAN)
    row_index = iota((SPAN, 1), 0) - window
    row_in = (row_index >= 0) & (row_index < TOK)
    row_region = region_ids(row_index, edge, 8)
    lane_region = region_ids((iota((1, GROUP * SPAN), 1) & (SPAN - 1)) - window, edge, 16)
    allowed = row_region == lane_region
    first_half = iota((SPAN, LANES), 1) < SPAN
    keep = row_in.astype(F32)
    groups = att_ref.shape[1] // LANES
    for group in range(groups):
        lanes = pl.ds(group * LANES, LANES)
        wide = pl.ds(group * GROUP * SPAN, GROUP * SPAN)
        query, key, value = (qkv[part, base, lanes] for part in range(3))
        logits = dot_cols(query, spread_heads(key, masks)) * (HD**-0.5) + bias_ref[:, wide]
        logits = jnp.where(allowed, logits, NEG_FILL)
        tops = []
        for half in range(GROUP * SPAN // LANES):
            piece = logits[:, half * LANES : (half + 1) * LANES]
            top_low = jnp.max(jnp.where(first_half, piece, 2 * NEG_FILL), -1, keepdims=True)
            top_high = jnp.max(jnp.where(first_half, 2 * NEG_FILL, piece), -1, keepdims=True)
            tops.append(jnp.where(first_half, top_low, top_high))
        terms = jnp.exp(logits - jnp.concatenate(tops, axis=1))
        totals = dot(terms.astype(BF16), ones)
        probs = (terms * (keep / totals)).astype(BF16)
        probs_ref[window, :, wide] = probs
        attended = dot(probs, spread_heads(value, masks))
        att_ref[base, lanes] = jnp.where(
            row_in, attended, att_ref[base, lanes].astype(F32)
        ).astype(BF16)


def attention_backward(window, qkv, d_att, probs_ref, d_bias_ref, d_qkv):
    base = pl.ds(pl.multiple_of(window * (TOK - 1), 16), SPAN)
    masks = head_masks()
    ones = same_head(GROUP * SPAN, GROUP * SPAN)
    row_index = iota((SPAN, 1), 0) - window
    row_in = (row_index >= 0) & (row_index < TOK)
    groups = d_att.shape[1] // LANES
    factor = HD**-0.5

    def put(part, lanes, values):
        d_qkv[part, base, lanes] = jnp.where(
            row_in, values, d_qkv[part, base, lanes].astype(F32)
        ).astype(BF16)

    for group in range(groups):
        lanes = pl.ds(group * LANES, LANES)
        wide = pl.ds(group * GROUP * SPAN, GROUP * SPAN)
        query, key, value = (qkv[part, base, lanes] for part in range(3))
        upstream = d_att[base, lanes]
        probs = probs_ref[window, :, wide]
        probs_wide = probs.astype(F32)
        d_probs = dot_cols(upstream, spread_heads(value, masks))
        weighted = d_probs * probs_wide
        delta = dot(weighted.astype(BF16), ones)
        d_logits = (weighted - probs_wide * delta).astype(BF16)
        d_bias_ref[:, wide] += d_logits.astype(F32)
        put(0, lanes, dot(d_logits, spread_heads(key, masks)) * factor)
        put(1, lanes, pick_heads(dot_rows(d_logits, query)) * factor)
        put(2, lanes, pick_heads(dot_rows(probs, upstream)))


def sum_rows(values):
    return jnp.sum(values, 0, keepdims=True)


class Local:
    def __init__(self, refs, first_window):
        self.__dict__.update(refs)
        self.first_window = first_window
        self.rows, self.wide = self.x.shape
        self.width = self.section.shape[1]
        self.units = self.hidden.shape[1]
        self.windows = self.rows // TOK
        self.heads = self.width // HD
        self.chunk = 16
        self.steps = self.rows // self.chunk
        self.tile = self.units // self.gu.shape[0]

    def gain(self, row, lanes):
        return self.gains[row : row + 1, :lanes]

    def stat(self, at, index):
        return self.stats[at, index : index + 1]

    def keep_stats(self, at, index, mean, inv):
        self.stats[at, index : index + 1] = mean
        self.stats[at, index + 1 : index + 2] = inv

    def prepare(self):
        def keep_rows(window):
            base = pl.ds(pl.multiple_of(window * (TOK - 1), 16), SPAN)
            index = iota((SPAN, 1), 0) - window
            inside = (index >= 0) & (index < TOK)
            valid = self.valid[self.first_window + window].astype(F32)
            self.stats[base, 6:7] = jnp.where(inside, valid, self.stats[base, 6:7])

        each(self.windows, keep_rows)

    def table_bias(self):
        build_bias(self.table(), self.spread, self.bias)

    def merge_norm(self):
        gain, shift = self.gain(0, self.wide), self.gain(1, self.wide)

        def step(index):
            at = rows_at(index, self.chunk)
            normed, mean, inv = norm_rows(self.x[at, :].astype(F32))
            self.merged[at, :] = (normed * gain + shift).astype(BF16)
            self.keep_stats(at, 0, mean, inv)

        each(self.steps, step, 7)

    def merge(self):
        self.section[...] = dot(self.merged[...], self.wm[...]).astype(BF16)

    def attn_norm(self):
        gain, shift = self.gain(2, self.width), self.gain(3, self.width)

        def step(index):
            at = rows_at(index, self.chunk)
            normed, mean, inv = norm_rows(self.section[at, :].astype(F32))
            self.attn_in[at, :] = (normed * gain + shift).astype(BF16)
            self.keep_stats(at, 2, mean, inv)

        each(self.steps, step, 7)

    def project(self):
        for part in range(3):
            product = dot(self.attn_in[...], self.wqkv[part])
            if part != 1:
                product = product + self.qkv_bias(part)
            self.qkv[part] = product.astype(BF16)

    def attend(self, first, last):
        def step(index):
            window = first + index
            edge = self.edge[self.first_window + window]
            attention_forward(window, edge, self.qkv, self.bias, self.probs, self.att)
            shift_both(self.bias, True)

        each(last - first, step)

    def attn_out(self):
        self.resid[...] = dot(self.att[...], self.wp[...])

    def mlp_norm(self):
        gain, shift = self.gain(4, self.width), self.gain(5, self.width)
        proj_bias = self.gain(6, self.width)

        def step(index):
            at = rows_at(index, self.chunk)
            total = self.section[at, :].astype(F32) + self.resid[at, :] + proj_bias
            self.resid[at, :] = total
            normed, mean, inv = norm_rows(total)
            self.mlp_in[at, :] = (normed * gain + shift).astype(BF16)
            self.keep_stats(at, 4, mean, inv)

        each(self.steps, step, 7)

    def up(self):
        def part(index):
            columns = rows_at(index, self.tile)
            self.pre[...] = dot(self.mlp_in[...], self.wu[:, columns])
            shift = self.up_bias(index)

            def activate(step):
                at = rows_at(step, self.chunk)
                value, rate = gelu_both(self.pre[at, :] + shift)
                self.hidden[at, columns] = value.astype(BF16)
                self.slope[at, columns] = rate.astype(BF16)

            each(self.steps, activate, 7)

        each(self.units // self.tile, part)

    def down(self):
        self.pre[...] = dot(self.hidden[...], self.wd[...])

    def finish(self):
        down_bias = self.gain(7, self.width)

        def step(index, total):
            at = rows_at(index, self.chunk)
            mask = self.stat(at, 6)
            block = (self.resid[at, :] + self.pre[at, :] + down_bias) * mask
            self.out[at, :] = block.astype(BF16)
            grad = self.grad_out[at, :].astype(F32) * mask
            self.d_mlp[at, :] = grad.astype(BF16)
            return total + fold(grad)

        total = lax.fori_loop(
            0, self.steps, step, jnp.zeros((8, self.width), F32), unroll=7
        )
        self.put_sum(7, total)

    def down_back(self, index):
        columns = rows_at(index, self.tile)
        self.pre[...] = dot_cols(self.d_mlp[...], self.wd[columns, :])
        put_blocks(self.gd, index, dot_rows(self.hidden[:, columns], self.d_mlp[...]))

        def activate(step, total):
            at = rows_at(step, self.chunk)
            grad = (self.pre[at, :] * self.slope[at, columns].astype(F32)).astype(BF16)
            self.hidden[at, columns] = grad
            return total + fold(grad.astype(F32))

        total = lax.fori_loop(0, self.steps, activate, jnp.zeros((8, self.tile), F32), unroll=7)
        self.put_up_sum(index, total)
        put_blocks(self.gu, index, dot_rows(self.mlp_in[...], self.hidden[:, columns]))

    def up_back(self):
        self.pre[...] = dot_cols(self.hidden[...], self.wu[...])

    def mlp_back(self):
        gain = self.gain(4, self.width)

        def step(index, totals):
            at = rows_at(index, self.chunk)
            inv = self.stat(at, 5)
            normed = (self.resid[at, :] - self.stat(at, 4)) * inv
            upstream = self.pre[at, :]
            d_resid = self.d_mlp[at, :].astype(F32) + norm_back(upstream, normed, inv, gain)
            self.resid[at, :] = d_resid
            self.d_mlp[at, :] = d_resid.astype(BF16)
            return (
                totals[0] + fold(upstream * normed),
                totals[1] + fold(upstream),
                totals[2] + fold(d_resid),
            )

        blank = jnp.zeros((8, self.width), F32)
        totals = lax.fori_loop(0, self.steps, step, (blank, blank, blank), unroll=7)
        for row, total in zip((5, 6, 4), totals):
            self.put_sum(row, total)

    def proj_back(self):
        size = self.width // self.gp.shape[0]
        product = dot_rows(self.att[...], self.d_mlp[...])
        for index in range(self.gp.shape[0]):
            put_blocks(self.gp, index, product[index * size : (index + 1) * size])
        self.att[...] = dot_cols(self.d_mlp[...], self.wp[...]).astype(BF16)
        self.d_bias[...] = jnp.zeros_like(self.d_bias)

    def attend_back(self, first, last):
        def step(index):
            shift_both(self.d_bias, False)
            attention_backward(
                last - 1 - index, self.qkv, self.att, self.probs, self.d_bias, self.qkv
            )

        each(last - first, step)

    def bias_back(self):
        self.put_table(reduce_bias(self.d_bias, self.spread, self.heads))
        ones = jnp.full((8, self.rows), 1.0, BF16)
        self.put_sum(8, dot(ones, self.qkv[0]), True)
        self.put_sum(9, dot(ones, self.qkv[2]), True)

    def qkv_back(self):
        for part in range(3):
            put_columns(self.gqkv, part, dot_rows(self.attn_in[...], self.qkv[part]))
        self.pre[...] = (
            dot_cols(self.qkv[0], self.wqkv[0])
            + dot_cols(self.qkv[1], self.wqkv[1])
            + dot_cols(self.qkv[2], self.wqkv[2])
        )

    def attn_back(self):
        gain = self.gain(2, self.width)

        def step(index, totals):
            at = rows_at(index, self.chunk)
            inv = self.stat(at, 3)
            normed = (self.section[at, :].astype(F32) - self.stat(at, 2)) * inv
            upstream = self.pre[at, :]
            d_section = self.resid[at, :] + norm_back(upstream, normed, inv, gain)
            self.d_mlp[at, :] = d_section.astype(BF16)
            return totals[0] + fold(upstream * normed), totals[1] + fold(upstream)

        blank = jnp.zeros((8, self.width), F32)
        totals = lax.fori_loop(0, self.steps, step, (blank, blank), unroll=7)
        self.put_sum(2, totals[0])
        self.put_sum(3, totals[1])

    def merge_weight_back(self):
        put_columns(self.gm, 0, dot_rows(self.merged[...], self.d_mlp[...]))

    def merge_in_back(self):
        self.d_in[...] = dot_cols(self.d_mlp[...], self.wm[...])

    def merge_back(self):
        gain = self.gain(0, self.wide)

        def step(index, totals):
            at = rows_at(index, self.chunk)
            inv = self.stat(at, 1)
            normed = (self.x[at, :].astype(F32) - self.stat(at, 0)) * inv
            upstream = self.d_in[at, :]
            self.d_in[at, :] = norm_back(upstream, normed, inv, gain)
            return totals[0] + fold(upstream * normed), totals[1] + fold(upstream)

        blank = jnp.zeros((8, self.wide), F32)
        totals = lax.fori_loop(0, self.steps, step, (blank, blank), unroll=7)
        self.put_sum(0, totals[0])
        self.put_sum(1, totals[1])

    def put_sum(self, row, values, summed=False):
        values = values[0:1] if summed else sum_rows(values)
        for block in range(values.shape[1] // LANES):
            place = SUM_ROWS[row] + block
            self.sums[place : place + 1, :] = values[:, block * LANES : (block + 1) * LANES]

    def put_up_sum(self, index, total):
        values = sum_rows(total)
        blocks = self.tile // LANES
        for block in range(blocks):
            place = SUM_ROWS[10] + index * blocks + block
            self.sums[pl.ds(place, 1), :] = values[:, block * LANES : (block + 1) * LANES]

    def put_table(self, values):
        for half in range(2):
            place = SUM_ROWS[11] + half * self.heads
            self.sums[place : place + self.heads, :] = values[:, half * LANES : (half + 1) * LANES]


SUM_ROWS = (0, 8, 16, 20, 24, 28, 32, 36, 40, 44, 48, 64)
SUM_SIZE = 128


def put_blocks(ref, shard, values):
    rows = values.shape[0]
    for block in range(values.shape[1] // LANES):
        at = pl.ds(block * rows, rows)
        ref[shard, at, :] = values[:, block * LANES : (block + 1) * LANES].astype(BF16)


def put_columns(ref, part, values):
    rows = values.shape[0]
    for shard in range(ref.shape[0]):
        piece = values[:, shard * LANES : (shard + 1) * LANES]
        ref[shard, part * rows : (part + 1) * rows, :] = piece.astype(BF16)


def local_scratch(rows, wide, width, units):
    heads = width // HD
    windows = rows // TOK
    return dict(
        merged=pltpu.VMEM((rows, wide), BF16),
        section=pltpu.VMEM((rows, width), BF16),
        attn_in=pltpu.VMEM((rows, width), BF16),
        qkv=pltpu.VMEM((3, rows, width), BF16),
        probs=pltpu.VMEM((windows, SPAN, heads * SPAN), BF16),
        att=pltpu.VMEM((rows, width), BF16),
        resid=pltpu.VMEM((rows, width), F32),
        mlp_in=pltpu.VMEM((rows, width), BF16),
        hidden=pltpu.VMEM((rows, units), BF16),
        slope=pltpu.VMEM((rows, units), BF16),
        pre=pltpu.VMEM((rows, width), F32),
        d_mlp=pltpu.VMEM((rows, width), BF16),
        stats=pltpu.VMEM((rows, 8), F32),
        bias=pltpu.VMEM((SPAN, heads * SPAN), F32),
        d_bias=pltpu.VMEM((SPAN, heads * SPAN), F32),
        spread=pltpu.VMEM((SPAN * heads, LANES), F32),
    )


MESH_ID = pl.DeviceIdType.MESH


class Links:
    def __init__(self, send_sems, recv_sems, plan):
        self.send_sems, self.recv_sems, self.plan = send_sems, recv_sems, plan
        self.sent = []
        self.sp, self.tp = lax.axis_index("sp"), lax.axis_index("tp")

    def place(self, way):
        kind, distance = way
        if kind == "tp":
            return self.sp, self.tp ^ distance
        return self.sp ^ distance, self.tp

    def copy(self, name, way, source, target):
        slot = self.plan.setdefault(name, len(self.plan))
        return pltpu.make_async_remote_copy(
            src_ref=source,
            dst_ref=target,
            send_sem=self.send_sems.at[slot],
            recv_sem=self.recv_sems.at[slot],
            device_id=self.place(way),
            device_id_type=MESH_ID,
        )

    def send(self, name, way, source, target):
        copy = self.copy(name, way, source, target)
        copy.start()
        self.sent.append(copy)

    def receive(self, name, way, target):
        self.copy(name, way, target, target).wait_recv()

    def keep(self, name, source, target):
        slot = self.plan.setdefault(name, len(self.plan))
        copy = pltpu.make_async_copy(source, target, self.recv_sems.at[slot])
        copy.start()
        return copy

    def greet(self, ways):
        barrier = pltpu.get_barrier_semaphore()
        for way in ways:
            pl.semaphore_signal(
                barrier, inc=1, device_id=self.place(way), device_id_type=MESH_ID
            )
        pl.semaphore_wait(barrier, len(ways))

    def drain(self):
        for copy in self.sent:
            copy.wait_send()


CORE, ACROSS, BESIDE = ("tp", 1), ("tp", 2), ("sp", 1)


def far_ways(sp_size):
    return [("sp", 2 * step) for step in range(1, sp_size // 2)]


class Gather:
    def __init__(self, links, name, own, whole, view, split):
        self.links, self.name, self.own, self.whole = links, name, own, whole
        self.view, self.split = view, split
        self.half = links.sp & 1

    def part(self, shard, half=None):
        return self.view(self.whole, shard, half)

    def label(self, step):
        return (self.name, step)

    def start(self):
        links = self.links
        mine = links.tp
        self.local = links.keep(self.label("own"), self.own, self.part(mine))
        half = self.half if self.split else None
        links.send(
            self.label("x"), ACROSS, self.view(self.own, None, half), self.part(mine, half)
        )
        links.send(self.label("c"), CORE, self.own, self.part(mine))

    def forward(self):
        links = self.links
        other = links.tp ^ 2
        half = self.half if self.split else None
        block = self.part(other, half)
        links.receive(self.label("x"), ACROSS, block)
        if self.split:
            links.send(self.label("y"), BESIDE, block, block)
        links.send(self.label("xc"), CORE, block, block)

    def forward_beside(self):
        if self.split:
            links = self.links
            block = self.part(links.tp ^ 2, 1 - self.half)
            links.receive(self.label("y"), BESIDE, block)
            links.send(self.label("yc"), CORE, block, block)

    def finish(self):
        links = self.links
        self.local.wait()
        links.receive(self.label("c"), CORE, self.part(links.tp ^ 1))
        half = self.half if self.split else None
        links.receive(self.label("xc"), CORE, self.part(links.tp ^ 3, half))
        if self.split:
            links.receive(self.label("yc"), CORE, self.part(links.tp ^ 3, 1 - self.half))


def column_view(size, halves):
    def view(ref, shard, half):
        rank = len(ref.shape)
        rows = ref.shape[rank - 2]
        at = slice(None) if half is None else pl.ds(
            pl.multiple_of(half * (rows // 2), 16), rows // 2
        )
        lanes = slice(None) if shard is None else pl.ds(pl.multiple_of(shard * size, LANES), size)
        return ref.at[(slice(None),) * (rank - 2) + (at, lanes)]

    return view


def row_view(size):
    def view(ref, shard, half):
        start = 0 if shard is None else shard * size
        if half is None:
            return ref.at[pl.ds(start, size), :]
        start = start + half * (size // 2)
        return ref.at[pl.ds(pl.multiple_of(start, 16), size // 2), :]

    return view


def lead_view(ref, shard, half):
    return ref if shard is None else ref.at[shard]


def add_rows(target, start, rows, terms, chunk=128):
    chunk = math.gcd(rows, chunk)

    def step(index):
        offset = index * chunk

        def at(first):
            return pl.ds(pl.multiple_of(first + offset, 16), chunk)

        total = None
        for ref, first in terms:
            value = ref[at(first), :].astype(F32)
            total = value if total is None else total + value
        target[at(start), :] = total.astype(target.dtype)

    each(rows // chunk, step)


class Reduce:
    def __init__(self, links, name, grads, core_in, across_in, beside_in, far_in, result, group):
        self.links, self.name, self.grads = links, name, grads
        self.core_in, self.across_in, self.beside_in = core_in, across_in, beside_in
        self.far_in, self.result, self.group = far_in, result, group
        self.rows = grads.shape[1]
        self.half_rows = self.rows // 2
        self.piece = self.half_rows // group
        self.half = links.sp & 1
        self.seat = links.sp >> 1
        self.steps = [
            self.core_send, self.core_add, self.across_add, self.beside_add, self.far_add,
            self.far_done, self.beside_done,
        ]

    def run(self):
        self.steps.pop(0)()

    def label(self, *step):
        return (self.name,) + step

    def core_send(self):
        links = self.links
        for across in range(2):
            links.send(
                self.label("c", across), CORE, self.grads.at[(links.tp & 1) ^ 1 | 2 * across],
                self.core_in.at[across],
            )

    def core_add(self):
        links = self.links
        for across in range(2):
            links.receive(self.label("c", across), CORE, self.core_in.at[across])
        other = links.tp ^ 2
        block = self.grads.at[other]
        add_rows(block, 0, self.rows, [(block, 0), (self.core_in.at[other >> 1], 0)])
        links.send(self.label("x"), ACROSS, block, self.across_in)

    def across_add(self):
        links = self.links
        links.receive(self.label("x"), ACROSS, self.across_in)
        block = self.grads.at[links.tp]
        terms = [(block, 0), (self.core_in.at[links.tp >> 1], 0), (self.across_in, 0)]
        add_rows(block, 0, self.rows, terms)
        links.send(
            self.label("y"), BESIDE, self.rows_of(block, 1 - self.half), self.beside_in
        )

    def rows_of(self, ref, half, piece=None):
        if piece is None:
            return ref.at[pl.ds(pl.multiple_of(half * self.half_rows, 16), self.half_rows), :]
        start = half * self.half_rows + piece * self.piece
        return ref.at[pl.ds(pl.multiple_of(start, 16), self.piece), :]

    def beside_add(self):
        links = self.links
        links.receive(self.label("y"), BESIDE, self.beside_in)
        block = self.grads.at[links.tp]
        mine = self.half * self.half_rows
        add_rows(block, mine, self.half_rows, [(block, mine), (self.beside_in, 0)])
        for step in range(1, self.group):
            links.send(
                self.label("z", step), ("sp", 2 * step),
                self.rows_of(block, self.half, self.seat ^ step), self.far_in.at[step - 1],
            )

    def far_add(self):
        links = self.links
        block = self.grads.at[links.tp]
        mine = self.half * self.half_rows + self.seat * self.piece
        terms = [(block, mine)]
        for step in range(1, self.group):
            links.receive(self.label("z", step), ("sp", 2 * step), self.far_in.at[step - 1])
            terms.append((self.far_in.at[step - 1], 0))
        add_rows(self.result, mine, self.piece, terms)
        done = self.rows_of(self.result, self.half, self.seat)
        for step in range(1, self.group):
            links.send(self.label("a", step), ("sp", 2 * step), done, done)

    def far_done(self):
        links = self.links
        for step in range(1, self.group):
            links.receive(
                self.label("a", step), ("sp", 2 * step),
                self.rows_of(self.result, self.half, self.seat ^ step),
            )
        done = self.rows_of(self.result, self.half)
        links.send(self.label("b"), BESIDE, done, done)

    def beside_done(self):
        self.links.receive(
            self.label("b"), BESIDE, self.rows_of(self.result, 1 - self.half)
        )


class Total:
    def __init__(self, links, name, stages, inboxes, far_in, result, group):
        self.links, self.name, self.stages, self.inboxes = links, name, stages, inboxes
        self.far_in, self.result, self.group = far_in, result, group
        self.piece = result.shape[0] // group
        self.seat = links.sp >> 1
        self.ways = (CORE, ACROSS, BESIDE)
        self.steps = [
            functools.partial(self.exchange, 0), functools.partial(self.add, 0),
            functools.partial(self.add, 1), functools.partial(self.add, 2), self.far_add,
            self.far_done,
        ]

    def run(self):
        self.steps.pop(0)()

    def label(self, *step):
        return (self.name,) + step

    def at(self, ref, piece):
        return ref.at[pl.ds(pl.multiple_of(piece * self.piece, 8), self.piece), :]

    def exchange(self, stage):
        self.links.send(
            self.label("e", stage), self.ways[stage], self.stages.at[stage],
            self.inboxes.at[stage],
        )

    def add(self, stage):
        self.links.receive(self.label("e", stage), self.ways[stage], self.inboxes.at[stage])
        self.stages[stage + 1] = self.stages[stage] + self.inboxes[stage]
        if stage < 2:
            self.exchange(stage + 1)
            return
        for step in range(1, self.group):
            self.links.send(
                self.label("z", step), ("sp", 2 * step),
                self.at(self.stages.at[3], self.seat ^ step), self.far_in.at[step - 1],
            )

    def far_add(self):
        total = self.at(self.stages.at[3], self.seat)[...]
        for step in range(1, self.group):
            self.links.receive(self.label("z", step), ("sp", 2 * step), self.far_in.at[step - 1])
            total = total + self.far_in[step - 1]
        done = self.at(self.result, self.seat)
        done[...] = total
        for step in range(1, self.group):
            self.links.send(self.label("a", step), ("sp", 2 * step), done, done)

    def far_done(self):
        for step in range(1, self.group):
            self.links.receive(
                self.label("a", step), ("sp", 2 * step), self.at(self.result, self.seat ^ step)
            )


GRADS = ("gd", "gu", "gp", "gqkv", "gm")
WEIGHTS = ("wm", "wqkv", "wp", "wu", "wd")
INPUTS = ("valid", "edge", "x", "grad_out", "gains", "pack") + tuple("own_" + n for n in WEIGHTS)
OUTPUTS = ("out", "d_in", "o_gm", "o_gqkv", "o_gp", "o_gu", "o_gd", "o_sums")


def whole_kernel(names, group, plan, *refs):
    refs = dict(zip(names, refs, strict=True))
    links = Links(refs.pop("send_sems"), refs.pop("recv_sems"), plan)
    links.greet([CORE, ACROSS, BESIDE] + far_ways(2 * group))

    own = {name: refs.pop("own_" + name) for name in WEIGHTS}
    views = dict(
        wm=column_view(own["wm"].shape[1], True),
        wqkv=column_view(own["wqkv"].shape[2], True),
        wp=row_view(own["wp"].shape[0]),
        wu=column_view(own["wu"].shape[1], True),
        wd=row_view(own["wd"].shape[0]),
    )
    gathers = {
        name: Gather(links, name, own[name], refs[name], views[name], name != "wm")
        for name in WEIGHTS
    }
    gathers["pack"] = Gather(links, "pack", refs.pop("pack"), refs["packs"], lead_view, False)
    for name in ("wm", "pack", "wqkv", "wp", "wu", "wd"):
        gathers[name].start()

    packs = refs.pop("packs")
    results = {name: refs.pop("r_" + name) for name in GRADS}
    outs = {name: refs.pop("o_" + name) for name in GRADS}
    reduces = {
        name: Reduce(
            links, name, refs[name], refs.pop("c_" + name), refs.pop("x_" + name),
            refs.pop("y_" + name), refs.pop("z_" + name), results[name], group,
        )
        for name in GRADS
    }
    stages, inboxes = refs.pop("sum_stages"), refs.pop("sum_inboxes")
    refs["sums"] = stages.at[0]
    total = Total(links, "sums", stages, inboxes, refs.pop("sum_far"), refs.pop("o_sums"), group)

    shards = packs.shape[0]

    def table():
        rows = refs["rel_rows"]
        return jnp.concatenate(
            [packs[shard, 0:rows, : 2 * LANES] for shard in range(shards)], axis=0
        )

    def qkv_bias(part):
        row = 4 if part == 0 else 5
        return jnp.concatenate(
            [packs[shard, row : row + 1, :LANES] for shard in range(shards)], axis=1
        )

    def up_bias(index):
        return packs[index, 6:7, :]

    refs.update(table=table, qkv_bias=qkv_bias, up_bias=up_bias, rel_rows=4)
    local = Local(refs, links.tp * (refs["x"].shape[0] // TOK))

    def output(name):
        fin, out = results[name], outs[name]
        if name == "gm":
            out[...] = fin[...].astype(F32)
        elif name == "gqkv":
            rows = out.shape[1]
            for part in range(3):
                out[part] = fin[part * rows : (part + 1) * rows, :].astype(F32)
        else:
            rows = out.shape[0]
            for block in range(out.shape[1] // LANES):
                lanes = slice(block * LANES, (block + 1) * LANES)
                out[:, lanes] = fin[block * rows : (block + 1) * rows, :].astype(F32)

    stages[0] = jnp.zeros_like(stages[0])
    local.prepare()
    local.merge_norm()
    gathers["wm"].forward()
    gathers["pack"].forward()
    gathers["wm"].finish()
    gathers["pack"].finish()
    local.merge()
    gathers["wqkv"].forward()
    gathers["wp"].forward()
    local.attn_norm()
    local.table_bias()
    gathers["wqkv"].forward_beside()
    gathers["wp"].forward_beside()
    gathers["wqkv"].finish()
    local.project()
    windows = local.windows
    quarter = windows // 4
    local.attend(0, quarter)
    gathers["wu"].forward()
    gathers["wp"].finish()
    local.attend(quarter, 2 * quarter)
    gathers["wu"].forward_beside()
    gathers["wd"].forward()
    local.attend(2 * quarter, 3 * quarter)
    gathers["wd"].forward_beside()
    local.attend(3 * quarter, windows)
    local.attn_out()
    local.mlp_norm()
    gathers["wu"].finish()
    local.up()
    gathers["wd"].finish()
    local.down()
    local.finish()

    each(refs["gd"].shape[0], local.down_back)
    reduces["gd"].run()
    reduces["gu"].run()
    local.up_back()
    reduces["gd"].run()
    reduces["gu"].run()
    local.mlp_back()
    local.proj_back()
    reduces["gp"].run()
    local.attend_back(3 * quarter, windows)
    reduces["gp"].run()
    reduces["gd"].run()
    local.attend_back(2 * quarter, 3 * quarter)
    reduces["gd"].run()
    reduces["gu"].run()
    local.attend_back(quarter, 2 * quarter)
    reduces["gd"].run()
    reduces["gu"].run()
    reduces["gp"].run()
    local.attend_back(0, quarter)
    reduces["gd"].run()
    reduces["gu"].run()
    reduces["gp"].run()
    local.bias_back()
    local.qkv_back()
    reduces["gqkv"].run()
    reduces["gd"].run()
    reduces["gu"].run()
    reduces["gp"].run()
    local.attn_back()
    reduces["gqkv"].run()
    reduces["gp"].run()
    output("gd")
    local.merge_weight_back()
    reduces["gm"].run()
    reduces["gu"].run()
    local.merge_in_back()
    reduces["gm"].run()
    reduces["gp"].run()
    local.merge_back()
    total.run()
    total.run()
    reduces["gqkv"].run()
    reduces["gm"].run()
    total.run()
    reduces["gqkv"].run()
    reduces["gm"].run()
    total.run()
    output("gu")
    output("gp")
    reduces["gqkv"].run()
    reduces["gm"].run()
    total.run()
    reduces["gqkv"].run()
    reduces["gm"].run()
    total.run()
    reduces["gqkv"].run()
    reduces["gm"].run()
    output("gqkv")
    output("gm")
    links.drain()


def whole_call(group, inputs):
    rows, wide = inputs["x"].shape
    shards = 4
    width = inputs["own_wu"].shape[0]
    units = shards * inputs["own_wu"].shape[1]
    depth = dict(gd=units, gu=units, gp=width, gqkv=3 * width, gm=wide)
    scratch = local_scratch(rows, wide, width, units)
    scratch.update(
        wm=pltpu.VMEM((wide, width), BF16),
        wqkv=pltpu.VMEM((3, width, width), BF16),
        wp=pltpu.VMEM((width, width), BF16),
        wu=pltpu.VMEM((width, units), BF16),
        wd=pltpu.VMEM((units, width), BF16),
        packs=pltpu.VMEM((shards,) + inputs["pack"].shape, F32),
    )
    for name in GRADS:
        size = depth[name]
        scratch[name] = pltpu.VMEM((shards, size, LANES), BF16)
        scratch["c_" + name] = pltpu.VMEM((2, size, LANES), BF16)
        scratch["x_" + name] = pltpu.VMEM((size, LANES), BF16)
        scratch["y_" + name] = pltpu.VMEM((size // 2, LANES), BF16)
        scratch["z_" + name] = pltpu.VMEM((group - 1, size // 2 // group, LANES), BF16)
        scratch["r_" + name] = pltpu.VMEM((size, LANES), BF16)
    scratch["sum_stages"] = pltpu.VMEM((4, SUM_SIZE, LANES), F32)
    scratch["sum_inboxes"] = pltpu.VMEM((3, SUM_SIZE, LANES), F32)
    scratch["sum_far"] = pltpu.VMEM((group - 1, SUM_SIZE // group, LANES), F32)
    count = 6 * 6 + len(GRADS) * (5 + 2 * group) + 4 + 2 * group
    scratch["send_sems"] = pltpu.SemaphoreType.DMA((count,))
    scratch["recv_sems"] = pltpu.SemaphoreType.DMA((count,))
    outs = dict(
        out=jax.ShapeDtypeStruct((rows, width), BF16),
        d_in=jax.ShapeDtypeStruct((rows, wide), F32),
        o_gm=jax.ShapeDtypeStruct(inputs["own_wm"].shape, F32),
        o_gqkv=jax.ShapeDtypeStruct(inputs["own_wqkv"].shape, F32),
        o_gp=jax.ShapeDtypeStruct(inputs["own_wp"].shape, F32),
        o_gu=jax.ShapeDtypeStruct(inputs["own_wu"].shape, F32),
        o_gd=jax.ShapeDtypeStruct(inputs["own_wd"].shape, F32),
        o_sums=jax.ShapeDtypeStruct((SUM_SIZE, LANES), F32),
    )
    names = INPUTS + OUTPUTS + tuple(scratch)
    vmem = pl.BlockSpec(memory_space=pltpu.VMEM)
    smem = pl.BlockSpec(memory_space=pltpu.SMEM)
    hbm = pl.BlockSpec(memory_space=pl.ANY)
    return pl.pallas_call(
        functools.partial(whole_kernel, names, group, {}),
        out_shape=[outs[name] for name in OUTPUTS],
        in_specs=[smem, smem, vmem, vmem, vmem, hbm] + [hbm] * len(WEIGHTS),
        out_specs=[vmem] * len(OUTPUTS),
        scratch_shapes=list(scratch.values()),
        compiler_params=pltpu.CompilerParams(
            vmem_limit_bytes=63 * MIB, collective_id=0, has_side_effects=True
        ),
    )(*[inputs[name] for name in INPUTS])


def pad_to(values, rows, lanes):
    return jnp.pad(values, ((0, rows - values.shape[0]), (0, lanes - values.shape[1])))


def on_device(
    inputs, grad_out, window_valid, window_edge, merge_gain, merge_bias, merge_weight, attn_gain,
    attn_bias, query_key_value_weight, qv_bias, rel_table, proj_weight, proj_bias, mlp_gain,
    mlp_bias, up_weight, up_bias, down_weight, down_bias,
):
    tp_index = lax.axis_index("tp")
    wide, width, tile = merge_gain.shape[0], down_bias.shape[0], up_bias.shape[0]
    gains = jnp.concatenate(
        [
            pad_to(vector.astype(F32)[None], 1, wide)
            for vector in (
                merge_gain, merge_bias, attn_gain, attn_bias, mlp_gain, mlp_bias, proj_bias,
                down_bias,
            )
        ],
        axis=0,
    )
    pack = jnp.concatenate(
        [
            pad_to(rel_table.T.astype(F32), 4, tile),
            pad_to(qv_bias.astype(F32), 2, tile),
            pad_to(up_bias.astype(F32)[None], 2, tile),
        ],
        axis=0,
    )
    out, d_in, gm, gqkv, gp, gu, gd, sums = whole_call(
        lax.axis_size("sp") // 2,
        dict(
            valid=window_valid, edge=window_edge, x=inputs, grad_out=grad_out, gains=gains,
            pack=pack, own_wm=merge_weight,
            own_wqkv=jnp.transpose(query_key_value_weight, (1, 0, 2)), own_wp=proj_weight,
            own_wu=up_weight, own_wd=down_weight,
        ),
    )

    def vector(row, size):
        return lax.slice_in_dim(sums, SUM_ROWS[row], SUM_ROWS[row] + size // LANES).reshape(-1)

    def mine(whole, size):
        return lax.dynamic_slice_in_dim(whole, tp_index * size, size, 0)

    heads = width // HD
    table = jnp.concatenate(
        [sums[SUM_ROWS[11] + half * heads :][:heads] for half in range(2)], axis=1
    )[:, :REL]
    qv = jnp.stack([mine(vector(row, width), qv_bias.shape[1]) for row in (8, 9)])
    return (
        out,
        d_in,
        vector(0, wide),
        vector(1, wide),
        gm,
        vector(2, width),
        vector(3, width),
        jnp.transpose(gqkv, (1, 0, 2)),
        qv,
        mine(table, rel_table.shape[1]).T,
        gp,
        vector(4, width),
        vector(5, width),
        vector(6, width),
        gu,
        mine(vector(10, 4 * tile), tile),
        gd,
        vector(7, width),
    )


def solution(mesh):
    placed = (
        P(("sp", "tp"), None),
        P(("sp", "tp"), None),
        P("sp"),
        P("sp"),
        P(),
        P(),
        P(None, "tp"),
        P(),
        P(),
        P(None, None, "tp"),
        P(None, "tp"),
        P(None, "tp"),
        P("tp", None),
        P(),
        P(),
        P(),
        P(None, "tp"),
        P("tp"),
        P("tp", None),
        P(),
    )
    return jax.shard_map(
        on_device,
        mesh=mesh,
        in_specs=placed,
        out_specs=(
            P(("sp", "tp"), None),
            P(("sp", "tp"), None),
            P(),
            P(),
            P(None, "tp"),
            P(),
            P(),
            P(None, None, "tp"),
            P(None, "tp"),
            P(None, "tp"),
            P("tp", None),
            P(),
            P(),
            P(),
            P(None, "tp"),
            P("tp"),
            P("tp", None),
            P(),
        ),
        check_vma=False,
    )
```

time: 476 us -> 205 us (0.43)
  Pallas kernels: 0 us -> 178 us
  waiting for transfers between devices: 160 us -> 0 us
  matrix products: 94.9 us -> 0 us
  local copies, waits for them, and re-layouts: 93.4 us -> 21 us
  blocking collectives: 70.2 us -> 0 us
  other arithmetic: 35.7 us -> 3.1 us
  between operations: 15.3 us -> 0.69 us
    pallas_call x0 -> x1, Pallas kernels: none -> 178 us  [whole_call(): pl.pallas_call(functools.partial(whole_kernel, names, group, {}), out_sha...]
    dot_general x23 -> x0, matrix products: 94.9 us -> none  [the longest x1 19.4 us: on_device(): jnp.dot(mlp_in, up_all, preferred_element_type=jnp.float32)]
    reduce_scatter x3 -> x0, waiting for transfers between devices: 88.5 us -> none  [the longest x2 54.5 us: on_device(): lax.psum_scatter(grad.astype(jnp.bfloat16), 'tp', scatter_dimension=0, ti...]
    psum x1 -> x0, waiting for transfers between devices: 49.1 us -> none  [on_device(): lax.psum(lax.psum_scatter(grad.astype(jnp.bfloat16), 'tp', scatter_dimens...]
    psum x1 -> x0, blocking collectives: 43.2 us -> none  [on_device(): lax.psum((d_merge_gain, d_merge_bias, d_attn_gain, d_attn_bias, d_proj_bi...]
    convert_element_type x10 -> x0, local copies, waits for them, and re-layouts: 35.8 us -> none  [the longest x2 8.34 us: attend_backward(): d_values.reshape(flat_shape).astype(jnp.bfloat16)]
    all_gather x4 -> x0, blocking collectives: 27 us -> none  [the longest x2 15.7 us: on_device(): gather_first = lambda block: lax.all_gather(block, 'tp', axis=0, tiled=True)]
    unnamed x12 -> x0, waiting for transfers between devices: 22.1 us -> none
  transfers between devices with their start and end apart: 10 -> 0, of which waited for: 5 -> 0; matrix products, arithmetic and copies ran while one was open for 28% -> 0% of each run, Pallas kernels for 0% -> 0%
where the time goes in v2:
time: 205 us; the launch traced here: 203 us
  Pallas kernels  178 us (87%)
  local copies, waits for them, and re-layouts  21 us (10%)
  other arithmetic  3.1 us (2%)
    pallas_call x1, Pallas kernels, whole_call(): pl.pallas_call(functools.partial(whole_kernel, names, group, {}), out_sha...  178 us
    unnamed x17, local copies, waits for them, and re-layouts  10.6 us
    broadcast_in_dim x8, local copies, waits for them, and re-layouts, on_device(): vector.astype(F32)[None]  5.48 us

profile of v2, /device:TPU:0, one launch (start us, length us, event | category | flops | bytes accessed | tf_op | source)
XLA Modules:
  0.0 203.2 jit_solution(2483646563263253502)
XLA Ops:
  0.7 0.7 broadcast_in_dim.38
  1.4 0.7 broadcast_in_dim.39
  2.0 0.7 broadcast_in_dim.42
  2.7 0.7 broadcast_in_dim.40
  3.4 0.7 broadcast_in_dim.41
  4.1 0.7 broadcast_in_dim.44
  4.8 0.7 broadcast_in_dim.43
  5.5 0.7 broadcast_in_dim.36
  6.2 0.7 broadcast_in_dim.37
  6.9 1.3 fusion.6.refs_5_
  8.3 0.6 concatenate.14.refs_4_
  8.9 178.5 %shard_map.331 = (bf16[784,512]{1,0:T(8,128)(2,1)}, f32[784,1024]{1,0:T(8,128)}, f32[1024,128]{1,0:T(8,128)}, f32[3,512,128]{2,1,0:T(8,128)}, f32[128,512]{1,0:T...) custom-call(s32[64]{0:T(128)} %refs_0_.1, s32[64]{0:T(128)} %refs_1_.1, ...), custom_call_target="tpu_custom_call" | custom-call | tf_op jit(solution)/shard_map/pallas_call | solution.py:1082
  187.4 1.3 slice_bitcast_fusion.1
  188.7 1.4 slice_bitcast_fusion.3
  190.0 0.7 slice_bitcast_fusion
  190.8 0.7 dynamic_slice.15
  192.1 0.6 fusion.8
  192.7 2.1 %copy.45 = bf16[784,512]{1,0:T(8,128)(2,1)} copy(bf16[784,512]{1,0:T(8,128)(2,1)} %get-tuple-element.67) | data formatting | bytes 1605632
  194.7 4.2 %copy.46 = f32[784,1024]{1,0:T(8,128)} copy(f32[784,1024]{1,0:T(8,128)} %get-tuple-element.68) | data formatting | bytes 6422528
  198.9 0.8 copy.47
  199.7 0.9 copy.48
  200.6 0.7 copy.49
  201.3 1.0 copy.50
  202.3 1.0 copy.51
  (19 shorter events, 0.8 us)
Async XLA Ops:
  194.7 4.2 %copy-start.3 = (f32[1024,128]{1,0:T(8,128)S(1)}, f32[1024,128]{1,0:T(8,128)}, u32[]{:S(2)}) copy-start(f32[1024,128]{1,0:T(8,128)} %get-tuple-element.71) | copy-start | bytes 1572868
  194.7 5.0 %copy-start.2 = (f32[3,512,128]{2,1,0:T(8,128)S(1)}, f32[3,512,128]{2,1,0:T(8,128)}, u32[]{:S(2)}) copy-start(f32[3,512,128]{2,1,0:T(8,128)} %get-tuple-element.30) | copy-start | bytes 2359300
  194.7 5.9 %copy-start.4 = (f32[128,512]{1,0:T(8,128)S(1)}, f32[128,512]{1,0:T(8,128)}, u32[]{:S(2)}) copy-start(f32[128,512]{1,0:T(8,128)} %get-tuple-element.77) | copy-start | bytes 786436
  194.7 6.6 %copy-start.1 = (f32[512,512]{1,0:T(8,128)S(1)}, f32[512,512]{1,0:T(8,128)}, u32[]{:S(2)}) copy-start(f32[512,512]{1,0:T(8,128)} %get-tuple-element.81) | copy-start | bytes 3145732
  198.9 3.4 %copy-start = (f32[512,512]{1,0:T(8,128)S(1)}, f32[512,512]{1,0:T(8,128)}, u32[]{:S(2)}) copy-start(f32[512,512]{1,0:T(8,128)} %get-tuple-element.83) | copy-start | bytes 3145732

commit v3 on v2

--- a/solution.py
+++ b/solution.py
@@ -278,6 +278,13 @@
         self.stats[at, index : index + 1] = mean
         self.stats[at, index + 1 : index + 2] = inv
 
+    def spread_vectors(self):
+        for row, ref in enumerate(self.vectors):
+            values = ref[...].astype(F32)
+            for block in range(values.shape[0]):
+                lanes = slice(block * LANES, (block + 1) * LANES)
+                self.gains[row : row + 1, lanes] = values[block : block + 1]
+
     def prepare(self):
         def keep_rows(window):
             base = pl.ds(pl.multiple_of(window * (TOK - 1), 16), SPAN)
@@ -316,12 +323,11 @@
 
         each(self.steps, step, 7)
 
-    def project(self):
-        for part in range(3):
-            product = dot(self.attn_in[...], self.wqkv[part])
-            if part != 1:
-                product = product + self.qkv_bias(part)
-            self.qkv[part] = product.astype(BF16)
+    def project(self, part):
+        product = dot(self.attn_in[...], self.wqkv[part])
+        if part != 1:
+            product = product + self.qkv_bias(part)
+        self.qkv[part] = product.astype(BF16)
 
     def attend(self, first, last):
         def step(index):
@@ -368,15 +374,10 @@
     def down(self):
         self.pre[...] = dot(self.hidden[...], self.wd[...])
 
-    def finish(self):
-        down_bias = self.gain(7, self.width)
-
+    def grad_rows(self):
         def step(index, total):
             at = rows_at(index, self.chunk)
-            mask = self.stat(at, 6)
-            block = (self.resid[at, :] + self.pre[at, :] + down_bias) * mask
-            self.out[at, :] = block.astype(BF16)
-            grad = self.grad_out[at, :].astype(F32) * mask
+            grad = self.grad_out[at, :].astype(F32) * self.stat(at, 6)
             self.d_mlp[at, :] = grad.astype(BF16)
             return total + fold(grad)
 
@@ -385,23 +386,45 @@
         )
         self.put_sum(7, total)
 
-    def down_back(self, index):
-        columns = rows_at(index, self.tile)
-        self.pre[...] = dot_cols(self.d_mlp[...], self.wd[columns, :])
-        put_blocks(self.gd, index, dot_rows(self.hidden[:, columns], self.d_mlp[...]))
-
-        def activate(step, total):
-            at = rows_at(step, self.chunk)
-            grad = (self.pre[at, :] * self.slope[at, columns].astype(F32)).astype(BF16)
-            self.hidden[at, columns] = grad
-            return total + fold(grad.astype(F32))
-
-        total = lax.fori_loop(0, self.steps, activate, jnp.zeros((8, self.tile), F32), unroll=7)
-        self.put_up_sum(index, total)
-        put_blocks(self.gu, index, dot_rows(self.mlp_in[...], self.hidden[:, columns]))
+    def finish(self):
+        down_bias = self.gain(7, self.width)
+
+        def step(index):
+            at = rows_at(index, self.chunk)
+            block = (self.resid[at, :] + self.pre[at, :] + down_bias) * self.stat(at, 6)
+            self.out[at, :] = block.astype(BF16)
+
+        each(self.steps, step, 7)
+
+    def down_weight_back(self):
+        def part(index):
+            columns = rows_at(index, self.tile)
+            put_blocks(self.gd, index, dot_rows(self.hidden[:, columns], self.d_mlp[...]))
+
+        each(self.units // self.tile, part)
+
+    def hidden_back(self, first, last):
+        def part(step):
+            index = first + step
+            columns = rows_at(index, self.tile)
+            self.pre[...] = dot_cols(self.d_mlp[...], self.wd[columns, :])
+
+            def activate(step, total):
+                at = rows_at(step, self.chunk)
+                grad = (self.pre[at, :] * self.slope[at, columns].astype(F32)).astype(BF16)
+                self.d_pre[at, columns] = grad
+                return total + fold(grad.astype(F32))
+
+            total = lax.fori_loop(
+                0, self.steps, activate, jnp.zeros((8, self.tile), F32), unroll=7
+            )
+            self.put_up_sum(index, total)
+            put_blocks(self.gu, index, dot_rows(self.mlp_in[...], self.d_pre[:, columns]))
+
+        each(last - first, part)
 
     def up_back(self):
-        self.pre[...] = dot_cols(self.hidden[...], self.wu[...])
+        self.pre[...] = dot_cols(self.d_pre[...], self.wu[...])
 
     def mlp_back(self):
         gain = self.gain(4, self.width)
@@ -412,7 +435,7 @@
             normed = (self.resid[at, :] - self.stat(at, 4)) * inv
             upstream = self.pre[at, :]
             d_resid = self.d_mlp[at, :].astype(F32) + norm_back(upstream, normed, inv, gain)
-            self.resid[at, :] = d_resid
+            self.d_resid[at, :] = d_resid
             self.d_mlp[at, :] = d_resid.astype(BF16)
             return (
                 totals[0] + fold(upstream * normed),
@@ -448,9 +471,11 @@
         self.put_sum(8, dot(ones, self.qkv[0]), True)
         self.put_sum(9, dot(ones, self.qkv[2]), True)
 
-    def qkv_back(self):
+    def qkv_weight_back(self):
         for part in range(3):
             put_columns(self.gqkv, part, dot_rows(self.attn_in[...], self.qkv[part]))
+
+    def qkv_back(self):
         self.pre[...] = (
             dot_cols(self.qkv[0], self.wqkv[0])
             + dot_cols(self.qkv[1], self.wqkv[1])
@@ -465,7 +490,7 @@
             inv = self.stat(at, 3)
             normed = (self.section[at, :].astype(F32) - self.stat(at, 2)) * inv
             upstream = self.pre[at, :]
-            d_section = self.resid[at, :] + norm_back(upstream, normed, inv, gain)
+            d_section = self.d_resid[at, :] + norm_back(upstream, normed, inv, gain)
             self.d_mlp[at, :] = d_section.astype(BF16)
             return totals[0] + fold(upstream * normed), totals[1] + fold(upstream)
 
@@ -480,11 +505,11 @@
     def merge_in_back(self):
         self.d_in[...] = dot_cols(self.d_mlp[...], self.wm[...])
 
-    def merge_back(self):
+    def merge_back(self, first, last, totals=None):
         gain = self.gain(0, self.wide)
 
         def step(index, totals):
-            at = rows_at(index, self.chunk)
+            at = rows_at(first + index, self.chunk)
             inv = self.stat(at, 1)
             normed = (self.x[at, :].astype(F32) - self.stat(at, 0)) * inv
             upstream = self.d_in[at, :]
@@ -492,9 +517,11 @@
             return totals[0] + fold(upstream * normed), totals[1] + fold(upstream)
 
         blank = jnp.zeros((8, self.wide), F32)
-        totals = lax.fori_loop(0, self.steps, step, (blank, blank), unroll=7)
-        self.put_sum(0, totals[0])
-        self.put_sum(1, totals[1])
+        totals = lax.fori_loop(0, last - first, step, totals or (blank, blank), unroll=7)
+        if last == self.steps:
+            self.put_sum(0, totals[0])
+            self.put_sum(1, totals[1])
+        return totals
 
     def put_sum(self, row, values, summed=False):
         values = values[0:1] if summed else sum_rows(values)
@@ -549,6 +576,9 @@
         slope=pltpu.VMEM((rows, units), BF16),
         pre=pltpu.VMEM((rows, width), F32),
         d_mlp=pltpu.VMEM((rows, width), BF16),
+        d_pre=pltpu.VMEM((rows, units), BF16),
+        d_resid=pltpu.VMEM((rows, width), F32),
+        gains=pltpu.VMEM((8, wide), F32),
         stats=pltpu.VMEM((rows, 8), F32),
         bias=pltpu.VMEM((SPAN, heads * SPAN), F32),
         d_bias=pltpu.VMEM((SPAN, heads * SPAN), F32),
@@ -712,25 +742,34 @@
 
 
 class Reduce:
-    def __init__(self, links, name, grads, core_in, across_in, beside_in, far_in, result, group):
+    def __init__(self, links, name, grads, core_in, first_in, second_in, far_in, result, group,
+                 across_first):
         self.links, self.name, self.grads = links, name, grads
-        self.core_in, self.across_in, self.beside_in = core_in, across_in, beside_in
+        self.core_in, self.first_in, self.second_in = core_in, first_in, second_in
         self.far_in, self.result, self.group = far_in, result, group
         self.rows = grads.shape[1]
         self.half_rows = self.rows // 2
         self.piece = self.half_rows // group
         self.half = links.sp & 1
         self.seat = links.sp >> 1
-        self.steps = [
-            self.core_send, self.core_add, self.across_add, self.beside_add, self.far_add,
-            self.far_done, self.beside_done,
-        ]
+        self.across = links.tp >> 1
+        if across_first:
+            middle = [self.core_add_across, self.across_beside, self.beside_last]
+        else:
+            middle = [self.core_add_beside, self.beside_across, self.across_last]
+        self.steps = [self.core_send] + middle + [self.far_add, self.far_done, self.beside_done]
 
     def run(self):
         self.steps.pop(0)()
 
     def label(self, *step):
         return (self.name,) + step
+
+    def rows_of(self, ref, half, piece=None):
+        if piece is None:
+            return ref.at[pl.ds(pl.multiple_of(half * self.half_rows, 16), self.half_rows), :]
+        start = half * self.half_rows + piece * self.piece
+        return ref.at[pl.ds(pl.multiple_of(start, 16), self.piece), :]
 
     def core_send(self):
         links = self.links
@@ -740,39 +779,62 @@
                 self.core_in.at[across],
             )
 
-    def core_add(self):
+    def core_receive(self):
+        for across in range(2):
+            self.links.receive(self.label("c", across), CORE, self.core_in.at[across])
+
+    def core_add_across(self):
+        self.core_receive()
+        other = self.links.tp ^ 2
+        block = self.grads.at[other]
+        add_rows(block, 0, self.rows, [(block, 0), (self.core_in.at[self.across ^ 1], 0)])
+        self.links.send(self.label("x"), ACROSS, block, self.first_in)
+
+    def across_beside(self):
+        links = self.links
+        links.receive(self.label("x"), ACROSS, self.first_in)
+        block = self.grads.at[links.tp]
+        terms = [(block, 0), (self.core_in.at[self.across], 0), (self.first_in, 0)]
+        add_rows(block, 0, self.rows, terms)
+        links.send(
+            self.label("y"), BESIDE, self.rows_of(block, 1 - self.half), self.second_in
+        )
+
+    def beside_last(self):
+        self.links.receive(self.label("y"), BESIDE, self.second_in)
+        self.add_and_spread([(self.second_in, 0)])
+
+    def core_add_beside(self):
+        links = self.links
+        self.core_receive()
+        for across in range(2):
+            block = self.grads.at[(links.tp & 1) | 2 * across]
+            add_rows(block, 0, self.rows, [(block, 0), (self.core_in.at[across], 0)])
+            links.send(
+                self.label("y", across), BESIDE, self.rows_of(block, 1 - self.half),
+                self.first_in.at[across],
+            )
+
+    def beside_across(self):
         links = self.links
         for across in range(2):
-            links.receive(self.label("c", across), CORE, self.core_in.at[across])
-        other = links.tp ^ 2
-        block = self.grads.at[other]
-        add_rows(block, 0, self.rows, [(block, 0), (self.core_in.at[other >> 1], 0)])
-        links.send(self.label("x"), ACROSS, block, self.across_in)
-
-    def across_add(self):
-        links = self.links
-        links.receive(self.label("x"), ACROSS, self.across_in)
-        block = self.grads.at[links.tp]
-        terms = [(block, 0), (self.core_in.at[links.tp >> 1], 0), (self.across_in, 0)]
-        add_rows(block, 0, self.rows, terms)
-        links.send(
-            self.label("y"), BESIDE, self.rows_of(block, 1 - self.half), self.beside_in
-        )
-
-    def rows_of(self, ref, half, piece=None):
-        if piece is None:
-            return ref.at[pl.ds(pl.multiple_of(half * self.half_rows, 16), self.half_rows), :]
-        start = half * self.half_rows + piece * self.piece
-        return ref.at[pl.ds(pl.multiple_of(start, 16), self.piece), :]
-
-    def beside_add(self):
-        links = self.links
-        links.receive(self.label("y"), BESIDE, self.beside_in)
-        block = self.grads.at[links.tp]
+            links.receive(self.label("y", across), BESIDE, self.first_in.at[across])
+        block = self.grads.at[links.tp ^ 2]
         mine = self.half * self.half_rows
-        add_rows(block, mine, self.half_rows, [(block, mine), (self.beside_in, 0)])
+        terms = [(block, mine), (self.first_in.at[self.across ^ 1], 0)]
+        add_rows(block, mine, self.half_rows, terms)
+        links.send(self.label("x"), ACROSS, self.rows_of(block, self.half), self.second_in)
+
+    def across_last(self):
+        self.links.receive(self.label("x"), ACROSS, self.second_in)
+        self.add_and_spread([(self.first_in.at[self.across], 0), (self.second_in, 0)])
+
+    def add_and_spread(self, terms):
+        block = self.grads.at[self.links.tp]
+        mine = self.half * self.half_rows
+        add_rows(block, mine, self.half_rows, [(block, mine)] + terms)
         for step in range(1, self.group):
-            links.send(
+            self.links.send(
                 self.label("z", step), ("sp", 2 * step),
                 self.rows_of(block, self.half, self.seat ^ step), self.far_in.at[step - 1],
             )
@@ -863,53 +925,79 @@
             )
 
 
+UNITS = (
+    ("gd", 0, 1024, True), ("gd", 1024, 1024, True),
+    ("gu", 0, 1024, True), ("gu", 1024, 1024, True),
+    ("gp", 0, 512, True),
+    ("gqkv", 0, 1024, True), ("gqkv", 1024, 512, False),
+    ("gm", 0, 512, True), ("gm", 512, 512, False),
+)
 GRADS = ("gd", "gu", "gp", "gqkv", "gm")
 WEIGHTS = ("wm", "wqkv", "wp", "wu", "wd")
-INPUTS = ("valid", "edge", "x", "grad_out", "gains", "pack") + tuple("own_" + n for n in WEIGHTS)
-OUTPUTS = ("out", "d_in", "o_gm", "o_gqkv", "o_gp", "o_gu", "o_gd", "o_sums")
+VECTORS = (
+    "merge_gain", "merge_bias", "attn_gain", "attn_bias", "mlp_gain", "mlp_bias", "proj_bias",
+    "down_bias",
+)
+INPUTS = (
+    ("valid", "edge", "x", "grad_out", "rel", "qv", "ub") + VECTORS
+    + tuple("own_" + name for name in WEIGHTS)
+)
+OUTPUTS = ("h_out", "h_d_in") + tuple("r_" + name for name in GRADS) + ("r_sums",)
+
+
+def unit_name(name, first):
+    return name + str(first)
 
 
 def whole_kernel(names, group, plan, *refs):
     refs = dict(zip(names, refs, strict=True))
     links = Links(refs.pop("send_sems"), refs.pop("recv_sems"), plan)
+    own_pack, packs = refs.pop("pack"), refs.pop("packs")
+    rel, qv, ub = refs.pop("rel"), refs.pop("qv"), refs.pop("ub")
+    heads_here = rel.shape[0]
+    own_pack[...] = jnp.zeros_like(own_pack)
+    own_pack[0:heads_here, 0:REL] = rel[...].astype(F32)
+    own_pack[4:6, 0:LANES] = qv[...].astype(F32)
+    for block in range(ub.shape[0]):
+        lanes = slice(block * LANES, (block + 1) * LANES)
+        own_pack[6:7, lanes] = ub[block : block + 1, :].astype(F32)
+
+    own = {name: refs.pop("own_" + name) for name in WEIGHTS}
+    whole = {name: refs[name] for name in WEIGHTS}
+    for part, name in enumerate(("wq", "wk", "wv")):
+        own[name], whole[name] = own["wqkv"].at[part], whole["wqkv"].at[part]
+    columns = column_view(LANES, True)
+    views = dict(
+        wm=columns, wq=columns, wk=columns, wv=columns, wp=row_view(own["wp"].shape[0]),
+        wu=column_view(own["wu"].shape[1], True), wd=row_view(own["wd"].shape[0]),
+    )
+    gathers = {"pack": Gather(links, "pack", own_pack, packs, lead_view, False)}
+    for name in ("wm", "wq", "wk", "wv", "wp", "wu", "wd"):
+        gathers[name] = Gather(links, name, own[name], whole[name], views[name], name != "wm")
     links.greet([CORE, ACROSS, BESIDE] + far_ways(2 * group))
-
-    own = {name: refs.pop("own_" + name) for name in WEIGHTS}
-    views = dict(
-        wm=column_view(own["wm"].shape[1], True),
-        wqkv=column_view(own["wqkv"].shape[2], True),
-        wp=row_view(own["wp"].shape[0]),
-        wu=column_view(own["wu"].shape[1], True),
-        wd=row_view(own["wd"].shape[0]),
-    )
-    gathers = {
-        name: Gather(links, name, own[name], refs[name], views[name], name != "wm")
-        for name in WEIGHTS
-    }
-    gathers["pack"] = Gather(links, "pack", refs.pop("pack"), refs["packs"], lead_view, False)
-    for name in ("wm", "pack", "wqkv", "wp", "wu", "wd"):
-        gathers[name].start()
-
-    packs = refs.pop("packs")
+    for gather in gathers.values():
+        gather.start()
+
     results = {name: refs.pop("r_" + name) for name in GRADS}
-    outs = {name: refs.pop("o_" + name) for name in GRADS}
-    reduces = {
-        name: Reduce(
-            links, name, refs[name], refs.pop("c_" + name), refs.pop("x_" + name),
-            refs.pop("y_" + name), refs.pop("z_" + name), results[name], group,
+    reduces = {}
+    for name, first, rows, across_first in UNITS:
+        unit = unit_name(name, first)
+        part = pl.ds(first, rows)
+        reduces.setdefault(name, []).append(
+            Reduce(
+                links, unit, refs[name].at[:, part, :], refs.pop("c_" + unit),
+                refs.pop("f_" + unit), refs.pop("s_" + unit), refs.pop("z_" + unit),
+                results[name].at[part, :], group, across_first,
+            )
         )
-        for name in GRADS
-    }
     stages, inboxes = refs.pop("sum_stages"), refs.pop("sum_inboxes")
     refs["sums"] = stages.at[0]
-    total = Total(links, "sums", stages, inboxes, refs.pop("sum_far"), refs.pop("o_sums"), group)
-
+    total = Total(links, "sums", stages, inboxes, refs.pop("sum_far"), refs.pop("r_sums"), group)
     shards = packs.shape[0]
 
     def table():
-        rows = refs["rel_rows"]
         return jnp.concatenate(
-            [packs[shard, 0:rows, : 2 * LANES] for shard in range(shards)], axis=0
+            [packs[shard, 0:heads_here, : 2 * LANES] for shard in range(shards)], axis=0
         )
 
     def qkv_bias(part):
@@ -921,126 +1009,211 @@
     def up_bias(index):
         return packs[index, 6:7, :]
 
-    refs.update(table=table, qkv_bias=qkv_bias, up_bias=up_bias, rel_rows=4)
+    refs["vectors"] = [refs.pop(name) for name in VECTORS]
+    refs.update(table=table, qkv_bias=qkv_bias, up_bias=up_bias)
+    h_out, h_d_in = refs.pop("h_out"), refs.pop("h_d_in")
     local = Local(refs, links.tp * (refs["x"].shape[0] // TOK))
 
-    def output(name):
-        fin, out = results[name], outs[name]
-        if name == "gm":
-            out[...] = fin[...].astype(F32)
-        elif name == "gqkv":
+    def forward(*names):
+        for name in names:
+            gathers[name].forward()
+
+    def beside(*names):
+        for name in names:
+            gathers[name].forward_beside()
+
+    def ready(*names):
+        for name in names:
+            gathers[name].finish()
+
+    def run(*units):
+        for name, index in units:
+            reduces[name][index].run()
+
+    gd0, gd1, gu0, gu1, gp0 = ("gd", 0), ("gd", 1), ("gu", 0), ("gu", 1), ("gp", 0)
+    qkv0, qkv1, gm0, gm1 = ("gqkv", 0), ("gqkv", 1), ("gm", 0), ("gm", 1)
+    windows, steps = local.windows, local.steps
+
+    stages[0] = jnp.zeros_like(stages[0])
+    local.spread_vectors()
+    local.merge_norm()
+    local.prepare()
+    forward("pack")
+    local.grad_rows()
+    ready("pack")
+    local.table_bias()
+    forward("wm")
+    ready("wm")
+    local.merge()
+    forward("wq")
+    local.attn_norm()
+    forward("wk", "wv")
+    beside("wq")
+    ready("wq")
+    local.project(0)
+    beside("wk")
+    ready("wk")
+    local.project(1)
+    beside("wv")
+    ready("wv")
+    local.project(2)
+    forward("wp")
+
+    def attend(first, last):
+        local.attend(first * windows // 8, last * windows // 8)
+
+    attend(0, 2)
+    beside("wp")
+    forward("wu")
+    attend(2, 4)
+    ready("wp")
+    forward("wd")
+    attend(4, 6)
+    beside("wu", "wd")
+    attend(6, 8)
+    local.attn_out()
+    local.mlp_norm()
+    ready("wu")
+    local.up()
+    ready("wd")
+
+    def attend_back(index):
+        local.attend_back((7 - index) * windows // 8, (8 - index) * windows // 8)
+
+    tiles = local.units // local.tile
+    local.down_weight_back()
+    run(gd0, gd1)
+    local.hidden_back(0, tiles // 2)
+    run(gd0, gd1)
+    local.hidden_back(tiles // 2, tiles)
+    run(gu0, gu1)
+    local.up_back()
+    run(gu0, gu1)
+    local.mlp_back()
+    run(gd0)
+    local.proj_back()
+    run(gp0)
+    attend_back(0)
+    run(gp0, gd1)
+    attend_back(1)
+    run(gd0)
+    attend_back(2)
+    run(gu0, gd1)
+    attend_back(3)
+    run(gd0)
+    attend_back(4)
+    run(gu1, gu0)
+    attend_back(5)
+    run(gd1, gd0, gp0)
+    attend_back(6)
+    run(gu1, gu0)
+    attend_back(7)
+    run(gd1, gp0)
+    local.qkv_weight_back()
+    run(qkv0, qkv1, gu1, gu0)
+    local.qkv_back()
+    run(qkv0, qkv1, gp0)
+    local.attn_back()
+    run(gd0, gu1, gd1)
+    local.merge_weight_back()
+    run(gm0, gm1, qkv1, gp0)
+    local.merge_in_back()
+    run(gm0, gm1)
+    local.bias_back()
+    run(qkv0, qkv1)
+    local.down()
+    local.finish()
+    done = [links.keep("out", local.out, h_out)]
+    run(gm1, gm0)
+    totals = local.merge_back(0, 4 * steps // 7)
+    run(qkv0, qkv1, gm1, gm0)
+    local.merge_back(4 * steps // 7, steps, totals)
+    done.append(links.keep("d_in", local.d_in, h_d_in))
+    total.run()
+    run(qkv0, qkv1)
+    total.run()
+    run(gm0, gm1)
+    total.run()
+    run(qkv0, qkv1, gu0, gu1, gp0)
+    total.run()
+    run(gm0, gm1)
+    total.run()
+    run(qkv0, gm0, gm1)
+    total.run()
+    for copy in done:
+        copy.wait()
+    links.drain()
+
+
+def finish_kernel(names, *refs):
+    refs = dict(zip(names, refs, strict=True))
+    tp = lax.axis_index("tp")
+    pieces, number = [], 0
+    for name in ("d_in", "out"):
+        source, target, held = refs["h_" + name], refs["o_" + name], refs["v_" + name]
+        size = held.shape[0] // PIECES
+        for index in range(PIECES):
+            at = pl.ds(index * size, size)
+            sems = refs["sems"].at[number], refs["sems"].at[number + 1]
+            number += 2
+            pieces.append(
+                (
+                    pltpu.make_async_copy(source.at[at], held.at[at], sems[0]),
+                    pltpu.make_async_copy(held.at[at], target.at[at], sems[1]),
+                )
+            )
+    for incoming, _ in pieces:
+        incoming.start()
+    sums = refs["r_sums"]
+    for row, name in enumerate(
+        ("merge_gain", "merge_bias", "attn_gain", "attn_bias", "proj_bias", "mlp_gain",
+         "mlp_bias", "down_bias")
+    ):
+        out = refs["o_" + name]
+        out[...] = sums[SUM_ROWS[row] : SUM_ROWS[row] + out.shape[0], :]
+    for index in range(2):
+        refs["o_qv"][index : index + 1, :] = sums[pl.ds(SUM_ROWS[8 + index] + tp, 1), :]
+    blocks = refs["o_ub"].shape[0]
+    for index in range(blocks):
+        refs["o_ub"][index : index + 1, :] = sums[
+            pl.ds(SUM_ROWS[10] + tp * blocks + index, 1), :
+        ]
+    mine = refs["o_rel"].shape[0]
+    heads = SHARDS * mine
+    for index in range(mine):
+        first = SUM_ROWS[11] + tp * mine + index
+        low, high = sums[pl.ds(first, 1), :], sums[pl.ds(first + heads, 1), :]
+        refs["o_rel"][index : index + 1, :LANES] = low
+        refs["o_rel"][index : index + 1, LANES:] = high[:, : REL - LANES]
+    for name in GRADS:
+        result, out = refs["r_" + name], refs["o_" + name]
+        if len(out.shape) == 3:
             rows = out.shape[1]
-            for part in range(3):
-                out[part] = fin[part * rows : (part + 1) * rows, :].astype(F32)
+            for part in range(out.shape[0]):
+                out[part] = result[part * rows : (part + 1) * rows, :].astype(F32)
         else:
             rows = out.shape[0]
             for block in range(out.shape[1] // LANES):
                 lanes = slice(block * LANES, (block + 1) * LANES)
-                out[:, lanes] = fin[block * rows : (block + 1) * rows, :].astype(F32)
-
-    stages[0] = jnp.zeros_like(stages[0])
-    local.prepare()
-    local.merge_norm()
-    gathers["wm"].forward()
-    gathers["pack"].forward()
-    gathers["wm"].finish()
-    gathers["pack"].finish()
-    local.merge()
-    gathers["wqkv"].forward()
-    gathers["wp"].forward()
-    local.attn_norm()
-    local.table_bias()
-    gathers["wqkv"].forward_beside()
-    gathers["wp"].forward_beside()
-    gathers["wqkv"].finish()
-    local.project()
-    windows = local.windows
-    quarter = windows // 4
-    local.attend(0, quarter)
-    gathers["wu"].forward()
-    gathers["wp"].finish()
-    local.attend(quarter, 2 * quarter)
-    gathers["wu"].forward_beside()
-    gathers["wd"].forward()
-    local.attend(2 * quarter, 3 * quarter)
-    gathers["wd"].forward_beside()
-    local.attend(3 * quarter, windows)
-    local.attn_out()
-    local.mlp_norm()
-    gathers["wu"].finish()
-    local.up()
-    gathers["wd"].finish()
-    local.down()
-    local.finish()
-
-    each(refs["gd"].shape[0], local.down_back)
-    reduces["gd"].run()
-    reduces["gu"].run()
-    local.up_back()
-    reduces["gd"].run()
-    reduces["gu"].run()
-    local.mlp_back()
-    local.proj_back()
-    reduces["gp"].run()
-    local.attend_back(3 * quarter, windows)
-    reduces["gp"].run()
-    reduces["gd"].run()
-    local.attend_back(2 * quarter, 3 * quarter)
-    reduces["gd"].run()
-    reduces["gu"].run()
-    local.attend_back(quarter, 2 * quarter)
-    reduces["gd"].run()
-    reduces["gu"].run()
-    reduces["gp"].run()
-    local.attend_back(0, quarter)
-    reduces["gd"].run()
-    reduces["gu"].run()
-    reduces["gp"].run()
-    local.bias_back()
-    local.qkv_back()
-    reduces["gqkv"].run()
-    reduces["gd"].run()
-    reduces["gu"].run()
-    reduces["gp"].run()
-    local.attn_back()
-    reduces["gqkv"].run()
-    reduces["gp"].run()
-    output("gd")
-    local.merge_weight_back()
-    reduces["gm"].run()
-    reduces["gu"].run()
-    local.merge_in_back()
-    reduces["gm"].run()
-    reduces["gp"].run()
-    local.merge_back()
-    total.run()
-    total.run()
-    reduces["gqkv"].run()
-    reduces["gm"].run()
-    total.run()
-    reduces["gqkv"].run()
-    reduces["gm"].run()
-    total.run()
-    output("gu")
-    output("gp")
-    reduces["gqkv"].run()
-    reduces["gm"].run()
-    total.run()
-    reduces["gqkv"].run()
-    reduces["gm"].run()
-    total.run()
-    reduces["gqkv"].run()
-    reduces["gm"].run()
-    output("gqkv")
-    output("gm")
-    links.drain()
+                out[:, lanes] = result[block * rows : (block + 1) * rows, :].astype(F32)
+    for incoming, outgoing in pieces:
+        incoming.wait()
+        outgoing.start()
+    for _, outgoing in pieces:
+        outgoing.wait()
+
+
+SHARDS = 4
+PIECES = 7
+VMEM_SPEC = pl.BlockSpec(memory_space=pltpu.VMEM)
+SMEM_SPEC = pl.BlockSpec(memory_space=pltpu.SMEM)
+HBM_SPEC = pl.BlockSpec(memory_space=pl.ANY)
 
 
 def whole_call(group, inputs):
     rows, wide = inputs["x"].shape
-    shards = 4
     width = inputs["own_wu"].shape[0]
-    units = shards * inputs["own_wu"].shape[1]
+    units = SHARDS * inputs["own_wu"].shape[1]
     depth = dict(gd=units, gu=units, gp=width, gqkv=3 * width, gm=wide)
     scratch = local_scratch(rows, wide, width, units)
     scratch.update(
@@ -1049,41 +1222,41 @@
         wp=pltpu.VMEM((width, width), BF16),
         wu=pltpu.VMEM((width, units), BF16),
         wd=pltpu.VMEM((units, width), BF16),
-        packs=pltpu.VMEM((shards,) + inputs["pack"].shape, F32),
+        pack=pltpu.VMEM((8, units // SHARDS), F32),
+        packs=pltpu.VMEM((SHARDS, 8, units // SHARDS), F32),
+        out=pltpu.VMEM((rows, width), BF16),
+        d_in=pltpu.VMEM((rows, wide), F32),
     )
     for name in GRADS:
-        size = depth[name]
-        scratch[name] = pltpu.VMEM((shards, size, LANES), BF16)
-        scratch["c_" + name] = pltpu.VMEM((2, size, LANES), BF16)
-        scratch["x_" + name] = pltpu.VMEM((size, LANES), BF16)
-        scratch["y_" + name] = pltpu.VMEM((size // 2, LANES), BF16)
-        scratch["z_" + name] = pltpu.VMEM((group - 1, size // 2 // group, LANES), BF16)
-        scratch["r_" + name] = pltpu.VMEM((size, LANES), BF16)
+        scratch[name] = pltpu.VMEM((SHARDS, depth[name], LANES), BF16)
+    for name, first, size, across_first in UNITS:
+        unit = unit_name(name, first)
+        half = size // 2
+        scratch["c_" + unit] = pltpu.VMEM((2, size, LANES), BF16)
+        first_shape = (size, LANES) if across_first else (2, half, LANES)
+        scratch["f_" + unit] = pltpu.VMEM(first_shape, BF16)
+        scratch["s_" + unit] = pltpu.VMEM((half, LANES), BF16)
+        scratch["z_" + unit] = pltpu.VMEM((group - 1, half // group, LANES), BF16)
     scratch["sum_stages"] = pltpu.VMEM((4, SUM_SIZE, LANES), F32)
     scratch["sum_inboxes"] = pltpu.VMEM((3, SUM_SIZE, LANES), F32)
     scratch["sum_far"] = pltpu.VMEM((group - 1, SUM_SIZE // group, LANES), F32)
-    count = 6 * 6 + len(GRADS) * (5 + 2 * group) + 4 + 2 * group
+    count = 8 * 6 + len(UNITS) * (5 + 2 * group) + 6 + 2 * group
     scratch["send_sems"] = pltpu.SemaphoreType.DMA((count,))
     scratch["recv_sems"] = pltpu.SemaphoreType.DMA((count,))
     outs = dict(
-        out=jax.ShapeDtypeStruct((rows, width), BF16),
-        d_in=jax.ShapeDtypeStruct((rows, wide), F32),
-        o_gm=jax.ShapeDtypeStruct(inputs["own_wm"].shape, F32),
-        o_gqkv=jax.ShapeDtypeStruct(inputs["own_wqkv"].shape, F32),
-        o_gp=jax.ShapeDtypeStruct(inputs["own_wp"].shape, F32),
-        o_gu=jax.ShapeDtypeStruct(inputs["own_wu"].shape, F32),
-        o_gd=jax.ShapeDtypeStruct(inputs["own_wd"].shape, F32),
-        o_sums=jax.ShapeDtypeStruct((SUM_SIZE, LANES), F32),
+        h_out=jax.ShapeDtypeStruct((rows, width), BF16),
+        h_d_in=jax.ShapeDtypeStruct((rows, wide), F32),
+        r_sums=jax.ShapeDtypeStruct((SUM_SIZE, LANES), F32),
     )
+    for name in GRADS:
+        outs["r_" + name] = jax.ShapeDtypeStruct((depth[name], LANES), BF16)
     names = INPUTS + OUTPUTS + tuple(scratch)
-    vmem = pl.BlockSpec(memory_space=pltpu.VMEM)
-    smem = pl.BlockSpec(memory_space=pltpu.SMEM)
-    hbm = pl.BlockSpec(memory_space=pl.ANY)
+    in_vmem = 5 + len(VECTORS)
     return pl.pallas_call(
         functools.partial(whole_kernel, names, group, {}),
         out_shape=[outs[name] for name in OUTPUTS],
-        in_specs=[smem, smem, vmem, vmem, vmem, hbm] + [hbm] * len(WEIGHTS),
-        out_specs=[vmem] * len(OUTPUTS),
+        in_specs=[SMEM_SPEC] * 2 + [VMEM_SPEC] * in_vmem + [HBM_SPEC] * len(WEIGHTS),
+        out_specs=[HBM_SPEC] * 2 + [VMEM_SPEC] * (len(OUTPUTS) - 2),
         scratch_shapes=list(scratch.values()),
         compiler_params=pltpu.CompilerParams(
             vmem_limit_bytes=63 * MIB, collective_id=0, has_side_effects=True
@@ -1091,8 +1264,20 @@
     )(*[inputs[name] for name in INPUTS])
 
 
-def pad_to(values, rows, lanes):
-    return jnp.pad(values, ((0, rows - values.shape[0]), (0, lanes - values.shape[1])))
+def finish_call(results, shapes):
+    names = OUTPUTS + tuple("o_" + name for name in shapes) + ("v_out", "v_d_in", "sems")
+    return pl.pallas_call(
+        functools.partial(finish_kernel, names),
+        out_shape=list(shapes.values()),
+        in_specs=[HBM_SPEC] * 2 + [VMEM_SPEC] * (len(OUTPUTS) - 2),
+        out_specs=[HBM_SPEC] * 2 + [VMEM_SPEC] * (len(shapes) - 2),
+        scratch_shapes=[
+            pltpu.VMEM(shapes["out"].shape, BF16),
+            pltpu.VMEM(shapes["d_in"].shape, F32),
+            pltpu.SemaphoreType.DMA((4 * PIECES,)),
+        ],
+        compiler_params=pltpu.CompilerParams(vmem_limit_bytes=63 * MIB),
+    )(*results)
 
 
 def on_device(
@@ -1100,66 +1285,33 @@
     attn_bias, query_key_value_weight, qv_bias, rel_table, proj_weight, proj_bias, mlp_gain,
     mlp_bias, up_weight, up_bias, down_weight, down_bias,
 ):
-    tp_index = lax.axis_index("tp")
-    wide, width, tile = merge_gain.shape[0], down_bias.shape[0], up_bias.shape[0]
-    gains = jnp.concatenate(
-        [
-            pad_to(vector.astype(F32)[None], 1, wide)
-            for vector in (
-                merge_gain, merge_bias, attn_gain, attn_bias, mlp_gain, mlp_bias, proj_bias,
-                down_bias,
-            )
-        ],
-        axis=0,
+    vectors = dict(
+        merge_gain=merge_gain, merge_bias=merge_bias, attn_gain=attn_gain, attn_bias=attn_bias,
+        mlp_gain=mlp_gain, mlp_bias=mlp_bias, proj_bias=proj_bias, down_bias=down_bias,
     )
-    pack = jnp.concatenate(
-        [
-            pad_to(rel_table.T.astype(F32), 4, tile),
-            pad_to(qv_bias.astype(F32), 2, tile),
-            pad_to(up_bias.astype(F32)[None], 2, tile),
-        ],
-        axis=0,
+    blocks = {name: vector.reshape(-1, LANES) for name, vector in vectors.items()}
+    arrays = dict(
+        valid=window_valid, edge=window_edge, x=inputs, grad_out=grad_out, rel=rel_table.T,
+        qv=qv_bias, ub=up_bias.reshape(-1, LANES), own_wm=merge_weight,
+        own_wqkv=jnp.transpose(query_key_value_weight, (1, 0, 2)), own_wp=proj_weight,
+        own_wu=up_weight, own_wd=down_weight, **blocks,
     )
-    out, d_in, gm, gqkv, gp, gu, gd, sums = whole_call(
-        lax.axis_size("sp") // 2,
-        dict(
-            valid=window_valid, edge=window_edge, x=inputs, grad_out=grad_out, gains=gains,
-            pack=pack, own_wm=merge_weight,
-            own_wqkv=jnp.transpose(query_key_value_weight, (1, 0, 2)), own_wp=proj_weight,
-            own_wu=up_weight, own_wd=down_weight,
-        ),
+    results = whole_call(lax.axis_size("sp") // 2, arrays)
+    f32_like = lambda array: jax.ShapeDtypeStruct(array.shape, F32)
+    shapes = dict(
+        out=jax.ShapeDtypeStruct(grad_out.shape, BF16), d_in=f32_like(inputs),
+        gm=f32_like(merge_weight), gqkv=f32_like(arrays["own_wqkv"]), gp=f32_like(proj_weight),
+        gu=f32_like(up_weight), gd=f32_like(down_weight), qv=f32_like(qv_bias),
+        rel=f32_like(arrays["rel"]), ub=f32_like(arrays["ub"]),
+        **{name: f32_like(block) for name, block in blocks.items()},
     )
-
-    def vector(row, size):
-        return lax.slice_in_dim(sums, SUM_ROWS[row], SUM_ROWS[row] + size // LANES).reshape(-1)
-
-    def mine(whole, size):
-        return lax.dynamic_slice_in_dim(whole, tp_index * size, size, 0)
-
-    heads = width // HD
-    table = jnp.concatenate(
-        [sums[SUM_ROWS[11] + half * heads :][:heads] for half in range(2)], axis=1
-    )[:, :REL]
-    qv = jnp.stack([mine(vector(row, width), qv_bias.shape[1]) for row in (8, 9)])
+    done = dict(zip(shapes, finish_call(results, shapes), strict=True))
+    flat = lambda name: done[name].reshape(-1)
     return (
-        out,
-        d_in,
-        vector(0, wide),
-        vector(1, wide),
-        gm,
-        vector(2, width),
-        vector(3, width),
-        jnp.transpose(gqkv, (1, 0, 2)),
-        qv,
-        mine(table, rel_table.shape[1]).T,
-        gp,
-        vector(4, width),
-        vector(5, width),
-        vector(6, width),
-        gu,
-        mine(vector(10, 4 * tile), tile),
-        gd,
-        vector(7, width),
+        done["out"], done["d_in"], flat("merge_gain"), flat("merge_bias"), done["gm"],
+        flat("attn_gain"), flat("attn_bias"), jnp.transpose(done["gqkv"], (1, 0, 2)), done["qv"],
+        done["rel"].T, done["gp"], flat("proj_bias"), flat("mlp_gain"), flat("mlp_bias"),
+        done["gu"], flat("ub"), done["gd"], flat("down_bias"),
     )
 
 

time: 205 us -> 162 us (0.79)
  local copies, waits for them, and re-layouts: 21 us -> 0 us
  Pallas kernels: 178 us -> 161 us
  other arithmetic: 3.1 us -> 0 us
    pallas_call x1, Pallas kernels: 178 us -> 154 us  [whole_call(): pl.pallas_call(functools.partial(whole_kernel, names, group, {}), out_sha...]
    unnamed x17 -> x0, local copies, waits for them, and re-layouts: 10.6 us -> none
    pallas_call x0 -> x1, Pallas kernels: none -> 6.71 us  [finish_call(): pl.pallas_call(functools.partial(finish_kernel, names), out_shape=list(sh...]
    broadcast_in_dim x9 -> x0, local copies, waits for them, and re-layouts: 6.16 us -> none  [the longest x8 5.48 us: on_device(): vector.astype(F32)[None]]
    reshape x3 -> x0, local copies, waits for them, and re-layouts: 3.39 us -> none  [vector(): lax.slice_in_dim(sums, SUM_ROWS[row], SUM_ROWS[row] + size // LANES)]
where the time goes in v3:
time: 162 us; the launch traced here: 161 us
  Pallas kernels  161 us (99%)
    pallas_call x1, Pallas kernels, whole_call(): pl.pallas_call(functools.partial(whole_kernel, names, group, {}), out_sha...  154 us
    pallas_call x1, Pallas kernels, finish_call(): pl.pallas_call(functools.partial(finish_kernel, names), out_shape=list(sh...  6.71 us

profile of v3, /device:TPU:0, one launch (start us, length us, event | category | flops | bytes accessed | tf_op | source)
XLA Modules:
  0.0 161.4 jit_solution(12637415594031566923)
XLA Ops:
  0.7 153.9 %shard_map.331 = (bf16[784,512]{1,0:T(8,128)(2,1)}, f32[784,1024]{1,0:T(8,128)}, bf16[2048,128]{1,0:T(8,128)(2,1)}, bf16[2048,128]{1,0:T(8,128)(2,1)}, bf16[512,...) custom-call(s32[64]{0:T(128)} %refs_0_.1, s32[64]{0:T(128)} %refs_1_.1, ...), custom_call_target="tpu_custom_call" | custom-call | tf_op jit(solution)/shard_map/pallas_call | solution.py:1255
  154.5 6.7 %shard_map.332 = (bf16[784,512]{1,0:T(8,128)(2,1)}, f32[784,1024]{1,0:T(8,128)}, f32[1024,128]{1,0:T(8,128)}, f32[3,512,128]{2,1,0:T(8,128)}, f32[128,512]{1,0:T...) custom-call(bf16[784,512]{1,0:T(8,128)(2,1)} %get-tuple-element.44.r, ...), custom_call_target="tpu_custom_call" | custom-call | tf_op jit(solution)/shard_map/pallas_call | solution.py:1269

commit v4 on v3

--- a/solution.py
+++ b/solution.py
@@ -186,69 +186,146 @@
     ref[...] = pltpu.roll(pltpu.roll(ref[...], down, 0), right, 1)
 
 
-def attention_forward(window, edge, qkv, bias_ref, probs_ref, att_ref):
-    base = pl.ds(pl.multiple_of(window * (TOK - 1), 16), SPAN)
+def attention_forward(first, edges, qkv, bias_ref, probs_ref, att_ref):
     masks = head_masks()
-    ones = same_head(GROUP * SPAN, GROUP * SPAN)
-    row_index = iota((SPAN, 1), 0) - window
-    row_in = (row_index >= 0) & (row_index < TOK)
-    row_region = region_ids(row_index, edge, 8)
-    lane_region = region_ids((iota((1, GROUP * SPAN), 1) & (SPAN - 1)) - window, edge, 16)
-    allowed = row_region == lane_region
+    size = GROUP * SPAN
+    ones = same_head(size, size)
     first_half = iota((SPAN, LANES), 1) < SPAN
-    keep = row_in.astype(F32)
-    groups = att_ref.shape[1] // LANES
-    for group in range(groups):
-        lanes = pl.ds(group * LANES, LANES)
-        wide = pl.ds(group * GROUP * SPAN, GROUP * SPAN)
-        query, key, value = (qkv[part, base, lanes] for part in range(3))
-        logits = dot_cols(query, spread_heads(key, masks)) * (HD**-0.5) + bias_ref[:, wide]
-        logits = jnp.where(allowed, logits, NEG_FILL)
-        tops = []
-        for half in range(GROUP * SPAN // LANES):
-            piece = logits[:, half * LANES : (half + 1) * LANES]
-            top_low = jnp.max(jnp.where(first_half, piece, 2 * NEG_FILL), -1, keepdims=True)
-            top_high = jnp.max(jnp.where(first_half, 2 * NEG_FILL, piece), -1, keepdims=True)
-            tops.append(jnp.where(first_half, top_low, top_high))
-        terms = jnp.exp(logits - jnp.concatenate(tops, axis=1))
-        totals = dot(terms.astype(BF16), ones)
-        probs = (terms * (keep / totals)).astype(BF16)
-        probs_ref[window, :, wide] = probs
-        attended = dot(probs, spread_heads(value, masks))
-        att_ref[base, lanes] = jnp.where(
-            row_in, attended, att_ref[base, lanes].astype(F32)
-        ).astype(BF16)
-
-
-def attention_backward(window, qkv, d_att, probs_ref, d_bias_ref, d_qkv):
-    base = pl.ds(pl.multiple_of(window * (TOK - 1), 16), SPAN)
+    groups = range(att_ref.shape[1] // LANES)
+
+    def part_of(array, group, width):
+        return array[:, group * width : (group + 1) * width]
+
+    def tops(values):
+        found = []
+        for half in range(size // LANES):
+            piece = part_of(values, half, LANES)
+            low = jnp.max(jnp.where(first_half, piece, 2 * NEG_FILL), -1, keepdims=True)
+            high = jnp.max(jnp.where(first_half, 2 * NEG_FILL, piece), -1, keepdims=True)
+            found.append(jnp.where(first_half, low, high))
+        return jnp.concatenate(found, axis=1)
+
+    bias = bias_ref[...]
+    states = []
+    for index, edge in enumerate(edges):
+        window = first + index
+        base = pl.ds(pl.multiple_of(window * (TOK - 1), 16), SPAN)
+        row_index = iota((SPAN, 1), 0) - window
+        row_in = (row_index >= 0) & (row_index < TOK)
+        row_region = region_ids(row_index, edge, 8)
+        lane_region = region_ids((iota((1, size), 1) & (SPAN - 1)) - window, edge, 16)
+        query, key, value = (qkv[part, base, :] for part in range(3))
+        states.append((window, base, row_in, row_region == lane_region, query, key, value, bias))
+        bias = pltpu.roll(pltpu.roll(bias, 1, 0), 1, 1)
+    bias_ref[...] = bias
+
+    logits = [
+        [
+            jnp.where(
+                allowed,
+                dot_cols(
+                    part_of(query, group, LANES), spread_heads(part_of(key, group, LANES), masks)
+                )
+                * (HD**-0.5)
+                + part_of(shifted, group, size),
+                NEG_FILL,
+            )
+            for group in groups
+        ]
+        for _, _, _, allowed, query, key, _, shifted in states
+    ]
+    terms = [[jnp.exp(values - tops(values)) for values in row] for row in logits]
+    totals = [[dot(values.astype(BF16), ones) for values in row] for row in terms]
+    probs = [
+        [
+            (terms[index][group] * (state[2].astype(F32) / totals[index][group])).astype(BF16)
+            for group in groups
+        ]
+        for index, state in enumerate(states)
+    ]
+    attended = [
+        jnp.concatenate(
+            [
+                dot(probs[index][group], spread_heads(part_of(state[6], group, LANES), masks))
+                for group in groups
+            ],
+            axis=1,
+        )
+        for index, state in enumerate(states)
+    ]
+    for index, (window, base, row_in, *_) in enumerate(states):
+        for group in groups:
+            probs_ref[window, :, pl.ds(group * size, size)] = probs[index][group]
+        before = att_ref[base, :].astype(F32)
+        att_ref[base, :] = jnp.where(row_in, attended[index], before).astype(BF16)
+
+
+def attention_backward(windows, qkv, d_att, probs_ref, d_bias_ref, d_qkv):
     masks = head_masks()
-    ones = same_head(GROUP * SPAN, GROUP * SPAN)
-    row_index = iota((SPAN, 1), 0) - window
-    row_in = (row_index >= 0) & (row_index < TOK)
-    groups = d_att.shape[1] // LANES
+    size = GROUP * SPAN
+    ones = same_head(size, size)
+    groups = range(d_att.shape[1] // LANES)
     factor = HD**-0.5
 
-    def put(part, lanes, values):
-        d_qkv[part, base, lanes] = jnp.where(
-            row_in, values, d_qkv[part, base, lanes].astype(F32)
-        ).astype(BF16)
-
-    for group in range(groups):
-        lanes = pl.ds(group * LANES, LANES)
-        wide = pl.ds(group * GROUP * SPAN, GROUP * SPAN)
-        query, key, value = (qkv[part, base, lanes] for part in range(3))
-        upstream = d_att[base, lanes]
-        probs = probs_ref[window, :, wide]
-        probs_wide = probs.astype(F32)
-        d_probs = dot_cols(upstream, spread_heads(value, masks))
-        weighted = d_probs * probs_wide
-        delta = dot(weighted.astype(BF16), ones)
-        d_logits = (weighted - probs_wide * delta).astype(BF16)
-        d_bias_ref[:, wide] += d_logits.astype(F32)
-        put(0, lanes, dot(d_logits, spread_heads(key, masks)) * factor)
-        put(1, lanes, pick_heads(dot_rows(d_logits, query)) * factor)
-        put(2, lanes, pick_heads(dot_rows(probs, upstream)))
+    def part_of(array, group, width):
+        return array[:, group * width : (group + 1) * width]
+
+    states = []
+    for window in windows:
+        base = pl.ds(pl.multiple_of(window * (TOK - 1), 16), SPAN)
+        query, key, value = (qkv[part, base, :] for part in range(3))
+        states.append((base, query, key, value, d_att[base, :], probs_ref[window]))
+    d_bias = d_bias_ref[...]
+
+    weighted = [
+        [
+            dot_cols(
+                part_of(upstream, group, LANES),
+                spread_heads(part_of(value, group, LANES), masks),
+            )
+            * part_of(probs, group, size).astype(F32)
+            for group in groups
+        ]
+        for _, _, _, value, upstream, probs in states
+    ]
+    deltas = [[dot(values.astype(BF16), ones) for values in row] for row in weighted]
+    d_logits = [
+        [
+            (
+                weighted[index][group]
+                - part_of(state[5], group, size).astype(F32) * deltas[index][group]
+            ).astype(BF16)
+            for group in groups
+        ]
+        for index, state in enumerate(states)
+    ]
+    for row in d_logits:
+        d_bias = pltpu.roll(pltpu.roll(d_bias, SPAN - 1, 0), d_bias.shape[1] - 1, 1)
+        d_bias = d_bias + jnp.concatenate([values.astype(F32) for values in row], axis=1)
+    d_bias_ref[...] = d_bias
+    results = []
+    for index, (base, query, key, value, upstream, probs) in enumerate(states):
+        row = d_logits[index]
+        d_query = [
+            dot(row[group], spread_heads(part_of(key, group, LANES), masks)) * factor
+            for group in groups
+        ]
+        d_key = [
+            pick_heads(dot_rows(row[group], part_of(query, group, LANES))) * factor
+            for group in groups
+        ]
+        d_value = [
+            pick_heads(dot_rows(part_of(probs, group, size), part_of(upstream, group, LANES)))
+            for group in groups
+        ]
+        results.append([jnp.concatenate(values, axis=1) for values in (d_query, d_key, d_value)])
+    for index, window in enumerate(windows):
+        base = states[index][0]
+        row_index = iota((SPAN, 1), 0) - window
+        row_in = (row_index >= 0) & (row_index < TOK)
+        for part in range(3):
+            old = d_qkv[part, base, :].astype(F32)
+            d_qkv[part, base, :] = jnp.where(row_in, results[index][part], old).astype(BF16)
 
 
 def sum_rows(values):
@@ -264,7 +341,7 @@
         self.units = self.hidden.shape[1]
         self.windows = self.rows // TOK
         self.heads = self.width // HD
-        self.chunk = 16
+        self.chunk = 112
         self.steps = self.rows // self.chunk
         self.tile = self.units // self.gu.shape[0]
 
@@ -307,7 +384,7 @@
             self.merged[at, :] = (normed * gain + shift).astype(BF16)
             self.keep_stats(at, 0, mean, inv)
 
-        each(self.steps, step, 7)
+        each(self.steps, step)
 
     def merge(self):
         self.section[...] = dot(self.merged[...], self.wm[...]).astype(BF16)
@@ -321,7 +398,7 @@
             self.attn_in[at, :] = (normed * gain + shift).astype(BF16)
             self.keep_stats(at, 2, mean, inv)
 
-        each(self.steps, step, 7)
+        each(self.steps, step)
 
     def project(self, part):
         product = dot(self.attn_in[...], self.wqkv[part])
@@ -329,17 +406,16 @@
             product = product + self.qkv_bias(part)
         self.qkv[part] = product.astype(BF16)
 
-    def attend(self, first, last):
+    def attend(self, first, last, together=4):
         def step(index):
-            window = first + index
-            edge = self.edge[self.first_window + window]
-            attention_forward(window, edge, self.qkv, self.bias, self.probs, self.att)
-            shift_both(self.bias, True)
-
-        each(last - first, step)
+            window = first + index * together
+            edges = [self.edge[self.first_window + window + more] for more in range(together)]
+            attention_forward(window, edges, self.qkv, self.bias, self.probs, self.att)
+
+        each((last - first) // together, step)
 
     def attn_out(self):
-        self.resid[...] = dot(self.att[...], self.wp[...])
+        self.pre[...] = dot(self.att[...], self.wp[...])
 
     def mlp_norm(self):
         gain, shift = self.gain(4, self.width), self.gain(5, self.width)
@@ -347,29 +423,27 @@
 
         def step(index):
             at = rows_at(index, self.chunk)
-            total = self.section[at, :].astype(F32) + self.resid[at, :] + proj_bias
+            total = self.section[at, :].astype(F32) + self.pre[at, :] + proj_bias
             self.resid[at, :] = total
             normed, mean, inv = norm_rows(total)
             self.mlp_in[at, :] = (normed * gain + shift).astype(BF16)
             self.keep_stats(at, 4, mean, inv)
 
-        each(self.steps, step, 7)
-
-    def up(self):
-        def part(index):
-            columns = rows_at(index, self.tile)
-            self.pre[...] = dot(self.mlp_in[...], self.wu[:, columns])
-            shift = self.up_bias(index)
-
-            def activate(step):
-                at = rows_at(step, self.chunk)
-                value, rate = gelu_both(self.pre[at, :] + shift)
-                self.hidden[at, columns] = value.astype(BF16)
-                self.slope[at, columns] = rate.astype(BF16)
-
-            each(self.steps, activate, 7)
-
-        each(self.units // self.tile, part)
+        each(self.steps, step)
+
+    def up(self, index):
+        columns = rows_at(index, self.tile)
+        self.pre[...] = dot(self.mlp_in[...], self.wu[:, columns])
+        shift = self.up_bias(index)
+
+        def activate(step):
+            at = rows_at(step, self.chunk)
+            value, rate = gelu_both(self.pre[at, :] + shift)
+            self.hidden[at, columns] = value.astype(BF16)
+            self.slope[at, columns] = rate.astype(BF16)
+
+        each(self.steps, activate, 7)
+        put_blocks(self.gd, index, dot_rows(self.hidden[:, columns], self.d_mlp[...]))
 
     def down(self):
         self.pre[...] = dot(self.hidden[...], self.wd[...])
@@ -382,7 +456,7 @@
             return total + fold(grad)
 
         total = lax.fori_loop(
-            0, self.steps, step, jnp.zeros((8, self.width), F32), unroll=7
+            0, self.steps, step, jnp.zeros((8, self.width), F32)
         )
         self.put_sum(7, total)
 
@@ -394,34 +468,21 @@
             block = (self.resid[at, :] + self.pre[at, :] + down_bias) * self.stat(at, 6)
             self.out[at, :] = block.astype(BF16)
 
-        each(self.steps, step, 7)
-
-    def down_weight_back(self):
-        def part(index):
-            columns = rows_at(index, self.tile)
-            put_blocks(self.gd, index, dot_rows(self.hidden[:, columns], self.d_mlp[...]))
-
-        each(self.units // self.tile, part)
-
-    def hidden_back(self, first, last):
-        def part(step):
-            index = first + step
-            columns = rows_at(index, self.tile)
-            self.pre[...] = dot_cols(self.d_mlp[...], self.wd[columns, :])
-
-            def activate(step, total):
-                at = rows_at(step, self.chunk)
-                grad = (self.pre[at, :] * self.slope[at, columns].astype(F32)).astype(BF16)
-                self.d_pre[at, columns] = grad
-                return total + fold(grad.astype(F32))
-
-            total = lax.fori_loop(
-                0, self.steps, activate, jnp.zeros((8, self.tile), F32), unroll=7
-            )
-            self.put_up_sum(index, total)
-            put_blocks(self.gu, index, dot_rows(self.mlp_in[...], self.d_pre[:, columns]))
-
-        each(last - first, part)
+        each(self.steps, step)
+
+    def hidden_back(self, index):
+        columns = rows_at(index, self.tile)
+        self.pre[...] = dot_cols(self.d_mlp[...], self.wd[columns, :])
+
+        def activate(step, total):
+            at = rows_at(step, self.chunk)
+            grad = (self.pre[at, :] * self.slope[at, columns].astype(F32)).astype(BF16)
+            self.d_pre[at, columns] = grad
+            return total + fold(grad.astype(F32))
+
+        total = lax.fori_loop(0, self.steps, activate, jnp.zeros((8, self.tile), F32))
+        self.put_up_sum(index, total)
+        put_blocks(self.gu, index, dot_rows(self.mlp_in[...], self.d_pre[:, columns]))
 
     def up_back(self):
         self.pre[...] = dot_cols(self.d_pre[...], self.wu[...])
@@ -436,7 +497,7 @@
             upstream = self.pre[at, :]
             d_resid = self.d_mlp[at, :].astype(F32) + norm_back(upstream, normed, inv, gain)
             self.d_resid[at, :] = d_resid
-            self.d_mlp[at, :] = d_resid.astype(BF16)
+            self.d_attn[at, :] = d_resid.astype(BF16)
             return (
                 totals[0] + fold(upstream * normed),
                 totals[1] + fold(upstream),
@@ -444,26 +505,25 @@
             )
 
         blank = jnp.zeros((8, self.width), F32)
-        totals = lax.fori_loop(0, self.steps, step, (blank, blank, blank), unroll=7)
+        totals = lax.fori_loop(0, self.steps, step, (blank, blank, blank))
         for row, total in zip((5, 6, 4), totals):
             self.put_sum(row, total)
 
     def proj_back(self):
         size = self.width // self.gp.shape[0]
-        product = dot_rows(self.att[...], self.d_mlp[...])
+        product = dot_rows(self.att[...], self.d_attn[...])
         for index in range(self.gp.shape[0]):
             put_blocks(self.gp, index, product[index * size : (index + 1) * size])
-        self.att[...] = dot_cols(self.d_mlp[...], self.wp[...]).astype(BF16)
+        self.att[...] = dot_cols(self.d_attn[...], self.wp[...]).astype(BF16)
         self.d_bias[...] = jnp.zeros_like(self.d_bias)
 
-    def attend_back(self, first, last):
+    def attend_back(self, first, last, together=2):
         def step(index):
-            shift_both(self.d_bias, False)
-            attention_backward(
-                last - 1 - index, self.qkv, self.att, self.probs, self.d_bias, self.qkv
-            )
-
-        each(last - first, step)
+            top = last - 1 - index * together
+            windows = [top - less for less in range(together)]
+            attention_backward(windows, self.qkv, self.att, self.probs, self.d_bias, self.qkv)
+
+        each((last - first) // together, step)
 
     def bias_back(self):
         self.put_table(reduce_bias(self.d_bias, self.spread, self.heads))
@@ -495,7 +555,7 @@
             return totals[0] + fold(upstream * normed), totals[1] + fold(upstream)
 
         blank = jnp.zeros((8, self.width), F32)
-        totals = lax.fori_loop(0, self.steps, step, (blank, blank), unroll=7)
+        totals = lax.fori_loop(0, self.steps, step, (blank, blank))
         self.put_sum(2, totals[0])
         self.put_sum(3, totals[1])
 
@@ -503,22 +563,24 @@
         put_columns(self.gm, 0, dot_rows(self.merged[...], self.d_mlp[...]))
 
     def merge_in_back(self):
-        self.d_in[...] = dot_cols(self.d_mlp[...], self.wm[...])
+        for half, ref in enumerate((self.pre, self.d_resid)):
+            rows = slice(half * self.width, (half + 1) * self.width)
+            ref[...] = dot_cols(self.d_mlp[...], self.wm[rows, :])
 
     def merge_back(self, first, last, totals=None):
         gain = self.gain(0, self.wide)
 
         def step(index, totals):
-            at = rows_at(first + index, self.chunk)
+            at = rows_at(first + index, 16)
             inv = self.stat(at, 1)
             normed = (self.x[at, :].astype(F32) - self.stat(at, 0)) * inv
-            upstream = self.d_in[at, :]
+            upstream = jnp.concatenate([self.pre[at, :], self.d_resid[at, :]], axis=1)
             self.d_in[at, :] = norm_back(upstream, normed, inv, gain)
             return totals[0] + fold(upstream * normed), totals[1] + fold(upstream)
 
         blank = jnp.zeros((8, self.wide), F32)
         totals = lax.fori_loop(0, last - first, step, totals or (blank, blank), unroll=7)
-        if last == self.steps:
+        if last == self.rows // 16:
             self.put_sum(0, totals[0])
             self.put_sum(1, totals[1])
         return totals
@@ -577,6 +639,7 @@
         pre=pltpu.VMEM((rows, width), F32),
         d_mlp=pltpu.VMEM((rows, width), BF16),
         d_pre=pltpu.VMEM((rows, units), BF16),
+        d_attn=pltpu.VMEM((rows, width), BF16),
         d_resid=pltpu.VMEM((rows, width), F32),
         gains=pltpu.VMEM((8, wide), F32),
         stats=pltpu.VMEM((rows, 8), F32),
@@ -754,13 +817,16 @@
         self.seat = links.sp >> 1
         self.across = links.tp >> 1
         if across_first:
-            middle = [self.core_add_across, self.across_beside, self.beside_last]
+            middle = self.core_add_across, self.across_beside, self.beside_last
         else:
-            middle = [self.core_add_beside, self.beside_across, self.across_last]
-        self.steps = [self.core_send] + middle + [self.far_add, self.far_done, self.beside_done]
-
-    def run(self):
-        self.steps.pop(0)()
+            middle = self.core_add_beside, self.beside_across, self.across_last
+        self.steps = dict(
+            far=self.core_far, near=self.core_near, add=middle[0], first=middle[1],
+            second=middle[2], spread=self.far_add, back=self.far_done, last=self.beside_done,
+        )
+
+    def run(self, step):
+        self.steps.pop(step)()
 
     def label(self, *step):
         return (self.name,) + step
@@ -771,20 +837,26 @@
         start = half * self.half_rows + piece * self.piece
         return ref.at[pl.ds(pl.multiple_of(start, 16), self.piece), :]
 
-    def core_send(self):
-        links = self.links
-        for across in range(2):
-            links.send(
-                self.label("c", across), CORE, self.grads.at[(links.tp & 1) ^ 1 | 2 * across],
-                self.core_in.at[across],
-            )
-
-    def core_receive(self):
-        for across in range(2):
-            self.links.receive(self.label("c", across), CORE, self.core_in.at[across])
+    def core_send(self, across, name):
+        shard = (self.links.tp & 1) ^ 1 | 2 * across
+        self.links.send(
+            self.label(name), CORE, self.grads.at[shard], self.core_in.at[across]
+        )
+
+    def core_far(self):
+        self.core_send(self.across ^ 1, "cf")
+
+    def core_near(self):
+        self.core_send(self.across, "cn")
+
+    def receive_far(self):
+        self.links.receive(self.label("cf"), CORE, self.core_in.at[self.across ^ 1])
+
+    def receive_near(self):
+        self.links.receive(self.label("cn"), CORE, self.core_in.at[self.across])
 
     def core_add_across(self):
-        self.core_receive()
+        self.receive_far()
         other = self.links.tp ^ 2
         block = self.grads.at[other]
         add_rows(block, 0, self.rows, [(block, 0), (self.core_in.at[self.across ^ 1], 0)])
@@ -792,6 +864,7 @@
 
     def across_beside(self):
         links = self.links
+        self.receive_near()
         links.receive(self.label("x"), ACROSS, self.first_in)
         block = self.grads.at[links.tp]
         terms = [(block, 0), (self.core_in.at[self.across], 0), (self.first_in, 0)]
@@ -806,7 +879,8 @@
 
     def core_add_beside(self):
         links = self.links
-        self.core_receive()
+        self.receive_far()
+        self.receive_near()
         for across in range(2):
             block = self.grads.at[(links.tp & 1) | 2 * across]
             add_rows(block, 0, self.rows, [(block, 0), (self.core_in.at[across], 0)])
@@ -939,7 +1013,7 @@
     "down_bias",
 )
 INPUTS = (
-    ("valid", "edge", "x", "grad_out", "rel", "qv", "ub") + VECTORS
+    ("valid", "edge", "rel", "qv", "ub") + VECTORS + ("h_x", "h_grad_out")
     + tuple("own_" + name for name in WEIGHTS)
 )
 OUTPUTS = ("h_out", "h_d_in") + tuple("r_" + name for name in GRADS) + ("r_sums",)
@@ -952,6 +1026,10 @@
 def whole_kernel(names, group, plan, *refs):
     refs = dict(zip(names, refs, strict=True))
     links = Links(refs.pop("send_sems"), refs.pop("recv_sems"), plan)
+    arriving = [
+        links.keep(name, refs.pop("h_" + name), refs[name]) for name in ("x", "grad_out")
+    ]
+    rows = refs["x"].shape[0]
     own_pack, packs = refs.pop("pack"), refs.pop("packs")
     rel, qv, ub = refs.pop("rel"), refs.pop("qv"), refs.pop("ub")
     heads_here = rel.shape[0]
@@ -980,15 +1058,13 @@
 
     results = {name: refs.pop("r_" + name) for name in GRADS}
     reduces = {}
-    for name, first, rows, across_first in UNITS:
+    for name, first, size, across_first in UNITS:
         unit = unit_name(name, first)
-        part = pl.ds(first, rows)
-        reduces.setdefault(name, []).append(
-            Reduce(
-                links, unit, refs[name].at[:, part, :], refs.pop("c_" + unit),
-                refs.pop("f_" + unit), refs.pop("s_" + unit), refs.pop("z_" + unit),
-                results[name].at[part, :], group, across_first,
-            )
+        part = pl.ds(first, size)
+        reduces[unit] = Reduce(
+            links, unit, refs[name].at[:, part, :], refs.pop("c_" + unit),
+            refs.pop("f_" + unit), refs.pop("s_" + unit), refs.pop("z_" + unit),
+            results[name].at[part, :], group, across_first,
         )
     stages, inboxes = refs.pop("sum_stages"), refs.pop("sum_inboxes")
     refs["sums"] = stages.at[0]
@@ -1012,7 +1088,7 @@
     refs["vectors"] = [refs.pop(name) for name in VECTORS]
     refs.update(table=table, qkv_bias=qkv_bias, up_bias=up_bias)
     h_out, h_d_in = refs.pop("h_out"), refs.pop("h_d_in")
-    local = Local(refs, links.tp * (refs["x"].shape[0] // TOK))
+    local = Local(refs, links.tp * (rows // TOK))
 
     def forward(*names):
         for name in names:
@@ -1026,14 +1102,16 @@
         for name in names:
             gathers[name].finish()
 
-    def run(*units):
-        for name, index in units:
-            reduces[name][index].run()
-
-    gd0, gd1, gu0, gu1, gp0 = ("gd", 0), ("gd", 1), ("gu", 0), ("gu", 1), ("gp", 0)
-    qkv0, qkv1, gm0, gm1 = ("gqkv", 0), ("gqkv", 1), ("gm", 0), ("gm", 1)
-    windows, steps = local.windows, local.steps
-
+    def run(step, *units):
+        for unit in units:
+            reduces[unit].run(step)
+
+    gd0, gd1, gu0, gu1, gp0 = "gd0", "gd1024", "gu0", "gu1024", "gp0"
+    qkv0, qkv1, gm0, gm1 = "gqkv0", "gqkv1024", "gm0", "gm512"
+    windows = local.windows
+
+    for copy in arriving:
+        copy.wait()
     stages[0] = jnp.zeros_like(stages[0])
     local.spread_vectors()
     local.merge_norm()
@@ -1058,88 +1136,107 @@
     ready("wv")
     local.project(2)
     forward("wp")
-
-    def attend(first, last):
-        local.attend(first * windows // 8, last * windows // 8)
-
-    attend(0, 2)
+    local.attend(0, windows // 4)
     beside("wp")
     forward("wu")
-    attend(2, 4)
+    local.attend(windows // 4, windows // 2)
     ready("wp")
+    local.attend(windows // 2, windows)
     forward("wd")
-    attend(4, 6)
-    beside("wu", "wd")
-    attend(6, 8)
     local.attn_out()
+    beside("wu")
     local.mlp_norm()
     ready("wu")
-    local.up()
+
+    tiles = [links.tp ^ bits for bits in (3, 2, 1, 0)]
+    local.up(tiles[0])
+    run("far", gd0, gd1)
+    beside("wd")
+    local.up(tiles[1])
+    run("add", gd0, gd1)
+    local.up(tiles[2])
+    run("near", gd0, gd1)
+    local.up(tiles[3])
     ready("wd")
+    local.hidden_back(tiles[0])
+    run("far", gu0, gu1)
+    local.hidden_back(tiles[1])
+    run("add", gu0, gu1)
+    local.hidden_back(tiles[2])
+    run("near", gu0, gu1)
+    run("first", gd0)
+    local.hidden_back(tiles[3])
+    local.up_back()
+    local.mlp_back()
+    run("second", gd0)
+    run("first", gd1)
+    local.proj_back()
+    run("far", gp0)
+    run("near", gp0)
 
     def attend_back(index):
-        local.attend_back((7 - index) * windows // 8, (8 - index) * windows // 8)
-
-    tiles = local.units // local.tile
-    local.down_weight_back()
-    run(gd0, gd1)
-    local.hidden_back(0, tiles // 2)
-    run(gd0, gd1)
-    local.hidden_back(tiles // 2, tiles)
-    run(gu0, gu1)
-    local.up_back()
-    run(gu0, gu1)
-    local.mlp_back()
-    run(gd0)
-    local.proj_back()
-    run(gp0)
+        local.attend_back((3 - index) * windows // 4, (4 - index) * windows // 4)
+
     attend_back(0)
-    run(gp0, gd1)
+    run("add", gp0)
     attend_back(1)
-    run(gd0)
+    run("spread", gd0)
+    run("first", gu0)
+    run("second", gd1)
     attend_back(2)
-    run(gu0, gd1)
     attend_back(3)
-    run(gd0)
-    attend_back(4)
-    run(gu1, gu0)
-    attend_back(5)
-    run(gd1, gd0, gp0)
-    attend_back(6)
-    run(gu1, gu0)
-    attend_back(7)
-    run(gd1, gp0)
     local.qkv_weight_back()
-    run(qkv0, qkv1, gu1, gu0)
+    run("far", qkv0, qkv1)
+    run("near", qkv0, qkv1)
+    run("back", gd0)
+    run("spread", gd1)
+    run("second", gu0)
+    run("first", gu1)
     local.qkv_back()
-    run(qkv0, qkv1, gp0)
+    run("add", qkv0, qkv1)
+    run("first", gp0)
     local.attn_back()
-    run(gd0, gu1, gd1)
+    run("spread", gu0)
+    run("back", gd1)
+    run("second", gu1)
     local.merge_weight_back()
-    run(gm0, gm1, qkv1, gp0)
+    run("far", gm0, gm1)
+    run("near", gm0, gm1)
+    run("second", gp0)
+    run("first", qkv1)
     local.merge_in_back()
-    run(gm0, gm1)
+    run("add", gm0, gm1)
+    run("back", gu0)
+    run("spread", gu1, gp0)
+    third = rows // 16 // 7
+    totals = local.merge_back(0, 3 * third)
+    run("first", qkv0)
+    run("second", qkv1)
+    local.merge_back(3 * third, 7 * third, totals)
+    done = [links.keep("d_in", local.d_in, h_d_in)]
+    run("back", gp0, gu1)
+    run("first", gm1, gm0)
     local.bias_back()
-    run(qkv0, qkv1)
+    total.run()
+    run("second", qkv0)
+    run("spread", qkv1)
     local.down()
+    total.run()
+    run("second", gm1, gm0)
     local.finish()
-    done = [links.keep("out", local.out, h_out)]
-    run(gm1, gm0)
-    totals = local.merge_back(0, 4 * steps // 7)
-    run(qkv0, qkv1, gm1, gm0)
-    local.merge_back(4 * steps // 7, steps, totals)
-    done.append(links.keep("d_in", local.d_in, h_d_in))
+    done.append(links.keep("out", local.out, h_out))
     total.run()
-    run(qkv0, qkv1)
+    run("spread", qkv0)
+    run("back", qkv1)
+    run("spread", gm1, gm0)
     total.run()
-    run(gm0, gm1)
+    run("last", gd0, gd1, gu0, gu1, gp0)
+    run("back", qkv0)
     total.run()
-    run(qkv0, qkv1, gu0, gu1, gp0)
+    run("back", gm1, gm0)
     total.run()
-    run(gm0, gm1)
-    total.run()
-    run(qkv0, gm0, gm1)
-    total.run()
+    run("last", qkv0, qkv1, gm0, gm1)
+    assert not any(reduce.steps for reduce in reduces.values())
     for copy in done:
         copy.wait()
     links.drain()
@@ -1211,7 +1308,7 @@
 
 
 def whole_call(group, inputs):
-    rows, wide = inputs["x"].shape
+    rows, wide = inputs["h_x"].shape
     width = inputs["own_wu"].shape[0]
     units = SHARDS * inputs["own_wu"].shape[1]
     depth = dict(gd=units, gu=units, gp=width, gqkv=3 * width, gm=wide)
@@ -1224,6 +1321,8 @@
         wd=pltpu.VMEM((units, width), BF16),
         pack=pltpu.VMEM((8, units // SHARDS), F32),
         packs=pltpu.VMEM((SHARDS, 8, units // SHARDS), F32),
+        x=pltpu.VMEM((rows, wide), BF16),
+        grad_out=pltpu.VMEM((rows, width), BF16),
         out=pltpu.VMEM((rows, width), BF16),
         d_in=pltpu.VMEM((rows, wide), F32),
     )
@@ -1240,7 +1339,7 @@
     scratch["sum_stages"] = pltpu.VMEM((4, SUM_SIZE, LANES), F32)
     scratch["sum_inboxes"] = pltpu.VMEM((3, SUM_SIZE, LANES), F32)
     scratch["sum_far"] = pltpu.VMEM((group - 1, SUM_SIZE // group, LANES), F32)
-    count = 8 * 6 + len(UNITS) * (5 + 2 * group) + 6 + 2 * group
+    count = 8 * 6 + len(UNITS) * (5 + 2 * group) + 8 + 2 * group
     scratch["send_sems"] = pltpu.SemaphoreType.DMA((count,))
     scratch["recv_sems"] = pltpu.SemaphoreType.DMA((count,))
     outs = dict(
@@ -1251,11 +1350,11 @@
     for name in GRADS:
         outs["r_" + name] = jax.ShapeDtypeStruct((depth[name], LANES), BF16)
     names = INPUTS + OUTPUTS + tuple(scratch)
-    in_vmem = 5 + len(VECTORS)
+    in_vmem = 3 + len(VECTORS)
     return pl.pallas_call(
         functools.partial(whole_kernel, names, group, {}),
         out_shape=[outs[name] for name in OUTPUTS],
-        in_specs=[SMEM_SPEC] * 2 + [VMEM_SPEC] * in_vmem + [HBM_SPEC] * len(WEIGHTS),
+        in_specs=[SMEM_SPEC] * 2 + [VMEM_SPEC] * in_vmem + [HBM_SPEC] * (2 + len(WEIGHTS)),
         out_specs=[HBM_SPEC] * 2 + [VMEM_SPEC] * (len(OUTPUTS) - 2),
         scratch_shapes=list(scratch.values()),
         compiler_params=pltpu.CompilerParams(
@@ -1291,7 +1390,7 @@
     )
     blocks = {name: vector.reshape(-1, LANES) for name, vector in vectors.items()}
     arrays = dict(
-        valid=window_valid, edge=window_edge, x=inputs, grad_out=grad_out, rel=rel_table.T,
+        valid=window_valid, edge=window_edge, h_x=inputs, h_grad_out=grad_out, rel=rel_table.T,
         qv=qv_bias, ub=up_bias.reshape(-1, LANES), own_wm=merge_weight,
         own_wqkv=jnp.transpose(query_key_value_weight, (1, 0, 2)), own_wp=proj_weight,
         own_wu=up_weight, own_wd=down_weight, **blocks,

time: 162 us -> 127 us (0.78)
  Pallas kernels: 161 us -> 126 us
    pallas_call x1, Pallas kernels: 154 us -> 119 us  [whole_call(): pl.pallas_call(functools.partial(whole_kernel, names, group, {}), out_sha...]
where the time goes in v4:
time: 127 us; the launch traced here: 126 us
  Pallas kernels  126 us (99%)
    pallas_call x1, Pallas kernels, whole_call(): pl.pallas_call(functools.partial(whole_kernel, names, group, {}), out_sha...  119 us
    pallas_call x1, Pallas kernels, finish_call(): pl.pallas_call(functools.partial(finish_kernel, names), out_shape=list(sh...  6.71 us

profile of v4, /device:TPU:0, one launch (start us, length us, event | category | flops | bytes accessed | tf_op | source)
XLA Modules:
  0.0 126.5 jit_solution(6281690634538003242)
XLA Ops:
  0.7 118.9 %shard_map.331 = (bf16[784,512]{1,0:T(8,128)(2,1)}, f32[784,1024]{1,0:T(8,128)}, bf16[2048,128]{1,0:T(8,128)(2,1)}, bf16[2048,128]{1,0:T(8,128)(2,1)}, bf16[512,...) custom-call(s32[64]{0:T(128)} %refs_0_.1, s32[64]{0:T(128)} %refs_1_.1, ...), custom_call_target="tpu_custom_call" | custom-call | tf_op jit(solution)/shard_map/pallas_call | solution.py:1354
  119.6 6.7 %shard_map.332 = (bf16[784,512]{1,0:T(8,128)(2,1)}, f32[784,1024]{1,0:T(8,128)}, f32[1024,128]{1,0:T(8,128)}, f32[3,512,128]{2,1,0:T(8,128)}, f32[128,512]{1,0:T...) custom-call(bf16[784,512]{1,0:T(8,128)(2,1)} %get-tuple-element.44.r, ...), custom_call_target="tpu_custom_call" | custom-call | tf_op jit(solution)/shard_map/pallas_call | solution.py:1368

commit v5 on v4

--- a/solution.py
+++ b/solution.py
@@ -355,6 +355,15 @@
         self.stats[at, index : index + 1] = mean
         self.stats[at, index + 1 : index + 2] = inv
 
+    def tiles(self):
+        return [lax.axis_index("tp") ^ bits for bits in (3, 2, 1, 0)]
+
+    def begin(self):
+        for copy in self.arriving:
+            copy.wait()
+        self.early[...] = jnp.zeros_like(self.early)
+        self.spread_vectors()
+
     def spread_vectors(self):
         for row, ref in enumerate(self.vectors):
             values = ref[...].astype(F32)
@@ -587,25 +596,30 @@
 
     def put_sum(self, row, values, summed=False):
         values = values[0:1] if summed else sum_rows(values)
+        place, ref = SUM_ROWS[row], self.late
+        if place >= LATE_ROWS:
+            place, ref = place - LATE_ROWS, self.early
         for block in range(values.shape[1] // LANES):
-            place = SUM_ROWS[row] + block
-            self.sums[place : place + 1, :] = values[:, block * LANES : (block + 1) * LANES]
+            lanes = slice(block * LANES, (block + 1) * LANES)
+            ref[place + block : place + block + 1, :] = values[:, lanes]
 
     def put_up_sum(self, index, total):
         values = sum_rows(total)
         blocks = self.tile // LANES
         for block in range(blocks):
-            place = SUM_ROWS[10] + index * blocks + block
-            self.sums[pl.ds(place, 1), :] = values[:, block * LANES : (block + 1) * LANES]
+            place = SUM_ROWS[10] - LATE_ROWS + index * blocks + block
+            self.early[pl.ds(place, 1), :] = values[:, block * LANES : (block + 1) * LANES]
 
     def put_table(self, values):
         for half in range(2):
-            place = SUM_ROWS[11] + half * self.heads
-            self.sums[place : place + self.heads, :] = values[:, half * LANES : (half + 1) * LANES]
+            place = SUM_ROWS[11] - LATE_ROWS + half * self.heads
+            lanes = slice(half * LANES, (half + 1) * LANES)
+            self.early[place : place + self.heads, :] = values[:, lanes]
 
 
 SUM_ROWS = (0, 8, 16, 20, 24, 28, 32, 36, 40, 44, 48, 64)
-SUM_SIZE = 128
+LATE_ROWS = 16
+SUM_SIZE = 96
 
 
 def put_blocks(ref, shard, values):
@@ -653,19 +667,22 @@
 
 
 class Links:
-    def __init__(self, send_sems, recv_sems, plan):
-        self.send_sems, self.recv_sems, self.plan = send_sems, recv_sems, plan
-        self.sent = []
+    def __init__(self, send_sems, recv_sems):
+        self.send_sems, self.recv_sems = send_sems, recv_sems
+        self.slots, self.sent = {}, []
         self.sp, self.tp = lax.axis_index("sp"), lax.axis_index("tp")
 
+    def slot(self, label):
+        return self.slots.setdefault(label, len(self.slots))
+
     def place(self, way):
-        kind, distance = way
-        if kind == "tp":
+        over_tp, distance = way
+        if over_tp:
             return self.sp, self.tp ^ distance
         return self.sp ^ distance, self.tp
 
-    def copy(self, name, way, source, target):
-        slot = self.plan.setdefault(name, len(self.plan))
+    def copy(self, label, way, source, target):
+        slot = self.slot(label)
         return pltpu.make_async_remote_copy(
             src_ref=source,
             dst_ref=target,
@@ -675,17 +692,16 @@
             device_id_type=MESH_ID,
         )
 
-    def send(self, name, way, source, target):
-        copy = self.copy(name, way, source, target)
+    def send(self, label, way, source, target):
+        copy = self.copy(label, way, source, target)
         copy.start()
         self.sent.append(copy)
 
-    def receive(self, name, way, target):
-        self.copy(name, way, target, target).wait_recv()
-
-    def keep(self, name, source, target):
-        slot = self.plan.setdefault(name, len(self.plan))
-        copy = pltpu.make_async_copy(source, target, self.recv_sems.at[slot])
+    def receive(self, label, way, target):
+        self.copy(label, way, target, target).wait_recv()
+
+    def keep(self, label, source, target):
+        copy = pltpu.make_async_copy(source, target, self.recv_sems.at[self.slot(label)])
         copy.start()
         return copy
 
@@ -702,82 +718,76 @@
             copy.wait_send()
 
 
-CORE, ACROSS, BESIDE = ("tp", 1), ("tp", 2), ("sp", 1)
-
-
-def far_ways(sp_size):
-    return [("sp", 2 * step) for step in range(1, sp_size // 2)]
+CORE, ACROSS, BESIDE = (True, 1), (True, 2), (False, 1)
+
+
+def far(step):
+    return False, 2 * step
 
 
 class Gather:
-    def __init__(self, links, name, own, whole, view, split):
-        self.links, self.name, self.own, self.whole = links, name, own, whole
+    def __init__(self, links, label, own, whole, view, split=True):
+        self.links, self.name, self.own, self.whole = links, label, own, whole
         self.view, self.split = view, split
-        self.half = links.sp & 1
+        self.half = links.sp & 1 if split else None
 
     def part(self, shard, half=None):
         return self.view(self.whole, shard, half)
 
     def label(self, step):
-        return (self.name, step)
+        return self.name, step
 
     def start(self):
         links = self.links
         mine = links.tp
-        self.local = links.keep(self.label("own"), self.own, self.part(mine))
-        half = self.half if self.split else None
+        source = self.view(self.own, None, None)
+        self.local = links.keep(self.label(0), source, self.part(mine))
         links.send(
-            self.label("x"), ACROSS, self.view(self.own, None, half), self.part(mine, half)
+            self.label(1), ACROSS, self.view(self.own, None, self.half),
+            self.part(mine, self.half),
         )
-        links.send(self.label("c"), CORE, self.own, self.part(mine))
+        links.send(self.label(2), CORE, source, self.part(mine))
 
     def forward(self):
         links = self.links
-        other = links.tp ^ 2
-        half = self.half if self.split else None
-        block = self.part(other, half)
-        links.receive(self.label("x"), ACROSS, block)
+        block = self.part(links.tp ^ 2, self.half)
+        links.receive(self.label(1), ACROSS, block)
         if self.split:
-            links.send(self.label("y"), BESIDE, block, block)
-        links.send(self.label("xc"), CORE, block, block)
-
-    def forward_beside(self):
-        if self.split:
-            links = self.links
-            block = self.part(links.tp ^ 2, 1 - self.half)
-            links.receive(self.label("y"), BESIDE, block)
-            links.send(self.label("yc"), CORE, block, block)
+            links.send(self.label(3), BESIDE, block, block)
+        links.send(self.label(4), CORE, block, block)
+
+    def beside(self):
+        links = self.links
+        block = self.part(links.tp ^ 2, 1 - self.half)
+        links.receive(self.label(3), BESIDE, block)
+        links.send(self.label(5), CORE, block, block)
 
     def finish(self):
         links = self.links
         self.local.wait()
-        links.receive(self.label("c"), CORE, self.part(links.tp ^ 1))
-        half = self.half if self.split else None
-        links.receive(self.label("xc"), CORE, self.part(links.tp ^ 3, half))
+        links.receive(self.label(2), CORE, self.part(links.tp ^ 1))
+        links.receive(self.label(4), CORE, self.part(links.tp ^ 3, self.half))
         if self.split:
-            links.receive(self.label("yc"), CORE, self.part(links.tp ^ 3, 1 - self.half))
-
-
-def column_view(size, halves):
+            links.receive(self.label(5), CORE, self.part(links.tp ^ 3, 1 - self.half))
+
+
+def column_view(size, first, rows):
     def view(ref, shard, half):
-        rank = len(ref.shape)
-        rows = ref.shape[rank - 2]
-        at = slice(None) if half is None else pl.ds(
-            pl.multiple_of(half * (rows // 2), 16), rows // 2
-        )
-        lanes = slice(None) if shard is None else pl.ds(pl.multiple_of(shard * size, LANES), size)
-        return ref.at[(slice(None),) * (rank - 2) + (at, lanes)]
+        start, count = (first, rows) if half is None else (first + half * (rows // 2), rows // 2)
+        at = pl.ds(start if half is None else pl.multiple_of(start, 16), count)
+        if shard is None:
+            return ref.at[at, :]
+        return ref.at[at, pl.ds(pl.multiple_of(shard * size, LANES), size)]
 
     return view
 
 
-def row_view(size):
+def row_view(size, first, rows):
     def view(ref, shard, half):
-        start = 0 if shard is None else shard * size
+        start = first if shard is None else shard * size + first
         if half is None:
-            return ref.at[pl.ds(start, size), :]
-        start = start + half * (size // 2)
-        return ref.at[pl.ds(pl.multiple_of(start, 16), size // 2), :]
+            return ref.at[pl.ds(start if shard is None else pl.multiple_of(start, 16), rows), :]
+        return ref.at[pl.ds(pl.multiple_of(start + half * (rows // 2), 16), rows // 2), :]
 
     return view
 
@@ -805,9 +815,9 @@
 
 
 class Reduce:
-    def __init__(self, links, name, grads, core_in, first_in, second_in, far_in, result, group,
+    def __init__(self, links, label, grads, core_in, first_in, second_in, far_in, result, group,
                  across_first):
-        self.links, self.name, self.grads = links, name, grads
+        self.links, self.name, self.grads = links, label, grads
         self.core_in, self.first_in, self.second_in = core_in, first_in, second_in
         self.far_in, self.result, self.group = far_in, result, group
         self.rows = grads.shape[1]
@@ -817,16 +827,11 @@
         self.seat = links.sp >> 1
         self.across = links.tp >> 1
         if across_first:
-            middle = self.core_add_across, self.across_beside, self.beside_last
+            self.add, self.first = self.core_add_across, self.across_beside
+            self.second = self.beside_last
         else:
-            middle = self.core_add_beside, self.beside_across, self.across_last
-        self.steps = dict(
-            far=self.core_far, near=self.core_near, add=middle[0], first=middle[1],
-            second=middle[2], spread=self.far_add, back=self.far_done, last=self.beside_done,
-        )
-
-    def run(self, step):
-        self.steps.pop(step)()
+            self.add, self.first = self.core_add_beside, self.beside_across
+            self.second = self.across_last
 
     def label(self, *step):
         return (self.name,) + step
@@ -837,44 +842,44 @@
         start = half * self.half_rows + piece * self.piece
         return ref.at[pl.ds(pl.multiple_of(start, 16), self.piece), :]
 
-    def core_send(self, across, name):
+    def core_send(self, across, step):
         shard = (self.links.tp & 1) ^ 1 | 2 * across
         self.links.send(
-            self.label(name), CORE, self.grads.at[shard], self.core_in.at[across]
+            self.label(step), CORE, self.grads.at[shard], self.core_in.at[across]
         )
 
-    def core_far(self):
-        self.core_send(self.across ^ 1, "cf")
-
-    def core_near(self):
-        self.core_send(self.across, "cn")
+    def far(self):
+        self.core_send(self.across ^ 1, 0)
+
+    def near(self):
+        self.core_send(self.across, 1)
 
     def receive_far(self):
-        self.links.receive(self.label("cf"), CORE, self.core_in.at[self.across ^ 1])
+        self.links.receive(self.label(0), CORE, self.core_in.at[self.across ^ 1])
 
     def receive_near(self):
-        self.links.receive(self.label("cn"), CORE, self.core_in.at[self.across])
+        self.links.receive(self.label(1), CORE, self.core_in.at[self.across])
 
     def core_add_across(self):
         self.receive_far()
         other = self.links.tp ^ 2
         block = self.grads.at[other]
         add_rows(block, 0, self.rows, [(block, 0), (self.core_in.at[self.across ^ 1], 0)])
-        self.links.send(self.label("x"), ACROSS, block, self.first_in)
+        self.links.send(self.label(2), ACROSS, block, self.first_in)
 
     def across_beside(self):
         links = self.links
         self.receive_near()
-        links.receive(self.label("x"), ACROSS, self.first_in)
+        links.receive(self.label(2), ACROSS, self.first_in)
         block = self.grads.at[links.tp]
         terms = [(block, 0), (self.core_in.at[self.across], 0), (self.first_in, 0)]
         add_rows(block, 0, self.rows, terms)
         links.send(
-            self.label("y"), BESIDE, self.rows_of(block, 1 - self.half), self.second_in
+            self.label(3), BESIDE, self.rows_of(block, 1 - self.half), self.second_in
         )
 
     def beside_last(self):
-        self.links.receive(self.label("y"), BESIDE, self.second_in)
+        self.links.receive(self.label(3), BESIDE, self.second_in)
         self.add_and_spread([(self.second_in, 0)])
 
     def core_add_beside(self):
@@ -885,22 +890,22 @@
             block = self.grads.at[(links.tp & 1) | 2 * across]
             add_rows(block, 0, self.rows, [(block, 0), (self.core_in.at[across], 0)])
             links.send(
-                self.label("y", across), BESIDE, self.rows_of(block, 1 - self.half),
+                self.label(3, across), BESIDE, self.rows_of(block, 1 - self.half),
                 self.first_in.at[across],
             )
 
     def beside_across(self):
         links = self.links
         for across in range(2):
-            links.receive(self.label("y", across), BESIDE, self.first_in.at[across])
+            links.receive(self.label(3, across), BESIDE, self.first_in.at[across])
         block = self.grads.at[links.tp ^ 2]
         mine = self.half * self.half_rows
         terms = [(block, mine), (self.first_in.at[self.across ^ 1], 0)]
         add_rows(block, mine, self.half_rows, terms)
-        links.send(self.label("x"), ACROSS, self.rows_of(block, self.half), self.second_in)
+        links.send(self.label(2), ACROSS, self.rows_of(block, self.half), self.second_in)
 
     def across_last(self):
-        self.links.receive(self.label("x"), ACROSS, self.second_in)
+        self.links.receive(self.label(2), ACROSS, self.second_in)
         self.add_and_spread([(self.first_in.at[self.across], 0), (self.second_in, 0)])
 
     def add_and_spread(self, terms):
@@ -909,474 +914,503 @@
         add_rows(block, mine, self.half_rows, [(block, mine)] + terms)
         for step in range(1, self.group):
             self.links.send(
-                self.label("z", step), ("sp", 2 * step),
+                self.label(4, step), far(step),
                 self.rows_of(block, self.half, self.seat ^ step), self.far_in.at[step - 1],
             )
 
-    def far_add(self):
+    def spread(self):
         links = self.links
         block = self.grads.at[links.tp]
         mine = self.half * self.half_rows + self.seat * self.piece
         terms = [(block, mine)]
         for step in range(1, self.group):
-            links.receive(self.label("z", step), ("sp", 2 * step), self.far_in.at[step - 1])
+            links.receive(self.label(4, step), far(step), self.far_in.at[step - 1])
             terms.append((self.far_in.at[step - 1], 0))
         add_rows(self.result, mine, self.piece, terms)
         done = self.rows_of(self.result, self.half, self.seat)
         for step in range(1, self.group):
-            links.send(self.label("a", step), ("sp", 2 * step), done, done)
-
-    def far_done(self):
+            links.send(self.label(5, step), far(step), done, done)
+
+    def back(self):
         links = self.links
         for step in range(1, self.group):
             links.receive(
-                self.label("a", step), ("sp", 2 * step),
+                self.label(5, step), far(step),
                 self.rows_of(self.result, self.half, self.seat ^ step),
             )
         done = self.rows_of(self.result, self.half)
-        links.send(self.label("b"), BESIDE, done, done)
-
-    def beside_done(self):
+        links.send(self.label(6), BESIDE, done, done)
+
+    def last(self):
         self.links.receive(
-            self.label("b"), BESIDE, self.rows_of(self.result, 1 - self.half)
+            self.label(6), BESIDE, self.rows_of(self.result, 1 - self.half)
         )
 
 
 class Total:
-    def __init__(self, links, name, stages, inboxes, far_in, result, group):
-        self.links, self.name, self.stages, self.inboxes = links, name, stages, inboxes
-        self.far_in, self.result, self.group = far_in, result, group
-        self.piece = result.shape[0] // group
+    def __init__(self, links, label, stages, inboxes, seats, result):
+        self.links, self.name, self.stages, self.inboxes = links, label, stages, inboxes
+        self.seats, self.result = seats, result
+        self.group = seats.shape[0]
         self.seat = links.sp >> 1
-        self.ways = (CORE, ACROSS, BESIDE)
-        self.steps = [
-            functools.partial(self.exchange, 0), functools.partial(self.add, 0),
-            functools.partial(self.add, 1), functools.partial(self.add, 2), self.far_add,
-            self.far_done,
-        ]
-
-    def run(self):
-        self.steps.pop(0)()
-
-    def label(self, *step):
-        return (self.name,) + step
-
-    def at(self, ref, piece):
-        return ref.at[pl.ds(pl.multiple_of(piece * self.piece, 8), self.piece), :]
-
-    def exchange(self, stage):
-        self.links.send(
-            self.label("e", stage), self.ways[stage], self.stages.at[stage],
-            self.inboxes.at[stage],
-        )
-
-    def add(self, stage):
-        self.links.receive(self.label("e", stage), self.ways[stage], self.inboxes.at[stage])
-        self.stages[stage + 1] = self.stages[stage] + self.inboxes[stage]
-        if stage < 2:
-            self.exchange(stage + 1)
-            return
+
+    def exchange(self, stage, way):
+        self.links.send((self.name, stage), way, self.stages.at[stage], self.inboxes.at[stage])
+
+    def take(self, stage, way):
+        self.links.receive((self.name, stage), way, self.inboxes.at[stage])
+        return self.stages[stage] + self.inboxes[stage]
+
+    def send(self):
+        self.exchange(0, CORE)
+
+    def core(self):
+        self.stages[1] = self.take(0, CORE)
+        self.exchange(1, ACROSS)
+
+    def across(self):
+        self.stages[2] = self.take(1, ACROSS)
+        self.exchange(2, BESIDE)
+
+    def beside(self):
+        mine = self.seats.at[self.seat]
+        mine[...] = self.take(2, BESIDE)
         for step in range(1, self.group):
-            self.links.send(
-                self.label("z", step), ("sp", 2 * step),
-                self.at(self.stages.at[3], self.seat ^ step), self.far_in.at[step - 1],
-            )
-
-    def far_add(self):
-        total = self.at(self.stages.at[3], self.seat)[...]
+            self.links.send((self.name, 3, step), far(step), mine, mine)
+
+    def last(self):
         for step in range(1, self.group):
-            self.links.receive(self.label("z", step), ("sp", 2 * step), self.far_in.at[step - 1])
-            total = total + self.far_in[step - 1]
-        done = self.at(self.result, self.seat)
-        done[...] = total
-        for step in range(1, self.group):
-            self.links.send(self.label("a", step), ("sp", 2 * step), done, done)
-
-    def far_done(self):
-        for step in range(1, self.group):
-            self.links.receive(
-                self.label("a", step), ("sp", 2 * step), self.at(self.result, self.seat ^ step)
-            )
-
-
-UNITS = (
-    ("gd", 0, 1024, True), ("gd", 1024, 1024, True),
-    ("gu", 0, 1024, True), ("gu", 1024, 1024, True),
-    ("gp", 0, 512, True),
-    ("gqkv", 0, 1024, True), ("gqkv", 1024, 512, False),
-    ("gm", 0, 512, True), ("gm", 512, 512, False),
+            self.links.receive((self.name, 3, step), far(step), self.seats.at[self.seat ^ step])
+        total = self.seats[0]
+        for seat in range(1, self.group):
+            total = total + self.seats[seat]
+        self.result[...] = total
+
+
+def schedule(local, g, u, done):
+    windows = local.windows
+    tiles = local.tiles()
+
+    def attend_back(first, last):
+        local.attend_back(windows - last * windows // 8, windows - first * windows // 8)
+
+    local.begin()
+    local.merge_norm()
+    g.pack.forward()
+    local.prepare()
+    g.wm0.forward()
+    local.grad_rows()
+    g.wm1.forward()
+    g.pack.finish()
+    local.table_bias()
+    g.wq.forward()
+    g.wm0.beside()
+    g.wk.forward()
+    g.wm0.finish()
+    g.wm1.beside()
+    g.wv.forward()
+    g.wm1.finish()
+    local.merge()
+    g.wq.beside()
+    local.attn_norm()
+    g.wk.beside()
+    g.wv.beside()
+    g.wu0.forward()
+    g.wq.finish()
+    local.project(0)
+    g.wu1.forward()
+    g.wk.finish()
+    local.project(1)
+    g.wv.finish()
+    local.project(2)
+    local.attend(0, windows // 4)
+    g.wp.forward()
+    local.attend(windows // 4, windows // 2)
+    g.wu0.beside()
+    g.wd0.forward()
+    local.attend(windows // 2, 3 * windows // 4)
+    local.attend(3 * windows // 4, windows)
+    g.wu1.beside()
+    g.wp.beside()
+    g.wd1.forward()
+    g.wp.finish()
+    local.attn_out()
+    local.mlp_norm()
+    g.wd0.beside()
+    g.wu0.finish()
+    g.wu1.finish()
+    local.up(tiles[0])
+    g.wd1.beside()
+    u.gd0.far()
+    u.gd1.far()
+    local.up(tiles[1])
+    u.gd0.add()
+    local.up(tiles[2])
+    u.gd0.near()
+    u.gd1.near()
+    local.up(tiles[3])
+    g.wd0.finish()
+    g.wd1.finish()
+    local.hidden_back(tiles[0])
+    u.gd1.add()
+    u.gu0.far()
+    u.gu1.far()
+    local.hidden_back(tiles[1])
+    u.gu0.add()
+    u.gd0.first()
+    u.gu1.add()
+    local.hidden_back(tiles[2])
+    u.gu0.near()
+    u.gu1.near()
+    local.hidden_back(tiles[3])
+    local.up_back()
+    u.gd1.first()
+    local.mlp_back()
+    u.gu0.first()
+    local.proj_back()
+    u.gd0.second()
+    u.gp0.far()
+    u.gp0.near()
+    attend_back(0, 2)
+    u.gp0.add()
+    attend_back(2, 4)
+    u.gu1.first()
+    u.gu0.second()
+    attend_back(4, 6)
+    u.gd0.spread()
+    u.gd1.second()
+    u.gp0.first()
+    attend_back(6, 8)
+    local.qkv_weight_back()
+    u.gp0.second()
+    u.gu1.second()
+    u.gu0.spread()
+    u.qkv0.far()
+    u.qkv0.near()
+    u.qkv1.far()
+    u.qkv1.near()
+    u.qkv2.far()
+    u.qkv2.near()
+    local.qkv_back()
+    u.qkv1.add()
+    u.gd0.back()
+    u.qkv0.add()
+    u.qkv2.add()
+    local.attn_back()
+    u.gd1.spread()
+    local.merge_weight_back()
+    u.gp0.spread()
+    u.gm0.far()
+    u.gm0.near()
+    u.gm1.far()
+    u.gm1.near()
+    local.merge_in_back()
+    u.qkv0.first()
+    u.gm0.add()
+    u.qkv1.first()
+    u.gm1.add()
+    u.gu1.spread()
+    part = local.rows // 16 // 7
+    totals = local.merge_back(0, 2 * part)
+    totals = local.merge_back(2 * part, 5 * part, totals)
+    u.qkv2.first()
+    u.gu0.back()
+    u.qkv0.second()
+    local.bias_back()
+    u.early.send()
+    u.gm0.first()
+    local.merge_back(5 * part, 7 * part, totals)
+    done.d_in()
+    u.late.send()
+    u.gm1.first()
+    u.early.core()
+    u.gd1.back()
+    u.qkv1.second()
+    local.down()
+    u.gp0.back()
+    u.qkv2.second()
+    u.late.core()
+    local.finish()
+    done.out()
+    u.gu1.back()
+    u.gm1.second()
+    u.early.across()
+    u.qkv0.spread()
+    u.gm0.second()
+    u.late.across()
+    u.qkv1.spread()
+    u.qkv2.spread()
+    u.gm1.spread()
+    u.qkv0.back()
+    u.gm0.spread()
+    u.early.beside()
+    u.late.beside()
+    u.qkv1.back()
+    u.qkv2.back()
+    u.gm1.back()
+    u.gm0.back()
+    u.gd0.last()
+    u.gu0.last()
+    u.gd1.last()
+    u.gp0.last()
+    u.gu1.last()
+    u.qkv0.last()
+    u.qkv1.last()
+    u.qkv2.last()
+    u.gm1.last()
+    u.early.last()
+    u.gm0.last()
+    u.late.last()
+
+
+SHARDS = 4
+PIECES = 7
+
+
+class Refs:
+    def __init__(self, names, refs):
+        self.__dict__.update(zip(names, refs, strict=True))
+
+
+UNITS = dict(
+    gd0=(0, 1024, True),
+    gd1=(1024, 1024, False),
+    gu0=(0, 1024, True),
+    gu1=(1024, 1024, True),
+    gp0=(0, 512, False),
+    qkv0=(0, 512, True),
+    qkv1=(512, 512, False),
+    qkv2=(1024, 512, True),
+    gm0=(0, 512, True),
+    gm1=(512, 512, False),
 )
-GRADS = ("gd", "gu", "gp", "gqkv", "gm")
-WEIGHTS = ("wm", "wqkv", "wp", "wu", "wd")
-VECTORS = (
-    "merge_gain", "merge_bias", "attn_gain", "attn_bias", "mlp_gain", "mlp_bias", "proj_bias",
-    "down_bias",
-)
-INPUTS = (
-    ("valid", "edge", "rel", "qv", "ub") + VECTORS + ("h_x", "h_grad_out")
-    + tuple("own_" + name for name in WEIGHTS)
-)
-OUTPUTS = ("h_out", "h_d_in") + tuple("r_" + name for name in GRADS) + ("r_sums",)
-
-
-def unit_name(name, first):
-    return name + str(first)
-
-
-def whole_kernel(names, group, plan, *refs):
-    refs = dict(zip(names, refs, strict=True))
-    links = Links(refs.pop("send_sems"), refs.pop("recv_sems"), plan)
-    arriving = [
-        links.keep(name, refs.pop("h_" + name), refs[name]) for name in ("x", "grad_out")
-    ]
-    rows = refs["x"].shape[0]
-    own_pack, packs = refs.pop("pack"), refs.pop("packs")
-    rel, qv, ub = refs.pop("rel"), refs.pop("qv"), refs.pop("ub")
-    heads_here = rel.shape[0]
-    own_pack[...] = jnp.zeros_like(own_pack)
-    own_pack[0:heads_here, 0:REL] = rel[...].astype(F32)
-    own_pack[4:6, 0:LANES] = qv[...].astype(F32)
+
+
+def fill_pack(pack, rel, qv, ub):
+    pack[...] = jnp.zeros_like(pack)
+    pack[0 : rel.shape[0], 0:REL] = rel[...].astype(F32)
+    pack[4:6, 0:LANES] = qv[...].astype(F32)
     for block in range(ub.shape[0]):
         lanes = slice(block * LANES, (block + 1) * LANES)
-        own_pack[6:7, lanes] = ub[block : block + 1, :].astype(F32)
-
-    own = {name: refs.pop("own_" + name) for name in WEIGHTS}
-    whole = {name: refs[name] for name in WEIGHTS}
-    for part, name in enumerate(("wq", "wk", "wv")):
-        own[name], whole[name] = own["wqkv"].at[part], whole["wqkv"].at[part]
-    columns = column_view(LANES, True)
-    views = dict(
-        wm=columns, wq=columns, wk=columns, wv=columns, wp=row_view(own["wp"].shape[0]),
-        wu=column_view(own["wu"].shape[1], True), wd=row_view(own["wd"].shape[0]),
+        pack[6:7, lanes] = ub[block : block + 1, :].astype(F32)
+
+
+def gathers_of(links, r):
+    wide, here = r.own_wm.shape
+    width, tile = r.own_wu.shape
+    columns = functools.partial(column_view, here)
+    up = functools.partial(column_view, tile)
+    down = functools.partial(row_view, tile)
+    parts = dict(
+        pack=(r.pack, r.packs, lead_view, False),
+        wm0=(r.own_wm, r.wm, columns(0, wide // 2)),
+        wm1=(r.own_wm, r.wm, columns(wide // 2, wide // 2)),
+        wq=(r.own_wqkv.at[0], r.wqkv.at[0], columns(0, width)),
+        wk=(r.own_wqkv.at[1], r.wqkv.at[1], columns(0, width)),
+        wv=(r.own_wqkv.at[2], r.wqkv.at[2], columns(0, width)),
+        wu0=(r.own_wu, r.wu, up(0, width // 2)),
+        wu1=(r.own_wu, r.wu, up(width // 2, width // 2)),
+        wp=(r.own_wp, r.wp, row_view(here, 0, here)),
+        wd0=(r.own_wd, r.wd, down(0, tile // 2)),
+        wd1=(r.own_wd, r.wd, down(tile // 2, tile // 2)),
     )
-    gathers = {"pack": Gather(links, "pack", own_pack, packs, lead_view, False)}
-    for name in ("wm", "wq", "wk", "wv", "wp", "wu", "wd"):
-        gathers[name] = Gather(links, name, own[name], whole[name], views[name], name != "wm")
-    links.greet([CORE, ACROSS, BESIDE] + far_ways(2 * group))
-    for gather in gathers.values():
+    made = [Gather(links, label, *part) for label, part in enumerate(parts.values())]
+    return Refs(parts, made)
+
+
+def reduces_of(links, r, boxes, first_label):
+    grads = (r.gd, r.gd, r.gu, r.gu, r.gp, r.gqkv, r.gqkv, r.gqkv, r.gm, r.gm)
+    results = (r.rd, r.rd, r.ru, r.ru, r.rp, r.rqkv, r.rqkv, r.rqkv, r.rm, r.rm)
+    made = []
+    for index, (first, size, across_first) in enumerate(UNITS.values()):
+        at = pl.ds(first, size)
+        group = boxes[index][3].shape[0] + 1
+        made.append(
+            Reduce(
+                links, first_label + index, grads[index].at[:, at, :], *boxes[index],
+                results[index].at[at, :], group, across_first,
+            )
+        )
+    return Refs(UNITS, made)
+
+
+def whole_kernel(names, group, *refs):
+    boxes = refs[len(names) :]
+    r = Refs(names, refs[: len(names)])
+    links = Links(r.send_sems, r.recv_sems)
+    arriving = [links.keep((-1, 0), r.h_x, r.x), links.keep((-1, 1), r.h_grad_out, r.grad_out)]
+    fill_pack(r.pack, r.rel, r.qv, r.ub)
+    links.greet([CORE, ACROSS, BESIDE] + [far(step) for step in range(1, group)])
+    g = gathers_of(links, r)
+    for gather in vars(g).values():
         gather.start()
-
-    results = {name: refs.pop("r_" + name) for name in GRADS}
-    reduces = {}
-    for name, first, size, across_first in UNITS:
-        unit = unit_name(name, first)
-        part = pl.ds(first, size)
-        reduces[unit] = Reduce(
-            links, unit, refs[name].at[:, part, :], refs.pop("c_" + unit),
-            refs.pop("f_" + unit), refs.pop("s_" + unit), refs.pop("z_" + unit),
-            results[name].at[part, :], group, across_first,
-        )
-    stages, inboxes = refs.pop("sum_stages"), refs.pop("sum_inboxes")
-    refs["sums"] = stages.at[0]
-    total = Total(links, "sums", stages, inboxes, refs.pop("sum_far"), refs.pop("r_sums"), group)
-    shards = packs.shape[0]
+    u = reduces_of(links, r, [boxes[4 * unit : 4 * unit + 4] for unit in range(len(UNITS))], 100)
+    late, early = pl.ds(0, LATE_ROWS), pl.ds(LATE_ROWS, SUM_SIZE - LATE_ROWS)
+    u.late = Total(links, 200, r.late_stages, r.late_in, r.late_seats, r.sums.at[late, :])
+    u.early = Total(links, 201, r.early_stages, r.early_in, r.early_seats, r.sums.at[early, :])
+    here = r.rel.shape[0]
 
     def table():
-        return jnp.concatenate(
-            [packs[shard, 0:heads_here, : 2 * LANES] for shard in range(shards)], axis=0
-        )
+        parts = [r.packs[shard, 0:here, : 2 * LANES] for shard in range(SHARDS)]
+        return jnp.concatenate(parts, axis=0)
 
     def qkv_bias(part):
         row = 4 if part == 0 else 5
-        return jnp.concatenate(
-            [packs[shard, row : row + 1, :LANES] for shard in range(shards)], axis=1
-        )
+        parts = [r.packs[shard, row : row + 1, :LANES] for shard in range(SHARDS)]
+        return jnp.concatenate(parts, axis=1)
 
     def up_bias(index):
-        return packs[index, 6:7, :]
-
-    refs["vectors"] = [refs.pop(name) for name in VECTORS]
-    refs.update(table=table, qkv_bias=qkv_bias, up_bias=up_bias)
-    h_out, h_d_in = refs.pop("h_out"), refs.pop("h_d_in")
-    local = Local(refs, links.tp * (rows // TOK))
-
-    def forward(*names):
-        for name in names:
-            gathers[name].forward()
-
-    def beside(*names):
-        for name in names:
-            gathers[name].forward_beside()
-
-    def ready(*names):
-        for name in names:
-            gathers[name].finish()
-
-    def run(step, *units):
-        for unit in units:
-            reduces[unit].run(step)
-
-    gd0, gd1, gu0, gu1, gp0 = "gd0", "gd1024", "gu0", "gu1024", "gp0"
-    qkv0, qkv1, gm0, gm1 = "gqkv0", "gqkv1024", "gm0", "gm512"
-    windows = local.windows
-
-    for copy in arriving:
-        copy.wait()
-    stages[0] = jnp.zeros_like(stages[0])
-    local.spread_vectors()
-    local.merge_norm()
-    local.prepare()
-    forward("pack")
-    local.grad_rows()
-    ready("pack")
-    local.table_bias()
-    forward("wm")
-    ready("wm")
-    local.merge()
-    forward("wq")
-    local.attn_norm()
-    forward("wk", "wv")
-    beside("wq")
-    ready("wq")
-    local.project(0)
-    beside("wk")
-    ready("wk")
-    local.project(1)
-    beside("wv")
-    ready("wv")
-    local.project(2)
-    forward("wp")
-    local.attend(0, windows // 4)
-    beside("wp")
-    forward("wu")
-    local.attend(windows // 4, windows // 2)
-    ready("wp")
-    local.attend(windows // 2, windows)
-    forward("wd")
-    local.attn_out()
-    beside("wu")
-    local.mlp_norm()
-    ready("wu")
-
-    tiles = [links.tp ^ bits for bits in (3, 2, 1, 0)]
-    local.up(tiles[0])
-    run("far", gd0, gd1)
-    beside("wd")
-    local.up(tiles[1])
-    run("add", gd0, gd1)
-    local.up(tiles[2])
-    run("near", gd0, gd1)
-    local.up(tiles[3])
-    ready("wd")
-    local.hidden_back(tiles[0])
-    run("far", gu0, gu1)
-    local.hidden_back(tiles[1])
-    run("add", gu0, gu1)
-    local.hidden_back(tiles[2])
-    run("near", gu0, gu1)
-    run("first", gd0)
-    local.hidden_back(tiles[3])
-    local.up_back()
-    local.mlp_back()
-    run("second", gd0)
-    run("first", gd1)
-    local.proj_back()
-    run("far", gp0)
-    run("near", gp0)
-
-    def attend_back(index):
-        local.attend_back((3 - index) * windows // 4, (4 - index) * windows // 4)
-
-    attend_back(0)
-    run("add", gp0)
-    attend_back(1)
-    run("spread", gd0)
-    run("first", gu0)
-    run("second", gd1)
-    attend_back(2)
-    attend_back(3)
-    local.qkv_weight_back()
-    run("far", qkv0, qkv1)
-    run("near", qkv0, qkv1)
-    run("back", gd0)
-    run("spread", gd1)
-    run("second", gu0)
-    run("first", gu1)
-    local.qkv_back()
-    run("add", qkv0, qkv1)
-    run("first", gp0)
-    local.attn_back()
-    run("spread", gu0)
-    run("back", gd1)
-    run("second", gu1)
-    local.merge_weight_back()
-    run("far", gm0, gm1)
-    run("near", gm0, gm1)
-    run("second", gp0)
-    run("first", qkv1)
-    local.merge_in_back()
-    run("add", gm0, gm1)
-    run("back", gu0)
-    run("spread", gu1, gp0)
-    third = rows // 16 // 7
-    totals = local.merge_back(0, 3 * third)
-    run("first", qkv0)
-    run("second", qkv1)
-    local.merge_back(3 * third, 7 * third, totals)
-    done = [links.keep("d_in", local.d_in, h_d_in)]
-    run("back", gp0, gu1)
-    run("first", gm1, gm0)
-    local.bias_back()
-    total.run()
-    run("second", qkv0)
-    run("spread", qkv1)
-    local.down()
-    total.run()
-    run("second", gm1, gm0)
-    local.finish()
-    done.append(links.keep("out", local.out, h_out))
-    total.run()
-    run("spread", qkv0)
-    run("back", qkv1)
-    run("spread", gm1, gm0)
-    total.run()
-    run("last", gd0, gd1, gu0, gu1, gp0)
-    run("back", qkv0)
-    total.run()
-    run("back", gm1, gm0)
-    total.run()
-    run("last", qkv0, qkv1, gm0, gm1)
-    assert not any(reduce.steps for reduce in reduces.values())
-    for copy in done:
+        return r.packs[index, 6:7, :]
+
+    vectors = (
+        r.merge_gain, r.merge_bias, r.attn_gain, r.attn_bias, r.mlp_gain, r.mlp_bias, r.proj_bias,
+        r.down_bias,
+    )
+    fields = dict(
+        vars(r), table=table, qkv_bias=qkv_bias, up_bias=up_bias, vectors=vectors,
+        arriving=arriving, early=r.early_stages.at[0], late=r.late_stages.at[0],
+    )
+    local = Local(fields, links.tp * (r.x.shape[0] // TOK))
+    leaving = []
+
+    def put_d_in():
+        leaving.append(links.keep((-1, 2), r.d_in, r.h_d_in))
+
+    def put_out():
+        leaving.append(links.keep((-1, 3), r.out, r.h_out))
+
+    schedule(local, g, u, Refs(dict(d_in=0, out=0), (put_d_in, put_out)))
+    for copy in leaving:
         copy.wait()
     links.drain()
 
 
+def wide_rows(result, out):
+    rows = out.shape[0]
+    for block in range(out.shape[1] // LANES):
+        lanes = slice(block * LANES, (block + 1) * LANES)
+        out[:, lanes] = result[block * rows : (block + 1) * rows, :].astype(F32)
+
+
 def finish_kernel(names, *refs):
-    refs = dict(zip(names, refs, strict=True))
+    r = Refs(names, refs)
     tp = lax.axis_index("tp")
-    pieces, number = [], 0
-    for name in ("d_in", "out"):
-        source, target, held = refs["h_" + name], refs["o_" + name], refs["v_" + name]
+    pieces = []
+    for source, target, held in ((r.h_d_in, r.o_d_in, r.v_d_in), (r.h_out, r.o_out, r.v_out)):
         size = held.shape[0] // PIECES
         for index in range(PIECES):
             at = pl.ds(index * size, size)
-            sems = refs["sems"].at[number], refs["sems"].at[number + 1]
-            number += 2
+            number = 2 * len(pieces)
             pieces.append(
                 (
-                    pltpu.make_async_copy(source.at[at], held.at[at], sems[0]),
-                    pltpu.make_async_copy(held.at[at], target.at[at], sems[1]),
+                    pltpu.make_async_copy(source.at[at], held.at[at], r.sems.at[number]),
+                    pltpu.make_async_copy(held.at[at], target.at[at], r.sems.at[number + 1]),
                 )
             )
     for incoming, _ in pieces:
         incoming.start()
-    sums = refs["r_sums"]
-    for row, name in enumerate(
-        ("merge_gain", "merge_bias", "attn_gain", "attn_bias", "proj_bias", "mlp_gain",
-         "mlp_bias", "down_bias")
-    ):
-        out = refs["o_" + name]
-        out[...] = sums[SUM_ROWS[row] : SUM_ROWS[row] + out.shape[0], :]
+    vectors = (
+        r.o_merge_gain, r.o_merge_bias, r.o_attn_gain, r.o_attn_bias, r.o_proj_bias, r.o_mlp_gain,
+        r.o_mlp_bias, r.o_down_bias,
+    )
+    for row, out in enumerate(vectors):
+        out[...] = r.sums[SUM_ROWS[row] : SUM_ROWS[row] + out.shape[0], :]
     for index in range(2):
-        refs["o_qv"][index : index + 1, :] = sums[pl.ds(SUM_ROWS[8 + index] + tp, 1), :]
-    blocks = refs["o_ub"].shape[0]
+        r.o_qv[index : index + 1, :] = r.sums[pl.ds(SUM_ROWS[8 + index] + tp, 1), :]
+    blocks = r.o_ub.shape[0]
     for index in range(blocks):
-        refs["o_ub"][index : index + 1, :] = sums[
-            pl.ds(SUM_ROWS[10] + tp * blocks + index, 1), :
-        ]
-    mine = refs["o_rel"].shape[0]
-    heads = SHARDS * mine
+        place = pl.ds(SUM_ROWS[10] + tp * blocks + index, 1)
+        r.o_ub[index : index + 1, :] = r.sums[place, :]
+    mine = r.o_rel.shape[0]
     for index in range(mine):
         first = SUM_ROWS[11] + tp * mine + index
-        low, high = sums[pl.ds(first, 1), :], sums[pl.ds(first + heads, 1), :]
-        refs["o_rel"][index : index + 1, :LANES] = low
-        refs["o_rel"][index : index + 1, LANES:] = high[:, : REL - LANES]
-    for name in GRADS:
-        result, out = refs["r_" + name], refs["o_" + name]
-        if len(out.shape) == 3:
-            rows = out.shape[1]
-            for part in range(out.shape[0]):
-                out[part] = result[part * rows : (part + 1) * rows, :].astype(F32)
-        else:
-            rows = out.shape[0]
-            for block in range(out.shape[1] // LANES):
-                lanes = slice(block * LANES, (block + 1) * LANES)
-                out[:, lanes] = result[block * rows : (block + 1) * rows, :].astype(F32)
+        low, high = r.sums[pl.ds(first, 1), :], r.sums[pl.ds(first + SHARDS * mine, 1), :]
+        r.o_rel[index : index + 1, :LANES] = low
+        r.o_rel[index : index + 1, LANES:] = high[:, : REL - LANES]
     for incoming, outgoing in pieces:
         incoming.wait()
         outgoing.start()
+    for result, out in ((r.rp, r.o_gp), (r.ru, r.o_gu), (r.rd, r.o_gd), (r.rm, r.o_gm)):
+        wide_rows(result, out)
+    rows = r.o_gqkv.shape[1]
+    for part in range(r.o_gqkv.shape[0]):
+        r.o_gqkv[part] = r.rqkv[part * rows : (part + 1) * rows, :].astype(F32)
     for _, outgoing in pieces:
         outgoing.wait()
 
 
-SHARDS = 4
-PIECES = 7
 VMEM_SPEC = pl.BlockSpec(memory_space=pltpu.VMEM)
 SMEM_SPEC = pl.BlockSpec(memory_space=pltpu.SMEM)
 HBM_SPEC = pl.BlockSpec(memory_space=pl.ANY)
 
 
-def whole_call(group, inputs):
-    rows, wide = inputs["h_x"].shape
-    width = inputs["own_wu"].shape[0]
-    units = SHARDS * inputs["own_wu"].shape[1]
-    depth = dict(gd=units, gu=units, gp=width, gqkv=3 * width, gm=wide)
+def whole_call(group, small, large):
+    rows, wide = large["h_x"].shape
+    width, tile = large["own_wu"].shape
+    units = SHARDS * tile
     scratch = local_scratch(rows, wide, width, units)
+    block = lambda *shape: pltpu.VMEM(shape, BF16)
+    exact = lambda *shape: pltpu.VMEM(shape, F32)
+    early = SUM_SIZE - LATE_ROWS
+    count = 11 * 6 + len(UNITS) * (6 + 2 * group) + 2 * (3 + group) + 4
     scratch.update(
-        wm=pltpu.VMEM((wide, width), BF16),
-        wqkv=pltpu.VMEM((3, width, width), BF16),
-        wp=pltpu.VMEM((width, width), BF16),
-        wu=pltpu.VMEM((width, units), BF16),
-        wd=pltpu.VMEM((units, width), BF16),
-        pack=pltpu.VMEM((8, units // SHARDS), F32),
-        packs=pltpu.VMEM((SHARDS, 8, units // SHARDS), F32),
-        x=pltpu.VMEM((rows, wide), BF16),
-        grad_out=pltpu.VMEM((rows, width), BF16),
-        out=pltpu.VMEM((rows, width), BF16),
-        d_in=pltpu.VMEM((rows, wide), F32),
+        wm=block(wide, width), wqkv=block(3, width, width), wp=block(width, width),
+        wu=block(width, units), wd=block(units, width), pack=exact(8, tile),
+        packs=exact(SHARDS, 8, tile), x=block(rows, wide), grad_out=block(rows, width),
+        out=block(rows, width), d_in=exact(rows, wide), gd=block(SHARDS, units, LANES),
+        gu=block(SHARDS, units, LANES), gp=block(SHARDS, width, LANES),
+        gqkv=block(SHARDS, 3 * width, LANES), gm=block(SHARDS, wide, LANES),
+        late_stages=exact(3, LATE_ROWS, LANES), late_in=exact(3, LATE_ROWS, LANES),
+        late_seats=exact(group, LATE_ROWS, LANES), early_stages=exact(3, early, LANES),
+        early_in=exact(3, early, LANES), early_seats=exact(group, early, LANES),
+        send_sems=pltpu.SemaphoreType.DMA((count,)), recv_sems=pltpu.SemaphoreType.DMA((count,)),
     )
-    for name in GRADS:
-        scratch[name] = pltpu.VMEM((SHARDS, depth[name], LANES), BF16)
-    for name, first, size, across_first in UNITS:
-        unit = unit_name(name, first)
+    boxes = []
+    for _, size, across_first in UNITS.values():
         half = size // 2
-        scratch["c_" + unit] = pltpu.VMEM((2, size, LANES), BF16)
-        first_shape = (size, LANES) if across_first else (2, half, LANES)
-        scratch["f_" + unit] = pltpu.VMEM(first_shape, BF16)
-        scratch["s_" + unit] = pltpu.VMEM((half, LANES), BF16)
-        scratch["z_" + unit] = pltpu.VMEM((group - 1, half // group, LANES), BF16)
-    scratch["sum_stages"] = pltpu.VMEM((4, SUM_SIZE, LANES), F32)
-    scratch["sum_inboxes"] = pltpu.VMEM((3, SUM_SIZE, LANES), F32)
-    scratch["sum_far"] = pltpu.VMEM((group - 1, SUM_SIZE // group, LANES), F32)
-    count = 8 * 6 + len(UNITS) * (5 + 2 * group) + 8 + 2 * group
-    scratch["send_sems"] = pltpu.SemaphoreType.DMA((count,))
-    scratch["recv_sems"] = pltpu.SemaphoreType.DMA((count,))
+        boxes += [
+            block(2, size, LANES),
+            block(size, LANES) if across_first else block(2, half, LANES),
+            block(half, LANES),
+            block(group - 1, half // group, LANES),
+        ]
+    result = lambda size: jax.ShapeDtypeStruct((size, LANES), BF16)
     outs = dict(
         h_out=jax.ShapeDtypeStruct((rows, width), BF16),
         h_d_in=jax.ShapeDtypeStruct((rows, wide), F32),
-        r_sums=jax.ShapeDtypeStruct((SUM_SIZE, LANES), F32),
+        rd=result(units), ru=result(units), rp=result(width), rqkv=result(3 * width),
+        rm=result(wide), sums=jax.ShapeDtypeStruct((SUM_SIZE, LANES), F32),
     )
-    for name in GRADS:
-        outs["r_" + name] = jax.ShapeDtypeStruct((depth[name], LANES), BF16)
-    names = INPUTS + OUTPUTS + tuple(scratch)
-    in_vmem = 3 + len(VECTORS)
-    return pl.pallas_call(
-        functools.partial(whole_kernel, names, group, {}),
-        out_shape=[outs[name] for name in OUTPUTS],
-        in_specs=[SMEM_SPEC] * 2 + [VMEM_SPEC] * in_vmem + [HBM_SPEC] * (2 + len(WEIGHTS)),
-        out_specs=[HBM_SPEC] * 2 + [VMEM_SPEC] * (len(OUTPUTS) - 2),
-        scratch_shapes=list(scratch.values()),
+    names = tuple(small) + tuple(large) + tuple(outs) + tuple(scratch)
+    made = pl.pallas_call(
+        functools.partial(whole_kernel, names, group),
+        out_shape=list(outs.values()),
+        in_specs=[SMEM_SPEC] * 2 + [VMEM_SPEC] * (len(small) - 2) + [HBM_SPEC] * len(large),
+        out_specs=[HBM_SPEC] * 2 + [VMEM_SPEC] * (len(outs) - 2),
+        scratch_shapes=list(scratch.values()) + boxes,
         compiler_params=pltpu.CompilerParams(
             vmem_limit_bytes=63 * MIB, collective_id=0, has_side_effects=True
         ),
-    )(*[inputs[name] for name in INPUTS])
+    )(*small.values(), *large.values())
+    return dict(zip(outs, made, strict=True))
 
 
 def finish_call(results, shapes):
-    names = OUTPUTS + tuple("o_" + name for name in shapes) + ("v_out", "v_d_in", "sems")
-    return pl.pallas_call(
+    (rows, width), (_, wide) = shapes["o_out"].shape, shapes["o_d_in"].shape
+    scratch = dict(
+        v_out=pltpu.VMEM((rows, width), BF16), v_d_in=pltpu.VMEM((rows, wide), F32),
+        sems=pltpu.SemaphoreType.DMA((4 * PIECES,)),
+    )
+    names = tuple(results) + tuple(shapes) + tuple(scratch)
+    made = pl.pallas_call(
         functools.partial(finish_kernel, names),
         out_shape=list(shapes.values()),
-        in_specs=[HBM_SPEC] * 2 + [VMEM_SPEC] * (len(OUTPUTS) - 2),
+        in_specs=[HBM_SPEC] * 2 + [VMEM_SPEC] * (len(results) - 2),
         out_specs=[HBM_SPEC] * 2 + [VMEM_SPEC] * (len(shapes) - 2),
-        scratch_shapes=[
-            pltpu.VMEM(shapes["out"].shape, BF16),
-            pltpu.VMEM(shapes["d_in"].shape, F32),
-            pltpu.SemaphoreType.DMA((4 * PIECES,)),
-        ],
+        scratch_shapes=list(scratch.values()),
         compiler_params=pltpu.CompilerParams(vmem_limit_bytes=63 * MIB),
-    )(*results)
+    )(*results.values())
+    return Refs(shapes, made)
 
 
 def on_device(
@@ -1384,33 +1418,37 @@
     attn_bias, query_key_value_weight, qv_bias, rel_table, proj_weight, proj_bias, mlp_gain,
     mlp_bias, up_weight, up_bias, down_weight, down_bias,
 ):
-    vectors = dict(
-        merge_gain=merge_gain, merge_bias=merge_bias, attn_gain=attn_gain, attn_bias=attn_bias,
-        mlp_gain=mlp_gain, mlp_bias=mlp_bias, proj_bias=proj_bias, down_bias=down_bias,
+    lines = lambda vector: vector.reshape(-1, LANES)
+    small = dict(
+        valid=window_valid, edge=window_edge, rel=rel_table.T, qv=qv_bias, ub=lines(up_bias),
+        merge_gain=lines(merge_gain), merge_bias=lines(merge_bias), attn_gain=lines(attn_gain),
+        attn_bias=lines(attn_bias), mlp_gain=lines(mlp_gain), mlp_bias=lines(mlp_bias),
+        proj_bias=lines(proj_bias), down_bias=lines(down_bias),
     )
-    blocks = {name: vector.reshape(-1, LANES) for name, vector in vectors.items()}
-    arrays = dict(
-        valid=window_valid, edge=window_edge, h_x=inputs, h_grad_out=grad_out, rel=rel_table.T,
-        qv=qv_bias, ub=up_bias.reshape(-1, LANES), own_wm=merge_weight,
-        own_wqkv=jnp.transpose(query_key_value_weight, (1, 0, 2)), own_wp=proj_weight,
-        own_wu=up_weight, own_wd=down_weight, **blocks,
+    qkv = jnp.transpose(query_key_value_weight, (1, 0, 2))
+    large = dict(
+        h_x=inputs, h_grad_out=grad_out, own_wm=merge_weight, own_wqkv=qkv, own_wp=proj_weight,
+        own_wu=up_weight, own_wd=down_weight,
     )
-    results = whole_call(lax.axis_size("sp") // 2, arrays)
-    f32_like = lambda array: jax.ShapeDtypeStruct(array.shape, F32)
+    results = whole_call(lax.axis_size("sp") // 2, small, large)
+    like = lambda array: jax.ShapeDtypeStruct(array.shape, F32)
     shapes = dict(
-        out=jax.ShapeDtypeStruct(grad_out.shape, BF16), d_in=f32_like(inputs),
-        gm=f32_like(merge_weight), gqkv=f32_like(arrays["own_wqkv"]), gp=f32_like(proj_weight),
-        gu=f32_like(up_weight), gd=f32_like(down_weight), qv=f32_like(qv_bias),
-        rel=f32_like(arrays["rel"]), ub=f32_like(arrays["ub"]),
-        **{name: f32_like(block) for name, block in blocks.items()},
+        o_out=jax.ShapeDtypeStruct(grad_out.shape, BF16), o_d_in=like(inputs),
+        o_gm=like(merge_weight), o_gqkv=like(qkv), o_gp=like(proj_weight), o_gu=like(up_weight),
+        o_gd=like(down_weight), o_qv=like(qv_bias), o_rel=like(rel_table.T),
+        o_ub=like(lines(up_bias)), o_merge_gain=like(lines(merge_gain)),
+        o_merge_bias=like(lines(merge_bias)), o_attn_gain=like(lines(attn_gain)),
+        o_attn_bias=like(lines(attn_bias)), o_proj_bias=like(lines(proj_bias)),
+        o_mlp_gain=like(lines(mlp_gain)), o_mlp_bias=like(lines(mlp_bias)),
+        o_down_bias=like(lines(down_bias)),
     )
-    done = dict(zip(shapes, finish_call(results, shapes), strict=True))
-    flat = lambda name: done[name].reshape(-1)
+    done = finish_call(results, shapes)
+    flat = lambda block: block.reshape(-1)
     return (
-        done["out"], done["d_in"], flat("merge_gain"), flat("merge_bias"), done["gm"],
-        flat("attn_gain"), flat("attn_bias"), jnp.transpose(done["gqkv"], (1, 0, 2)), done["qv"],
-        done["rel"].T, done["gp"], flat("proj_bias"), flat("mlp_gain"), flat("mlp_bias"),
-        done["gu"], flat("ub"), done["gd"], flat("down_bias"),
+        done.o_out, done.o_d_in, flat(done.o_merge_gain), flat(done.o_merge_bias), done.o_gm,
+        flat(done.o_attn_gain), flat(done.o_attn_bias), jnp.transpose(done.o_gqkv, (1, 0, 2)),
+        done.o_qv, done.o_rel.T, done.o_gp, flat(done.o_proj_bias), flat(done.o_mlp_gain),
+        flat(done.o_mlp_bias), done.o_gu, flat(done.o_ub), done.o_gd, flat(done.o_down_bias),
     )
 
 

time: 127 us -> 116 us (0.913)
  Pallas kernels: 126 us -> 115 us
    pallas_call x1, Pallas kernels: 119 us -> 108 us  [whole_call(): pl.pallas_call(functools.partial(whole_kernel, names, group), out_shape=l...]
where the time goes in v5:
time: 116 us
  Pallas kernels  115 us (99%)
    pallas_call x1, Pallas kernels, whole_call(): pl.pallas_call(functools.partial(whole_kernel, names, group), out_shape=l...  108 us
    pallas_call x1, Pallas kernels, finish_call(): pl.pallas_call(functools.partial(finish_kernel, names), out_shape=list(sh...  6.7 us

profile of v5, /device:TPU:0, one launch (start us, length us, event | category | flops | bytes accessed | tf_op | source)
XLA Modules:
  0.0 116.0 jit_solution(15064097277660891889)
XLA Ops:
  0.7 108.4 %shard_map.331 = (bf16[784,512]{1,0:T(8,128)(2,1)}, f32[784,1024]{1,0:T(8,128)}, bf16[2048,128]{1,0:T(8,128)(2,1)}, bf16[2048,128]{1,0:T(8,128)(2,1)}, bf16[512,...) custom-call(s32[64]{0:T(128)} %refs_0_.1, s32[64]{0:T(128)} %refs_1_.1, ...), custom_call_target="tpu_custom_call" | custom-call | tf_op jit(solution)/shard_map/pallas_call | solution.py:1385
  109.1 6.7 %shard_map.332 = (bf16[784,512]{1,0:T(8,128)(2,1)}, f32[784,1024]{1,0:T(8,128)}, f32[1024,128]{1,0:T(8,128)}, f32[3,512,128]{2,1,0:T(8,128)}, f32[128,512]{1,0:T...) custom-call(bf16[784,512]{1,0:T(8,128)(2,1)} %get-tuple-element.44.r, ...), custom_call_target="tpu_custom_call" | custom-call | tf_op jit(solution)/shard_map/pallas_call | solution.py:1405
